TPU v7x, 32 devices: a whole 2x2x4 slice. The times are simulated.
32 devices in a mesh: fsdp: 16 (over z, y, core), ns: 2 (over x).
Axes of the slice: x: 2, y: 2, z: 4, core: 2. Of those that a mesh axis runs over, the one named last changes fastest.
Arguments:
- patches: bfloat16 [32, 256, 768], P(('fsdp', 'ns')), may hold values from -6 to 6
- pad_mask: int32 [32, 256], P(('fsdp', 'ns')), may hold values from 0 to 1, as said below
- labels: int32 [32], P(('fsdp', 'ns')), may hold values from 0 to 999
- loss_weights: int32 [32], P(('fsdp', 'ns')), may hold values from 1 to 15
- class_emb: bfloat16 [1000, 512], replicated, may hold values from -6 to 6
- layer_mats: float32 [2, 9216, 768], P(None, 'fsdp')
- layer_zero: float32 [2, 9216, 768], P(None, 'fsdp')
- layer_ema: float32 [2, 9216, 768], P(None, 'fsdp')
- layer_momentum: float32 [2, 9216, 768], P(None, 'fsdp'), may hold values from -3.8146973e-06 to 3.8146973e-06
- row_params: float32 [1564, 768], P(None, 'fsdp')
- row_zero: float32 [1564, 768], P(None, 'fsdp')
- row_ema: float32 [1564, 768], P(None, 'fsdp')
- row_first: float32 [1564, 768], P(None, 'fsdp'), may hold values from -4.172325e-07 to 4.172325e-07
- row_second: float32 [1564, 768], P(None, 'fsdp'), may hold values from 1.3283907e-15 to 5.3135626e-15
Outputs:
- loss_sum: float32 [], replicated
- weight_sum: float32 [], replicated
- grad_norm: float32 [], replicated
- new_mats: float32 [2, 9216, 768], P(None, 'fsdp')
- new_momentum: float32 [2, 9216, 768], P(None, 'fsdp')
- ema_mats: float32 [2, 9216, 768], P(None, 'fsdp')
- mixed_mats: float32 [2, 9216, 768], P(None, 'fsdp')
- new_rows: float32 [1564, 768], P(None, 'fsdp')
- new_first: float32 [1564, 768], P(None, 'fsdp')
- new_second: float32 [1564, 768], P(None, 'fsdp')
- ema_rows: float32 [1564, 768], P(None, 'fsdp')
- mixed_rows: float32 [1564, 768], P(None, 'fsdp')
- down_bias_grad: float32 [2, 768], P(None, 'fsdp')
Inputs may be any that keep to these rules, and one draw needn't show every extreme that they name: `pad_mask`: in each image the ones are the first 128 to 256 slots; image 0 has all 256.
All inputs are finite; a program needn't handle non-finite values.
Results may differ from a plain program's by a relative error of at most 0.015.
Values may be sent and summed in bfloat16 or wider, within the bound.
A program may use at most 256 MiB of HBM per device.

v0:
```python
import math

import jax
import jax.numpy as jnp
from jax import lax
from jax.sharding import PartitionSpec as P

HEADS = 12
HDIM = 64
PIX = 768
EMB = 512
SEQ = 256
NS_STEPS = 5
STEPS_DONE = 10


HIGHEST = lax.Precision.HIGHEST
norm_epsilon = 1e-05
unit_epsilon = 1e-06
logit_scale = 50.0
clip_bound = 0.001
momentum_decay = 0.95
muon_rate = 0.05
weight_decay = 0.05
adam_rate = 0.2
first_decay = 0.9
second_decay = 0.98
adam_floor = 1e-08
ema_decay = 0.9
mix_share = 0.5
coeff_linear = 3.4445
coeff_cubic = -4.775
coeff_quintic = 2.0315


def shortened(shard):

    def short(part):
        return part.astype(jnp.bfloat16) if part.dtype == jnp.float32 else part

    return jax.tree.map(short, shard)


def matmul(left, right):
    return jnp.dot(left, right, preferred_element_type=jnp.float32)


def matmul_nt(left, right):
    return lax.dot_general(
        left, right, (((1,), (1,)), ((), ())), preferred_element_type=jnp.float32
    )


def matmul_tn(left, right):
    return lax.dot_general(
        left, right, (((0,), (0,)), ((), ())), preferred_element_type=jnp.float32
    )


def norm_forward(inputs, gain, shift):
    center = inputs - jnp.mean(inputs, -1, keepdims=True)
    scale = lax.rsqrt(jnp.mean(center * center, -1, keepdims=True) + norm_epsilon)
    return center * scale * gain + shift


def norm_backward(inputs, gain, upstream):
    center = inputs - jnp.mean(inputs, -1, keepdims=True)
    scale = lax.rsqrt(jnp.mean(center * center, -1, keepdims=True) + norm_epsilon)
    normal = center * scale
    scaled_up = upstream * gain
    inner = scale * (
        scaled_up
        - jnp.mean(scaled_up, -1, keepdims=True)
        - normal * jnp.mean(scaled_up * normal, -1, keepdims=True)
    )
    return (inner, jnp.sum(upstream * normal, 0), jnp.sum(upstream, 0))


def attention_scores(parts, valid_mask):
    raw = jnp.einsum(
        "iqhd,ikhd->ihqk", parts[:, :, 0], parts[:, :, 1], preferred_element_type=jnp.float32
    )
    return jnp.where(valid_mask[:, None, None, :] > 0, raw * HDIM ** (-0.5), -1000000000.0)


def gather_layer(shard):
    return lax.all_gather(shard.astype(jnp.bfloat16), "fsdp", axis=0, tiled=True)


def layer_forward(resid, weight_tensors, vector, valid_mask):
    images, seq = valid_mask.shape
    width = resid.shape[1]
    ffn = 4 * width
    normed = norm_forward(resid, vector[0], vector[1]).astype(jnp.bfloat16)
    bias = jnp.concatenate([vector[2], jnp.zeros_like(vector[2]), vector[3]])
    project = (matmul_nt(normed, weight_tensors[: 3 * width]) + bias).astype(jnp.bfloat16)
    parts = project.reshape(images, seq, 3, HEADS, HDIM)
    scores = attention_scores(parts, valid_mask)
    top_score = jnp.max(scores, -1, keepdims=True)
    expo = jnp.exp(scores - top_score)
    totals = jnp.sum(expo, -1, keepdims=True)
    log_total = top_score + jnp.log(totals)
    probs = (expo / totals).astype(jnp.bfloat16)
    context = jnp.einsum(
        "ihqk,ikhd->iqhd", probs, parts[:, :, 2], preferred_element_type=jnp.float32
    )
    context = context.reshape(images * seq, width).astype(jnp.bfloat16)
    mixed = resid + (matmul_nt(context, weight_tensors[3 * width : 4 * width]) + vector[4])
    normed_two = norm_forward(mixed, vector[5], vector[6]).astype(jnp.bfloat16)
    hidden_pre = matmul_nt(normed_two, weight_tensors[4 * width : 4 * width + ffn]) + vector[
        8:12
    ].reshape(ffn)
    hidden = (hidden_pre * jax.nn.sigmoid(1.702 * hidden_pre)).astype(jnp.bfloat16)
    output = mixed + (matmul(hidden, weight_tensors[4 * width + ffn :]) + vector[7])
    return (
        output,
        (resid, normed, project, log_total, context, mixed, normed_two, hidden_pre, hidden),
    )


def layer_backward(upstream, weight_tensors, vector, valid_mask, saved_activation):
    resid, normed, project, log_total, context, mixed, normed_two, hidden_pre, hidden = (
        saved_activation
    )
    images, seq = valid_mask.shape
    width = resid.shape[1]
    ffn = 4 * width
    out_grad = upstream.astype(jnp.bfloat16)
    grad_down = matmul_tn(hidden, out_grad)
    hidden_grad = matmul_nt(out_grad, weight_tensors[4 * width + ffn :])
    gate = jax.nn.sigmoid(1.702 * hidden_pre)
    pre_grad = (hidden_grad * (gate + 1.702 * hidden_pre * gate * (1.0 - gate))).astype(
        jnp.bfloat16
    )
    grad_up = matmul_tn(pre_grad, normed_two)
    second_in, gain_two, shift_two = norm_backward(
        mixed, vector[5], matmul(pre_grad, weight_tensors[4 * width : 4 * width + ffn])
    )
    mixed_grad = upstream + second_in
    attn_grad = mixed_grad.astype(jnp.bfloat16)
    grad_out = matmul_tn(attn_grad, context)
    context_grad = matmul(attn_grad, weight_tensors[3 * width : 4 * width]).astype(jnp.bfloat16)
    context_grad = context_grad.reshape(images, seq, HEADS, HDIM)
    parts = project.reshape(images, seq, 3, HEADS, HDIM)
    probs = jnp.exp(attention_scores(parts, valid_mask) - log_total)
    prob_grad = jnp.einsum(
        "iqhd,ikhd->ihqk", context_grad, parts[:, :, 2], preferred_element_type=jnp.float32
    )
    value_grad = jnp.einsum(
        "ihqk,iqhd->ikhd",
        probs.astype(jnp.bfloat16),
        context_grad,
        preferred_element_type=jnp.float32,
    )
    score_grad = (probs * (prob_grad - jnp.sum(prob_grad * probs, -1, keepdims=True))).astype(
        jnp.bfloat16
    )
    query_grad = jnp.einsum(
        "ihqk,ikhd->iqhd", score_grad, parts[:, :, 1], preferred_element_type=jnp.float32
    ) * HDIM ** (-0.5)
    key_grad = jnp.einsum(
        "ihqk,iqhd->ikhd", score_grad, parts[:, :, 0], preferred_element_type=jnp.float32
    ) * HDIM ** (-0.5)
    project_grad = (
        jnp.stack([query_grad, key_grad, value_grad], 2)
        .reshape(images * seq, 3 * width)
        .astype(jnp.bfloat16)
    )
    project_sum = jnp.sum(project_grad.astype(jnp.float32), 0)
    grad_qkv = matmul_tn(project_grad, normed)
    first_in, gain_one, shift_one = norm_backward(
        resid, vector[0], matmul(project_grad, weight_tensors[: 3 * width])
    )
    residual_gradient = mixed_grad + first_in
    grad_matrix = jnp.concatenate([grad_qkv, grad_out, grad_up, grad_down], 0)
    grad_vector = jnp.concatenate(
        [
            jnp.stack(
                [
                    gain_one,
                    shift_one,
                    project_sum[:width],
                    project_sum[2 * width :],
                    jnp.sum(attn_grad.astype(jnp.float32), 0),
                    gain_two,
                    shift_two,
                    jnp.sum(out_grad.astype(jnp.float32), 0),
                ]
            ),
            jnp.sum(pre_grad.astype(jnp.float32), 0).reshape(4, width),
        ],
        0,
    )
    return (residual_gradient, grad_matrix, grad_vector)


def gram_total(blocks):
    local = jnp.einsum("lcd,led->lce", blocks, blocks, precision=HIGHEST)
    return lax.psum(local.astype(jnp.bfloat16), "ns").astype(jnp.float32)


def newton_schulz(blocks):
    gram = gram_total(blocks)
    frob = jnp.sqrt(jnp.trace(gram, axis1=1, axis2=2))[:, None, None] + 1e-07
    blocks = blocks / frob
    gram = gram / (frob * frob)
    for turn in range(NS_STEPS):
        poly = coeff_cubic * gram + coeff_quintic * jnp.einsum(
            "lce,lef->lcf", gram, gram, precision=HIGHEST
        )
        blocks = coeff_linear * blocks + jnp.einsum("lce,led->lcd", poly, blocks, precision=HIGHEST)
        if turn + 1 < NS_STEPS:
            gram = gram_total(blocks)
    return blocks


def body(
    patches,
    pad_mask,
    labels,
    loss_weights,
    class_emb,
    layer_mats,
    layer_zero,
    layer_ema,
    layer_momentum,
    row_params,
    row_zero,
    row_ema,
    row_first,
    row_second,
):
    layers, columns, width = layer_mats.shape
    images, seq, pixels = patches.shape
    front = PIX + EMB + SEQ + 4
    valid_mask = pad_mask.astype(jnp.float32)
    gathered_rows = lax.all_gather(row_params.astype(jnp.bfloat16), "fsdp", axis=1, tiled=True)
    rows_value = gathered_rows.astype(jnp.float32)
    patch_weight = gathered_rows[:PIX]
    proj_rows = gathered_rows[PIX : PIX + EMB]
    position = rows_value[PIX + EMB : PIX + EMB + SEQ]
    head_vec = rows_value[PIX + EMB + SEQ : front]
    layer_vector_params = rows_value[front:].reshape(layers, 12, width)
    flat_patches = patches.reshape(images * seq, pixels)
    embedded = (matmul(flat_patches, patch_weight).reshape(images, seq, width) + position).reshape(
        images * seq, width
    )
    resid = norm_forward(embedded, head_vec[0], head_vec[1])
    kept_weights = []
    saved_activations = []
    for layer_number in range(layers):
        weight_tensors = gather_layer(layer_mats[layer_number])
        kept_weights.append(weight_tensors)
        resid, saved_activation = layer_forward(
            resid, weight_tensors, layer_vector_params[layer_number], valid_mask
        )
        saved_activations.append(saved_activation)
    counts = jnp.sum(valid_mask, -1, keepdims=True)
    pooled = jnp.sum(resid.reshape(images, seq, width) * valid_mask[..., None], 1) / counts
    pooled_norm = norm_forward(pooled, head_vec[2], head_vec[3]).astype(jnp.bfloat16)
    feature = matmul_nt(pooled_norm, proj_rows)
    inv_length = lax.rsqrt(jnp.sum(feature * feature, -1, keepdims=True) + unit_epsilon)
    unit_feat = (feature * inv_length).astype(jnp.bfloat16)
    classes = class_emb.astype(jnp.float32)
    class_unit = (
        classes * lax.rsqrt(jnp.sum(classes * classes, -1, keepdims=True) + unit_epsilon)
    ).astype(jnp.bfloat16)
    logits = logit_scale * matmul_nt(unit_feat, class_unit)
    top_logit = jnp.max(logits, -1, keepdims=True)
    shifted = jnp.exp(logits - top_logit)
    total_exp = jnp.sum(shifted, -1, keepdims=True)
    log_norm = top_logit + jnp.log(total_exp)
    onehot = (jnp.arange(logits.shape[1])[None, :] == labels[:, None]).astype(jnp.float32)
    losses = log_norm[:, 0] - jnp.sum(onehot * logits, -1)
    weights_value = loss_weights.astype(jnp.float32)
    loss_sum, weight_sum = lax.psum(
        (jnp.sum(weights_value * losses), jnp.sum(weights_value)), ("fsdp", "ns")
    )
    seed = weights_value / weight_sum
    logit_grad = seed[:, None] * (shifted / total_exp - onehot)
    unit_grad = logit_scale * jnp.dot(logit_grad, class_unit.astype(jnp.float32), precision=HIGHEST)
    feat_grad = inv_length * unit_grad - feature * inv_length**3 * jnp.sum(
        unit_grad * feature, -1, keepdims=True
    )
    grad_proj = jnp.dot(feat_grad.T, pooled_norm.astype(jnp.float32), precision=HIGHEST)
    pooled_grad, gain_post, shift_post = norm_backward(
        pooled, head_vec[2], jnp.dot(feat_grad, proj_rows.astype(jnp.float32), precision=HIGHEST)
    )
    residual_gradient = (valid_mask[..., None] * (pooled_grad / counts)[:, None, :]).reshape(
        images * seq, width
    )
    grad_mats = [None] * layers
    grad_vecs = [None] * layers
    for layer_number in reversed(range(layers)):
        weight_tensors = lax.all_gather(
            layer_mats[layer_number].astype(jnp.bfloat16), "fsdp", axis=0, tiled=True
        )
        residual_gradient, grad_matrix, grad_vector = layer_backward(
            residual_gradient,
            weight_tensors,
            layer_vector_params[layer_number],
            valid_mask,
            saved_activations[layer_number],
        )
        grad_mats[layer_number], grad_vecs[layer_number] = (
            lax.psum_scatter(grad_matrix, "fsdp", scatter_dimension=0, tiled=True),
            lax.psum_scatter(grad_vector, "fsdp", scatter_dimension=1, tiled=True),
        )
    embed_grad, gain_pre, shift_pre = norm_backward(embedded, head_vec[0], residual_gradient)
    position_grad = jnp.sum(embed_grad.reshape(images, seq, width), 0)
    patch_grad = matmul_tn(flat_patches, embed_grad.astype(jnp.bfloat16))
    front_grad = jnp.concatenate(
        [
            patch_grad,
            grad_proj,
            position_grad,
            jnp.stack([gain_pre, shift_pre, gain_post, shift_post]),
        ],
        0,
    )
    front_shard = lax.psum_scatter(front_grad, "fsdp", scatter_dimension=1, tiled=True)
    mat_grad = jnp.stack(grad_mats)
    row_grad = jnp.concatenate([front_shard] + grad_vecs, 0)
    pairs = lax.axis_size("ns")
    side = lax.axis_index("ns")
    half_depth = width // pairs
    half_rows = row_grad.shape[0] // pairs
    shard_width = row_grad.shape[1]
    mat_total, row_total = (
        lax.psum(mat_grad.astype(jnp.bfloat16), "ns").astype(jnp.float32),
        lax.psum(row_grad.astype(jnp.bfloat16), "ns").astype(jnp.float32),
    )
    mat_half = lax.dynamic_slice_in_dim(mat_total, side * half_depth, half_depth, 2)
    row_half = lax.dynamic_slice_in_dim(row_total, side * half_rows, half_rows, 0)
    squares = jnp.sum(mat_half * mat_half) + jnp.sum(row_half * row_half)
    grad_norm = jnp.sqrt(lax.psum(squares, ("fsdp", "ns")))
    clip = jnp.minimum(1.0, clip_bound / (grad_norm + 1e-06))
    momentum = momentum_decay * layer_momentum + clip * mat_total
    orth_half = newton_schulz(lax.dynamic_slice_in_dim(momentum, side * half_depth, half_depth, 2))
    orth = lax.all_gather(shortened(orth_half[:, :, None]), "ns", axis=2, tiled=True).reshape(
        layers, columns, width
    )
    clipped = clip * row_total
    new_first = first_decay * row_first + (1.0 - first_decay) * clipped
    new_second = second_decay * row_second + (1.0 - second_decay) * clipped * clipped
    down_bias_grad = clipped[front:].reshape(layers, 12, shard_width)[:, 7]
    new_mats = layer_mats - muon_rate * (0.2 * math.sqrt(width) * orth + weight_decay * layer_mats)
    ema_mats = ema_decay * layer_ema + (1.0 - ema_decay) * new_mats
    mixed_mats = mix_share * new_mats + (1.0 - mix_share) * layer_zero
    step_size = (
        new_first
        / (1.0 - first_decay**STEPS_DONE)
        / (jnp.sqrt(new_second / (1.0 - second_decay**STEPS_DONE)) + adam_floor)
    )
    new_rows = row_params - adam_rate * (step_size + weight_decay * row_params)
    ema_rows = ema_decay * row_ema + (1.0 - ema_decay) * new_rows
    mixed_rows = mix_share * new_rows + (1.0 - mix_share) * row_zero
    return (
        loss_sum,
        weight_sum,
        grad_norm,
        new_mats,
        momentum,
        ema_mats,
        mixed_mats,
        new_rows,
        new_first,
        new_second,
        ema_rows,
        mixed_rows,
        down_bias_grad,
    )


def solution(mesh):
    in_specs = (
        P(("fsdp", "ns"), None, None),
        P(("fsdp", "ns"), None),
        P(("fsdp", "ns")),
        P(("fsdp", "ns")),
        P(),
        P(None, "fsdp", None),
        P(None, "fsdp", None),
        P(None, "fsdp", None),
        P(None, "fsdp", None),
        P(None, "fsdp"),
        P(None, "fsdp"),
        P(None, "fsdp"),
        P(None, "fsdp"),
        P(None, "fsdp"),
    )
    out_specs = (
        P(),
        P(),
        P(),
        P(None, "fsdp", None),
        P(None, "fsdp", None),
        P(None, "fsdp", None),
        P(None, "fsdp", None),
        P(None, "fsdp"),
        P(None, "fsdp"),
        P(None, "fsdp"),
        P(None, "fsdp"),
        P(None, "fsdp"),
        P(None, "fsdp"),
    )
    return jax.shard_map(body, mesh=mesh, in_specs=in_specs, out_specs=out_specs, check_vma=False)
```

profile of v0, /device:TPU:0, one launch (start us, length us, event | category | flops | bytes accessed | tf_op | source)
XLA Modules:
  0.0 1623.0 jit_solution(16022641407821412463)
XLA Ops:
  14.0 42.9 %psum.71 = f32[]{:T(128)} all-reduce(f32[]{:T(128)} %bitcast.29), channel_id=1, replica_groups=mesh['fsdp'=16,'ns'=2] {'fsdp','ns'}, use_global_device_ids=true, to_apply=%region_24.25 | all-reduce | flops 1 | bytes 8 | tf_op jit(solution)/shard_map/psum | solution.py:276
  60.3 4.5 copy.99
  74.2 94.6 %all-gather.10.cloned.1.call-done = bf16[1,9216,768]{2,1,0:T(8,128)(2,1)} async-done(((bf16[1,576,768]{2,1,0:T(8,128)(2,1)}), bf16[1,9216,768]{2,1,0:T(8,128)(2,1)}) %all-gather.10.cloned.1.call-update) | async-done | bytes 14155792 | tf_op jit(solution)/shard_map/all_gather | solution.py:87
  168.8 3.3 fusion.14
  178.1 3.5 copy-done.66
  187.4 93.1 %all-gather.12.cloned.1.call-done = bf16[1,9216,768]{2,1,0:T(8,128)(2,1)} async-done(((bf16[1,576,768]{2,1,0:T(8,128)(2,1)}), bf16[1,9216,768]{2,1,0:T(8,128)(2,1)}) %all-gather.12.cloned.1.call-update) | async-done | bytes 14155792 | tf_op jit(solution)/shard_map/all_gather | solution.py:87
  280.5 4.4 fusion.15
  289.9 3.0 fusion.104
  323.1 3.1 fusion.161
  328.9 5.8 convert_reduce_fusion
  334.7 5.1 multiply_reduce_fusion.3
  346.2 3.1 multiply_reduce_fusion.1
  353.6 4.4 multiply_reduce_fusion.4
  383.6 3.5 multiply_reduce_fusion.6
  394.6 14.4 concatenate.43
  408.9 6.0 copy.124
  420.3 5.7 fusion.148
  426.0 22.6 %pad_maximum_fusion = f32[9216,768]{1,0:T(8,128)} fusion(f32[3072,768]{1,0:T(8,128)} %fusion.148, f32[3072,768]{1,0:T(8,128)S(1)} %fusion.157, f32[768,768]{1,0:T(8,128)S(1)} %fusion.145, f32[2304,768]{1,0:T(8,128)S(1)} %fusion.156), kind=kLoop, calls=%fused_computation | loop fusion | flops 21233664 | bytes 56623104 | tf_op jit(solution)/shard_map/concatenate | solution.py:175
  454.2 5.7 fusion.109
  459.9 22.6 %pad_maximum_fusion.1 = f32[9216,768]{1,0:T(8,128)} fusion(f32[3072,768]{1,0:T(8,128)} %fusion.109, f32[3072,768]{1,0:T(8,128)S(1)} %fusion.159, f32[768,768]{1,0:T(8,128)S(1)} %fusion.151, f32[2304,768]{1,0:T(8,128)S(1)} %fusion.158), kind=kLoop, calls=%fused_computation.1 | loop fusion | flops 21233664 | bytes 56623104 | tf_op jit(solution)/shard_map/concatenate | solution.py:175
  483.5 10.6 reduce-scatter.18.cloned.1.call-done
  495.0 79.7 %reduce-scatter.16.cloned.1.call-done = f32[48,1540]{1,0:T(8,128)} async-done(((f32[768,1540]{1,0:T(8,128)}), f32[48,1540]{1,0:T(8,128)}) %reduce-scatter.16.cloned.1.call-update) | async-done | bytes 295696
  576.4 271.2 %reduce-scatter.12.cloned.1.call-done = f32[576,768]{1,0:T(8,128)} async-done(((f32[9216,768]{1,0:T(8,128)}), f32[576,768]{1,0:T(8,128)}) %reduce-scatter.12.cloned.1.call-update) | async-done | bytes 1769488 | tf_op jit(solution)/shard_map/reduce_scatter | solution.py:306
  849.2 271.6 %reduce-scatter.14.cloned.1.call-done = f32[576,768]{1,0:T(8,128)} async-done(((f32[9216,768]{1,0:T(8,128)}), f32[576,768]{1,0:T(8,128)}) %reduce-scatter.14.cloned.1.call-update) | async-done | bytes 1769488 | tf_op jit(solution)/shard_map/reduce_scatter | solution.py:306
  1125.7 57.3 %all-reduce.19.cloned.1.call-done = (bf16[2,576,768]{2,1,0:T(8,128)(2,1)}, bf16[1564,48]{0,1:T(8,128)(2,1)}) async-done(((bf16[2,576,768]{2,1,0:T(8,128)(2,1)}, bf16[1564,48]{0,1:T(8,128)(2,1)}), (bf16[2,576,768]{2,1,0:T(8,128)(2,1)}, bf16[1564,48]{0,1:T(8,128)(2,1)})) %all-reduce.19.cloned.1.call-update) | async-done | bytes 1919632 | tf_op jit(solution)/shard_map/psum | solution.py:330
  1187.9 40.1 %all-reduce = (f32[]{:T(128)}, f32[]{:T(128)}) all-reduce(f32[]{:T(128)} %bitcast.28, f32[]{:T(128)S(6)} %add.444), channel_id=1, replica_groups=mesh['fsdp'=16,'ns'=2] {'fsdp','ns'}, use_global_device_ids=true, to_apply=%region_23.24 | all-reduce | flops 2 | bytes 16 | tf_op jit(solution)/shard_map/psum | solution.py:276
  1233.1 6.4 fusion.54
  1239.8 50.0 %all-reduce.9.cloned.1.call-done = bf16[2,576,576]{2,1,0:T(8,128)(2,1)} async-done(((bf16[2,576,576]{2,1,0:T(8,128)(2,1)}), bf16[2,576,576]{2,1,0:T(8,128)(2,1)}) %all-reduce.9.cloned.1.call-update) | async-done | bytes 1327120 | tf_op jit(solution)/shard_map/psum | solution.py:199
  1291.9 10.6 fusion.51
  1302.5 6.3 multiply_add_fusion.5
  1310.1 6.4 convolution_convert_fusion.3
  1316.5 49.5 %all-reduce.11.cloned.1.call-done = bf16[2,576,576]{2,1,0:T(8,128)(2,1)} async-done(((bf16[2,576,576]{2,1,0:T(8,128)(2,1)}), bf16[2,576,576]{2,1,0:T(8,128)(2,1)}) %all-reduce.11.cloned.1.call-update) | async-done | bytes 1327120 | tf_op jit(solution)/shard_map/psum | solution.py:199
  1366.0 3.4 fusion.176
  1369.4 7.5 multiply_add_fusion.4
  1376.9 6.4 convolution_convert_fusion.2
  1383.6 49.3 %all-reduce.13.cloned.1.call-done = bf16[2,576,576]{2,1,0:T(8,128)(2,1)} async-done(((bf16[2,576,576]{2,1,0:T(8,128)(2,1)}), bf16[2,576,576]{2,1,0:T(8,128)(2,1)}) %all-reduce.13.cloned.1.call-update) | async-done | bytes 1327120 | tf_op jit(solution)/shard_map/psum | solution.py:199
  1432.9 3.4 fusion.177
  1436.3 5.7 multiply_add_fusion.3
  1443.2 6.4 convolution_convert_fusion.1
  1449.8 49.2 %all-reduce.15.cloned.1.call-done = bf16[2,576,576]{2,1,0:T(8,128)(2,1)} async-done(((bf16[2,576,576]{2,1,0:T(8,128)(2,1)}), bf16[2,576,576]{2,1,0:T(8,128)(2,1)}) %all-reduce.15.cloned.1.call-update) | async-done | bytes 1327120 | tf_op jit(solution)/shard_map/psum | solution.py:199
  1499.1 3.4 fusion.178
  1502.5 7.5 multiply_add_fusion.2
  1510.0 6.4 convolution_convert_fusion
  1516.7 49.2 %all-reduce.17.cloned.1.call-done = bf16[2,576,576]{2,1,0:T(8,128)(2,1)} async-done(((bf16[2,576,576]{2,1,0:T(8,128)(2,1)}), bf16[2,576,576]{2,1,0:T(8,128)(2,1)}) %all-reduce.17.cloned.1.call-update) | async-done | bytes 1327120 | tf_op jit(solution)/shard_map/psum | solution.py:199
  1565.9 3.4 fusion.179
  1569.5 6.4 add_convert_fusion
  1578.6 26.9 %all-gather.14.cloned.1.call-done = bf16[2,576,768]{2,1,0:T(8,128)(2,1)} async-done(((bf16[2,576,384]{2,1,0:T(8,128)(2,1)}), bf16[2,576,768]{2,1,0:T(8,128)(2,1)}) %all-gather.14.cloned.1.call-update) | async-done | bytes 1769488 | tf_op jit(solution)/shard_map/all_gather | solution.py:340
  1605.5 6.4 add_multiply_fusion
  (497 shorter events, 144.2 us)
Async XLA Ops:
  7.2 64.0 %copy-start = (bf16[1,256,768]{2,1,0:T(8,128)(2,1)S(1)}, bf16[1,256,768]{2,1,0:T(8,128)(2,1)}, u32[]{:S(2)}) copy-start(bf16[1,256,768]{2,1,0:T(8,128)(2,1)} %param.14) | copy-start | bytes 1179652
  7.2 53.1 %all-gather.8.cloned.1.call-start = ((), (), s32[]{:S(2)}) async-start(), calls=%async_computation.5 | async-start | bytes 2715648 | tf_op jit(solution)/shard_map/all_gather | solution.py:237
  9.0 159.9 %all-gather.10.cloned.1.call-start = ((), (), s32[]{:S(2)}) async-start(), calls=%async_computation.13 | async-start | bytes 15040512 | tf_op jit(solution)/shard_map/all_gather | solution.py:87
  11.2 45.7 %copy-start.145 = (s32[1,256]{1,0:T(1,128)S(1)}, s32[1,256]{1,0:T(1,128)}, u32[]{:S(2)}) copy-start(s32[1,256]{1,0:T(1,128)} %param.15) | copy-start | bytes 3076
  11.2 47.7 %copy-start.26 = (bf16[1000,512]{1,0:T(8,128)(2,1)S(1)}, bf16[1000,512]{1,0:T(8,128)(2,1)}, u32[]{:S(2)}) copy-start(bf16[1000,512]{1,0:T(8,128)(2,1)} %param.18) | copy-start | bytes 3072004
  12.6 268.0 %all-gather.12.cloned.1.call-start = ((), (), s32[]{:S(2)}) async-start(), calls=%async_computation.14 | async-start | bytes 15040512 | tf_op jit(solution)/shard_map/all_gather | solution.py:87
  13.3 469.3 %reduce-scatter.20.cloned.1.call-start = ((), (), s32[]{:S(2)}) async-start(), calls=%async_computation.18 | async-start | bytes 417792
  70.6 101.5 %copy-start.79 = (f32[768]{0:T(1024)}, f32[768]{0:T(1024)S(1)}, u32[]{:S(2)}) copy-start(f32[768]{0:T(1024)S(1)} %get-tuple-element.54) | copy-start | bytes 9220
  70.6 101.5 %copy-start.95 = (f32[768]{0:T(1024)}, f32[768]{0:T(1024)S(1)}, u32[]{:S(2)}) copy-start(f32[768]{0:T(1024)S(1)} %get-tuple-element.53) | copy-start | bytes 9220
  70.6 107.5 %copy-start.60 = (f32[768]{0:T(1024)}, f32[768]{0:T(1024)S(1)}, u32[]{:S(2)}) copy-start(f32[768]{0:T(1024)S(1)} %get-tuple-element.56) | copy-start | bytes 9220
  70.6 107.5 %copy-start.64 = (f32[768]{0:T(1024)}, f32[768]{0:T(1024)S(1)}, u32[]{:S(2)}) copy-start(f32[768]{0:T(1024)S(1)} %get-tuple-element.55) | copy-start | bytes 9220
  70.6 209.9 %copy-start.76 = (f32[768]{0:T(1024)}, f32[768]{0:T(1024)S(1)}, u32[]{:S(2)}) copy-start(f32[768]{0:T(1024)S(1)} %get-tuple-element.46) | copy-start | bytes 9220
  73.3 98.8 %copy-start.4 = (f32[256,768]{1,0:T(8,128)}, f32[256,768]{1,0:T(8,128)S(1)}, u32[]{:S(2)}) copy-start(f32[256,768]{1,0:T(8,128)S(1)} %get-tuple-element.121) | copy-start | bytes 2359300
  73.3 104.8 %copy-start.74 = (f32[256]{0:T(256)}, f32[256]{0:T(256)S(1)}, u32[]{:S(2)}) copy-start(f32[256]{0:T(256)S(1)} %broadcast_multiply_fusion.16) | copy-start | bytes 3076
  73.6 98.6 %copy-start.81 = (f32[256]{0:T(256)}, f32[256]{0:T(256)S(1)}, u32[]{:S(2)}) copy-start(f32[256]{0:T(256)S(1)} %add_rsqrt_fusion.5) | copy-start | bytes 3076
  73.9 98.3 %copy-start.97 = (f32[256]{0:T(256)}, f32[256]{0:T(256)S(1)}, u32[]{:S(2)}) copy-start(f32[256]{0:T(256)S(1)} %broadcast_multiply_fusion.15) | copy-start | bytes 3076
  74.2 97.9 %copy-start.122 = (f32[256]{0:T(256)}, f32[256]{0:T(256)S(1)}, u32[]{:S(2)}) copy-start(f32[256]{0:T(256)S(1)} %add_rsqrt_fusion.4) | copy-start | bytes 3076
  184.3 96.2 %copy-start.93 = (f32[768]{0:T(1024)S(1)}, f32[768]{0:T(1024)}, u32[]{:S(2)}) copy-start(f32[768]{0:T(1024)} %get-tuple-element.45) | copy-start | bytes 9220
  186.3 98.6 %copy-start.99 = (f32[256]{0:T(256)}, f32[256]{0:T(256)S(1)}, u32[]{:S(2)}) copy-start(f32[256]{0:T(256)S(1)} %broadcast_multiply_fusion.13) | copy-start | bytes 3076
  187.4 97.5 %copy-start.124 = (f32[256]{0:T(256)}, f32[256]{0:T(256)S(1)}, u32[]{:S(2)}) copy-start(f32[256]{0:T(256)S(1)} %add_rsqrt_fusion.2) | copy-start | bytes 3076
  328.8 11.0 copy-start.116
  346.2 12.8 slice-start
  349.3 9.6 slice-start.1
  351.0 8.0 slice-start.2
  377.0 6.6 copy-start.6
  377.0 6.6 copy-start.61
  377.0 6.6 copy-start.65
  377.0 6.6 copy-start.75
  377.0 6.6 copy-start.80
  377.0 6.6 copy-start.83
  377.0 6.6 copy-start.98
  377.0 6.6 copy-start.123
  381.7 112.3 %reduce-scatter.18.cloned.1.call-start = ((), (), s32[]{:S(2)}) async-start(), calls=%async_computation.17 | async-start | bytes 417792
  393.8 180.8 %reduce-scatter.16.cloned.1.call-start = ((), (), s32[]{:S(2)}) async-start(), calls=%async_computation.16 | async-start | bytes 5431296
  415.0 432.6 %reduce-scatter.12.cloned.1.call-start = ((), (), s32[]{:S(2)}) async-start(), calls=%async_computation.6 | async-start | bytes 30081024 | tf_op jit(solution)/shard_map/reduce_scatter | solution.py:306
  448.7 672.0 %reduce-scatter.14.cloned.1.call-start = ((), (), s32[]{:S(2)}) async-start(), calls=%async_computation.7 | async-start | bytes 30081024 | tf_op jit(solution)/shard_map/reduce_scatter | solution.py:306
  482.5 700.4 %all-reduce.19.cloned.1.call-start = ((), (), s32[]{:S(2)}) async-start(), calls=%async_computation.19 | async-start | bytes 3858432 | tf_op jit(solution)/shard_map/psum | solution.py:330
  1123.7 166.1 %all-reduce.9.cloned.1.call-start = ((), (), s32[]{:S(2)}) async-start(), calls=%async_computation.8 | async-start | bytes 2949120 | tf_op jit(solution)/shard_map/psum | solution.py:199
  1182.9 45.9 %copy-start.37 = (bf16[2,576,768]{2,1,0:T(8,128)(2,1)S(1)}, bf16[2,576,768]{2,1,0:T(8,128)(2,1)}, u32[]{:S(2)}) copy-start(bf16[2,576,768]{2,1,0:T(8,128)(2,1)} %get-tuple-element.83) | copy-start | bytes 5308420
  1239.4 126.5 %all-reduce.11.cloned.1.call-start = ((), (), s32[]{:S(2)}) async-start(), calls=%async_computation.9 | async-start | bytes 2949120 | tf_op jit(solution)/shard_map/psum | solution.py:199
  1291.9 10.6 copy-start.30
  1291.9 10.6 copy-start.49
  1316.4 116.4 %all-reduce.13.cloned.1.call-start = ((), (), s32[]{:S(2)}) async-start(), calls=%async_computation.10 | async-start | bytes 2949120 | tf_op jit(solution)/shard_map/psum | solution.py:199
  1383.3 115.7 %all-reduce.15.cloned.1.call-start = ((), (), s32[]{:S(2)}) async-start(), calls=%async_computation.11 | async-start | bytes 2949120 | tf_op jit(solution)/shard_map/psum | solution.py:199
  1449.6 116.4 %all-reduce.17.cloned.1.call-start = ((), (), s32[]{:S(2)}) async-start(), calls=%async_computation.12 | async-start | bytes 2949120 | tf_op jit(solution)/shard_map/psum | solution.py:199
  1516.4 89.1 %all-gather.14.cloned.1.call-start = ((), (), s32[]{:S(2)}) async-start(), calls=%async_computation.15 | async-start | bytes 2654208 | tf_op jit(solution)/shard_map/all_gather | solution.py:340
  1569.4 6.5 copy-start.50
  1577.1 34.8 %copy-start.51 = (f32[1564,48]{0,1:T(8,128)}, f32[1564,48]{0,1:T(8,128)S(1)}, u32[]{:S(2)}) copy-start(f32[1564,48]{0,1:T(8,128)S(1)} %get-tuple-element.86) | copy-start | bytes 900868
  (122 other events, 348.6 us)
Sparse Core Ops, SparseCore 0:
  10.8 45.7 all-gather.7
  59.4 109.3 all-gather.9
  171.7 108.7 all-gather.11
  381.8 53.7 reduce-scatter.19
  439.4 54.6 reduce-scatter.17
  497.8 76.7 reduce-scatter.15
  579.4 268.1 reduce-scatter.11
  852.4 268.3 reduce-scatter.13
  1124.3 58.5 all-reduce.18
  1239.6 50.1 all-reduce.8
  1316.6 49.3 all-reduce.10
  1383.5 49.3 all-reduce.12
  1449.7 49.3 all-reduce.14
  1516.6 49.3 all-reduce.16
  1576.0 29.4 all-gather.13
where the time goes:
time: 1630 us; the launch traced here: 1620 us
  waiting for transfers between devices  1150 us (71%)
  matrix products  182 us (11%)
  other arithmetic  106 us (7%)
  blocking collectives  83.1 us (5%)
  local copies, waits for them, and re-layouts  69.8 us (4%)
  between operations  26.8 us (2%)
    reduce_scatter x2, waiting for transfers between devices, body(): lax.psum_scatter(grad_matrix, 'fsdp', scatter_dimension=0, tiled=True)  543 us
    psum x5, waiting for transfers between devices, gram_total(): return lax.psum(local.astype(jnp.bfloat16), 'ns').astype(jnp.float32)  247 us
    all_gather x2, waiting for transfers between devices, gather_layer(): lax.all_gather(shard.astype(jnp.bfloat16), 'fsdp', axis=0, tiled=True)  188 us
    unnamed x18, waiting for transfers between devices  91.2 us
    psum x2, blocking collectives, body(): lax.psum((jnp.sum(weights_value * losses), jnp.sum(weights_value)), ('fsd...  83.1 us
    psum x1, waiting for transfers between devices, body(): lax.psum(mat_grad.astype(jnp.bfloat16), 'ns').astype(jnp.float32)  57.3 us
    concatenate x2, other arithmetic, layer_backward(): grad_matrix = jnp.concatenate([grad_qkv, grad_out, grad_up, grad_down], 0)  45.2 us
    dot_general x5, matrix products, newton_schulz(): jnp.einsum('lce,led->lcd', poly, blocks, precision=HIGHEST)  33.4 us
  transfers between devices with their start and end apart: 15, of which 13 were waited for; matrix products, arithmetic and copies ran while one was open for 8% of the time, Pallas kernels for 0%

commit v1 on v0

--- a/solution.py
+++ b/solution.py
@@ -33,14 +33,6 @@
 coeff_quintic = 2.0315
 
 
-def shortened(shard):
-
-    def short(part):
-        return part.astype(jnp.bfloat16) if part.dtype == jnp.float32 else part
-
-    return jax.tree.map(short, shard)
-
-
 def matmul(left, right):
     return jnp.dot(left, right, preferred_element_type=jnp.float32)
 
@@ -172,7 +164,9 @@
         resid, vector[0], matmul(project_grad, weight_tensors[: 3 * width])
     )
     residual_gradient = mixed_grad + first_in
-    grad_matrix = jnp.concatenate([grad_qkv, grad_out, grad_up, grad_down], 0)
+    grad_matrix = jnp.concatenate(
+        [part.astype(jnp.bfloat16) for part in (grad_qkv, grad_out, grad_up, grad_down)], 0
+    )
     grad_vector = jnp.concatenate(
         [
             jnp.stack(
@@ -194,13 +188,12 @@
     return (residual_gradient, grad_matrix, grad_vector)
 
 
-def gram_total(blocks):
-    local = jnp.einsum("lcd,led->lce", blocks, blocks, precision=HIGHEST)
-    return lax.psum(local.astype(jnp.bfloat16), "ns").astype(jnp.float32)
+def gram_of(blocks):
+    return jnp.einsum("lcd,led->lce", blocks, blocks, precision=HIGHEST)
 
 
 def newton_schulz(blocks):
-    gram = gram_total(blocks)
+    gram = gram_of(blocks)
     frob = jnp.sqrt(jnp.trace(gram, axis1=1, axis2=2))[:, None, None] + 1e-07
     blocks = blocks / frob
     gram = gram / (frob * frob)
@@ -210,7 +203,7 @@
         )
         blocks = coeff_linear * blocks + jnp.einsum("lce,led->lcd", poly, blocks, precision=HIGHEST)
         if turn + 1 < NS_STEPS:
-            gram = gram_total(blocks)
+            gram = gram_of(blocks)
     return blocks
 
 
@@ -292,9 +285,7 @@
     grad_mats = [None] * layers
     grad_vecs = [None] * layers
     for layer_number in reversed(range(layers)):
-        weight_tensors = lax.all_gather(
-            layer_mats[layer_number].astype(jnp.bfloat16), "fsdp", axis=0, tiled=True
-        )
+        weight_tensors = kept_weights[layer_number]
         residual_gradient, grad_matrix, grad_vector = layer_backward(
             residual_gradient,
             weight_tensors,
@@ -336,10 +327,7 @@
     grad_norm = jnp.sqrt(lax.psum(squares, ("fsdp", "ns")))
     clip = jnp.minimum(1.0, clip_bound / (grad_norm + 1e-06))
     momentum = momentum_decay * layer_momentum + clip * mat_total
-    orth_half = newton_schulz(lax.dynamic_slice_in_dim(momentum, side * half_depth, half_depth, 2))
-    orth = lax.all_gather(shortened(orth_half[:, :, None]), "ns", axis=2, tiled=True).reshape(
-        layers, columns, width
-    )
+    orth = newton_schulz(momentum)
     clipped = clip * row_total
     new_first = first_decay * row_first + (1.0 - first_decay) * clipped
     new_second = second_decay * row_second + (1.0 - second_decay) * clipped * clipped

time: 1630 us -> 1150 us (0.71)
  waiting for transfers between devices: 1150 us -> 600 us
  matrix products: 182 us -> 227 us
  other arithmetic: 106 us -> 134 us
    psum x5 -> x0, waiting for transfers between devices: 247 us -> none  [gram_total(): return lax.psum(local.astype(jnp.bfloat16), 'ns').astype(jnp.float32)]
    reduce_scatter x2, waiting for transfers between devices: 543 us -> 297 us  [body(): lax.psum_scatter(grad_matrix, 'fsdp', scatter_dimension=0, tiled=True)]
    concatenate x2, other arithmetic: 45.2 us -> 84.8 us  [layer_backward(): jnp.concatenate([part.astype(jnp.bfloat16) for part in (grad_qkv, grad_ou...]
    unnamed x18 -> x12, waiting for transfers between devices: 91.2 us -> 58.8 us
    all_gather x1 -> x0, waiting for transfers between devices: 26.9 us -> none  [body(): lax.all_gather(shortened(orth_half[:, :, None]), 'ns', axis=2, tiled=True)]
    dot_general x5, matrix products: 33.4 us -> 53 us  [newton_schulz(): jnp.einsum('lce,led->lcd', poly, blocks, precision=HIGHEST)]
    dot_general x5, matrix products: 24.4 us -> 43.1 us  [newton_schulz(): jnp.einsum('lce,lef->lcf', gram, gram, precision=HIGHEST)]
    unnamed x315 -> x295, local copies, waits for them, and re-layouts: 32.9 us -> 28.5 us
  transfers between devices with their start and end apart: 15 -> 9, of which waited for: 13 -> 6; matrix products, arithmetic and copies ran while one was open for 8% -> 14% of each run, Pallas kernels for 0% -> 0%
where the time goes in v1:
time: 1150 us; the launch traced here: 1140 us
  waiting for transfers between devices  600 us (52%)
  matrix products  227 us (20%)
  other arithmetic  134 us (12%)
  blocking collectives  83.9 us (7%)
  local copies, waits for them, and re-layouts  65.7 us (6%)
  between operations  26.4 us (2%)
    reduce_scatter x2, waiting for transfers between devices, body(): lax.psum_scatter(grad_matrix, 'fsdp', scatter_dimension=0, tiled=True)  297 us
    all_gather x2, waiting for transfers between devices, gather_layer(): lax.all_gather(shard.astype(jnp.bfloat16), 'fsdp', axis=0, tiled=True)  187 us
    concatenate x2, other arithmetic, layer_backward(): jnp.concatenate([part.astype(jnp.bfloat16) for part in (grad_qkv, grad_ou...  84.8 us
    psum x2, blocking collectives, body(): lax.psum((jnp.sum(weights_value * losses), jnp.sum(weights_value)), ('fsd...  83.9 us
    unnamed x12, waiting for transfers between devices  58.8 us
    psum x1, waiting for transfers between devices, body(): lax.psum(mat_grad.astype(jnp.bfloat16), 'ns').astype(jnp.float32)  57.3 us
    dot_general x5, matrix products, newton_schulz(): jnp.einsum('lce,led->lcd', poly, blocks, precision=HIGHEST)  53 us
    dot_general x5, matrix products, gram_of(): return jnp.einsum('lcd,led->lce', blocks, blocks, precision=HIGHEST)  45.7 us
  transfers between devices with their start and end apart: 9, of which 6 were waited for; matrix products, arithmetic and copies ran while one was open for 14% of the time, Pallas kernels for 0%

profile of v1, /device:TPU:0, one launch (start us, length us, event | category | flops | bytes accessed | tf_op | source)
XLA Modules:
  0.0 1138.4 jit_solution(16553062554574963302)
XLA Ops:
  9.0 2.2 convert.16
  14.0 43.2 %psum.36 = f32[]{:T(128)} all-reduce(f32[]{:T(128)} %bitcast.29), channel_id=1, replica_groups=mesh['fsdp'=16,'ns'=2] {'fsdp','ns'}, use_global_device_ids=true, to_apply=%region_24.25 | all-reduce | flops 1 | bytes 8 | tf_op jit(solution)/shard_map/psum | solution.py:269
  60.6 4.5 copy.99
  65.1 2.5 convert_element_type.244
  74.6 94.2 %all-gather.8.cloned.1.call-done = bf16[1,9216,768]{2,1,0:T(8,128)(2,1)} async-done(((bf16[1,576,768]{2,1,0:T(8,128)(2,1)}), bf16[1,9216,768]{2,1,0:T(8,128)(2,1)}) %all-gather.8.cloned.1.call-update) | async-done | bytes 14155792 | tf_op jit(solution)/shard_map/all_gather | solution.py:79
  168.8 3.3 fusion.14
  178.1 3.6 copy-done.56
  187.4 93.1 %all-gather.10.cloned.1.call-done = bf16[1,9216,768]{2,1,0:T(8,128)(2,1)} async-done(((bf16[1,576,768]{2,1,0:T(8,128)(2,1)}), bf16[1,9216,768]{2,1,0:T(8,128)(2,1)}) %all-gather.10.cloned.1.call-update) | async-done | bytes 14155792 | tf_op jit(solution)/shard_map/all_gather | solution.py:79
  280.5 4.4 fusion.15
  284.9 2.8 copy.102
  290.1 3.0 fusion.91
  293.2 2.9 copy-done.47
  323.6 3.1 fusion.138
  329.4 5.8 convert_reduce_fusion
  335.2 5.1 multiply_reduce_fusion.3
  342.2 2.5 convolution_convert_fusion.9
  346.7 3.1 multiply_reduce_fusion.1
  354.1 4.4 multiply_reduce_fusion.4
  360.4 2.8 convert_reduce_fusion.1
  363.2 2.1 multiply_reduce_fusion.5
  383.9 3.5 multiply_reduce_fusion.6
  394.9 14.4 %concatenate.43 = f32[1540,768]{1,0:T(8,128)} concatenate(f32[768,768]{1,0:T(8,128)} %convolution_bitcast_fusion, f32[512,768]{1,0:T(8,128)} %broadcast_multiply_fusion, f32[256,768]{1,0:T(8,128)} %copy-done.29, f32[1,768]{1,0:T(1,128)S(1)} %stack.100, f32[1,768]{1,0:T(1,128)S(1)} %stack.101, f32[1,768]{1,0:T(1,128)S(1)} %mul.832, f32[1,768]{1,0:T(1,128)S(1)} %copy-done.108), dimensions={0} | concatenate | bytes 9461760 | tf_op jit(solution)/shard_map/concatenate | solution.py:303
  409.3 6.0 copy.124
  422.7 42.4 %pad_maximum_fusion = bf16[9216,768]{1,0:T(8,128)(2,1)} fusion(bf16[3072,768]{1,0:T(8,128)(2,1)S(1)} %convolution_convert_fusion.3, bf16[3072,768]{1,0:T(8,128)(2,1)S(1)} %convolution_convert_fusion.4, bf16[768,768]{1,0:T(8,128)(2,1)S(1)} %convolution_convert_fusion.7, bf16[2304,768]{1,0:T(8,128)(2,1)S(1)} %convolution_convert_fusion.5), kind=kLoop, calls=%fused_computation | loop fusion | flops 56623104 | bytes 28311552 | tf_op jit(solution)/shard_map/concatenate | solution.py:167
  472.8 42.4 %pad_maximum_fusion.1 = bf16[9216,768]{1,0:T(8,128)(2,1)} fusion(bf16[3072,768]{1,0:T(8,128)(2,1)S(1)} %convolution_convert_fusion, bf16[3072,768]{1,0:T(8,128)(2,1)S(1)} %convolution_convert_fusion.1, bf16[768,768]{1,0:T(8,128)(2,1)S(1)} %convolution_convert_fusion.6, bf16[2304,768]{1,0:T(8,128)(2,1)S(1)} %convolution_convert_fusion.2), kind=kLoop, calls=%fused_computation.1 | loop fusion | flops 56623104 | bytes 28311552 | tf_op jit(solution)/shard_map/concatenate | solution.py:167
  517.1 58.0 %reduce-scatter.16.cloned.1.call-done = f32[48,1540]{1,0:T(8,128)} async-done(((f32[768,1540]{1,0:T(8,128)}), f32[48,1540]{1,0:T(8,128)}) %reduce-scatter.16.cloned.1.call-update) | async-done | bytes 295696
  576.8 147.5 %reduce-scatter.12.cloned.1.call-done = bf16[576,768]{1,0:T(8,128)(2,1)} async-done(((bf16[9216,768]{1,0:T(8,128)(2,1)}), bf16[576,768]{1,0:T(8,128)(2,1)}) %reduce-scatter.12.cloned.1.call-update) | async-done | bytes 884752 | tf_op jit(solution)/shard_map/reduce_scatter | solution.py:297
  724.4 149.4 %reduce-scatter.14.cloned.1.call-done = bf16[576,768]{1,0:T(8,128)(2,1)} async-done(((bf16[9216,768]{1,0:T(8,128)(2,1)}), bf16[576,768]{1,0:T(8,128)(2,1)}) %reduce-scatter.14.cloned.1.call-update) | async-done | bytes 884752 | tf_op jit(solution)/shard_map/reduce_scatter | solution.py:297
  873.8 2.8 pad_maximum_fusion.2
  878.7 57.3 %all-reduce.4.cloned.1.call-done = (bf16[2,576,768]{2,1,0:T(8,128)(2,1)}, bf16[1564,48]{0,1:T(8,128)(2,1)}) async-done(((bf16[2,576,768]{2,1,0:T(8,128)(2,1)}, bf16[1564,48]{0,1:T(8,128)(2,1)}), (bf16[2,576,768]{2,1,0:T(8,128)(2,1)}, bf16[1564,48]{0,1:T(8,128)(2,1)})) %all-reduce.4.cloned.1.call-update) | async-done | bytes 1919632 | tf_op jit(solution)/shard_map/psum | solution.py:321
  940.9 40.6 %all-reduce = (f32[]{:T(128)}, f32[]{:T(128)}) all-reduce(f32[]{:T(128)} %bitcast.28, f32[]{:T(128)S(6)} %add.433), channel_id=1, replica_groups=mesh['fsdp'=16,'ns'=2] {'fsdp','ns'}, use_global_device_ids=true, to_apply=%region_23.24 | all-reduce | flops 2 | bytes 16 | tf_op jit(solution)/shard_map/psum | solution.py:269
  982.3 2.2 add_multiply_fusion.1
  985.3 2.5 multiply_add_fusion.5
  987.7 9.2 select_reduce_fusion
  996.9 8.9 fusion.99
  1005.8 9.7 multiply_add_fusion.4
  1015.6 8.9 fusion.152
  1024.5 8.9 fusion.153
  1033.4 9.3 multiply_add_fusion.3
  1042.8 9.2 fusion.154
  1051.9 8.5 fusion.155
  1060.4 9.6 multiply_add_fusion.2
  1070.0 9.1 fusion.156
  1079.1 8.5 fusion.157
  1087.6 9.4 multiply_add_fusion.1
  1097.0 9.3 fusion.158
  1106.4 8.4 fusion.159
  1115.7 14.9 %add_multiply_fusion = (f32[2,576,768]{2,1,0:T(8,128)}, f32[2,576,768]{2,1,0:T(8,128)}, f32[2,576,768]{2,1,0:T(8,128)}) fusion(f32[2,576,768]{2,1,0:T(8,128)S(1)} %copy-done.37, f32[2,576,768]{2,1,0:T(8,128)} %param.21, f32[2,576,768]{2,1,0:T(8,128)S(1)} %copy-done.8, f32[2,576,768]{2,1,0:T(8,128)S(1)} %multiply_add_fusion.1, ...), kind=kOutput, calls=%fused_computation.32 | convolution fusion | flops 6127902720 | bytes 30081024 | tf_op jit(solution)/shard_map/lce,led->lcd/dot_general | solution.py:204
  (454 shorter events, 112.5 us)
Async XLA Ops:
  7.2 64.4 %copy-start = (bf16[1,256,768]{2,1,0:T(8,128)(2,1)S(1)}, bf16[1,256,768]{2,1,0:T(8,128)(2,1)}, u32[]{:S(2)}) copy-start(bf16[1,256,768]{2,1,0:T(8,128)(2,1)} %param.14) | copy-start | bytes 1179652
  7.2 53.5 %all-gather.6.cloned.1.call-start = ((), (), s32[]{:S(2)}) async-start(), calls=%async_computation.5 | async-start | bytes 2715648 | tf_op jit(solution)/shard_map/all_gather | solution.py:230
  9.0 159.9 %all-gather.8.cloned.1.call-start = ((), (), s32[]{:S(2)}) async-start(), calls=%async_computation.8 | async-start | bytes 15040512 | tf_op jit(solution)/shard_map/all_gather | solution.py:79
  11.2 46.0 %copy-start.135 = (s32[1,256]{1,0:T(1,128)S(1)}, s32[1,256]{1,0:T(1,128)}, u32[]{:S(2)}) copy-start(s32[1,256]{1,0:T(1,128)} %param.15) | copy-start | bytes 3076
  11.2 48.1 %copy-start.21 = (bf16[1000,512]{1,0:T(8,128)(2,1)S(1)}, bf16[1000,512]{1,0:T(8,128)(2,1)}, u32[]{:S(2)}) copy-start(bf16[1000,512]{1,0:T(8,128)(2,1)} %param.18) | copy-start | bytes 3072004
  12.6 268.0 %all-gather.10.cloned.1.call-start = ((), (), s32[]{:S(2)}) async-start(), calls=%async_computation.9 | async-start | bytes 15040512 | tf_op jit(solution)/shard_map/all_gather | solution.py:79
  13.3 501.9 %reduce-scatter.20.cloned.1.call-start = ((), (), s32[]{:S(2)}) async-start(), calls=%async_computation.12 | async-start | bytes 417792
  70.9 101.2 %copy-start.78 = (f32[768]{0:T(1024)}, f32[768]{0:T(1024)S(1)}, u32[]{:S(2)}) copy-start(f32[768]{0:T(1024)S(1)} %get-tuple-element.54) | copy-start | bytes 9220
  71.0 101.2 %copy-start.100 = (f32[768]{0:T(1024)}, f32[768]{0:T(1024)S(1)}, u32[]{:S(2)}) copy-start(f32[768]{0:T(1024)S(1)} %get-tuple-element.53) | copy-start | bytes 9220
  71.0 107.1 %copy-start.50 = (f32[768]{0:T(1024)}, f32[768]{0:T(1024)S(1)}, u32[]{:S(2)}) copy-start(f32[768]{0:T(1024)S(1)} %get-tuple-element.56) | copy-start | bytes 9220
  71.0 107.1 %copy-start.54 = (f32[768]{0:T(1024)}, f32[768]{0:T(1024)S(1)}, u32[]{:S(2)}) copy-start(f32[768]{0:T(1024)S(1)} %get-tuple-element.55) | copy-start | bytes 9220
  71.0 111.8 %copy-start.69 = (f32[768]{0:T(1024)}, f32[768]{0:T(1024)S(1)}, u32[]{:S(2)}) copy-start(f32[768]{0:T(1024)S(1)} %get-tuple-element.49) | copy-start | bytes 9220
  73.7 98.5 %copy-start.4 = (f32[256,768]{1,0:T(8,128)}, f32[256,768]{1,0:T(8,128)S(1)}, u32[]{:S(2)}) copy-start(f32[256,768]{1,0:T(8,128)S(1)} %get-tuple-element.121) | copy-start | bytes 2359300
  73.7 104.4 %copy-start.64 = (f32[256]{0:T(256)}, f32[256]{0:T(256)S(1)}, u32[]{:S(2)}) copy-start(f32[256]{0:T(256)S(1)} %broadcast_multiply_fusion.16) | copy-start | bytes 3076
  73.9 98.2 %copy-start.72 = (f32[256]{0:T(256)}, f32[256]{0:T(256)S(1)}, u32[]{:S(2)}) copy-start(f32[256]{0:T(256)S(1)} %add_rsqrt_fusion.5) | copy-start | bytes 3076
  74.2 97.9 %copy-start.87 = (f32[256]{0:T(256)}, f32[256]{0:T(256)S(1)}, u32[]{:S(2)}) copy-start(f32[256]{0:T(256)S(1)} %broadcast_multiply_fusion.15) | copy-start | bytes 3076
  74.6 97.6 %copy-start.112 = (f32[256]{0:T(256)}, f32[256]{0:T(256)S(1)}, u32[]{:S(2)}) copy-start(f32[256]{0:T(256)S(1)} %add_rsqrt_fusion.4) | copy-start | bytes 3076
  184.3 96.2 %copy-start.75 = (f32[768]{0:T(1024)S(1)}, f32[768]{0:T(1024)}, u32[]{:S(2)}) copy-start(f32[768]{0:T(1024)} %get-tuple-element.46) | copy-start | bytes 9220
  184.3 96.2 %copy-start.98 = (f32[768]{0:T(1024)S(1)}, f32[768]{0:T(1024)}, u32[]{:S(2)}) copy-start(f32[768]{0:T(1024)} %get-tuple-element.45) | copy-start | bytes 9220
  186.3 98.6 %copy-start.89 = (f32[256]{0:T(256)}, f32[256]{0:T(256)S(1)}, u32[]{:S(2)}) copy-start(f32[256]{0:T(256)S(1)} %broadcast_multiply_fusion.13) | copy-start | bytes 3076
  187.4 97.5 %copy-start.114 = (f32[256]{0:T(256)}, f32[256]{0:T(256)S(1)}, u32[]{:S(2)}) copy-start(f32[256]{0:T(256)S(1)} %add_rsqrt_fusion.2) | copy-start | bytes 3076
  289.7 6.4 copy-start.47
  329.3 11.0 copy-start.106
  346.7 12.8 %slice-start = ((s8[14155776]{0:T(1024)(128)(4,1)}), s8[1572864]{0:T(1024)(128)(4,1)S(1)}, s32[]{:S(2)}) async-start(s8[14155776]{0:T(1024)(128)(4,1)} %bitcast.272), calls=%async_computation.14 | async-start | bytes 3145728
  349.8 9.6 slice-start.1
  351.5 8.0 slice-start.2
  377.4 6.4 copy-start.6
  377.4 6.4 copy-start.51
  377.4 6.4 copy-start.55
  377.5 6.4 copy-start.65
  377.5 6.4 copy-start.74
  377.5 6.4 copy-start.79
  377.5 6.4 copy-start.88
  377.5 6.4 copy-start.113
  382.2 134.0 %reduce-scatter.18.cloned.1.call-start = ((), (), s32[]{:S(2)}) async-start(), calls=%async_computation.11 | async-start | bytes 417792
  394.1 181.0 %reduce-scatter.16.cloned.1.call-start = ((), (), s32[]{:S(2)}) async-start(), calls=%async_computation.10 | async-start | bytes 5431296
  415.3 309.1 %reduce-scatter.12.cloned.1.call-start = ((), (), s32[]{:S(2)}) async-start(), calls=%async_computation.6 | async-start | bytes 15040512 | tf_op jit(solution)/shard_map/reduce_scatter | solution.py:297
  465.3 408.6 %reduce-scatter.14.cloned.1.call-start = ((), (), s32[]{:S(2)}) async-start(), calls=%async_computation.7 | async-start | bytes 15040512 | tf_op jit(solution)/shard_map/reduce_scatter | solution.py:297
  515.2 420.8 %all-reduce.4.cloned.1.call-start = ((), (), s32[]{:S(2)}) async-start(), calls=%async_computation.13 | async-start | bytes 3858432 | tf_op jit(solution)/shard_map/psum | solution.py:321
  936.0 46.3 %copy-start.42 = (f32[1564,48]{0,1:T(8,128)S(1)}, f32[1564,48]{0,1:T(8,128)}, u32[]{:S(2)}) copy-start(f32[1564,48]{0,1:T(8,128)} %param.23) | copy-start | bytes 900868
  936.0 46.3 %copy-start.48 = (f32[1564,48]{0,1:T(8,128)S(1)}, f32[1564,48]{0,1:T(8,128)}, u32[]{:S(2)}) copy-start(f32[1564,48]{0,1:T(8,128)} %param.24) | copy-start | bytes 900868
  937.8 47.4 %copy-start.30 = (bf16[2,576,768]{2,1,0:T(8,128)(2,1)S(1)}, bf16[2,576,768]{2,1,0:T(8,128)(2,1)}, u32[]{:S(2)}) copy-start(bf16[2,576,768]{2,1,0:T(8,128)(2,1)} %get-tuple-element.83) | copy-start | bytes 5308420
  984.5 130.3 %copy-start.43 = (f32[1564,48]{0,1:T(8,128)}, f32[1564,48]{0,1:T(8,128)S(1)}, u32[]{:S(2)}) copy-start(f32[1564,48]{0,1:T(8,128)S(1)} %get-tuple-element.86) | copy-start | bytes 900868
  987.7 18.1 %copy-start.7 = (f32[2,576,768]{2,1,0:T(8,128)}, f32[2,576,768]{2,1,0:T(8,128)S(1)}, u32[]{:S(2)}) copy-start(f32[2,576,768]{2,1,0:T(8,128)S(1)} %multiply_add_fusion.5) | copy-start | bytes 10616836
  1106.3 8.5 copy-start.49
  1106.4 9.3 copy-start.8
  1106.4 9.3 copy-start.37
  1115.6 14.9 %copy-start.1 = (bf16[1,256,768]{2,1,0:T(8,128)(2,1)S(1)}, bf16[1,256,768]{2,1,0:T(8,128)(2,1)}, u32[]{:S(2)}) copy-start(bf16[1,256,768]{2,1,0:T(8,128)(2,1)} %param.14) | copy-start | bytes 1179652
  (106 other events, 285.4 us)
Sparse Core Ops, SparseCore 0:
  10.8 45.7 all-gather.5
  59.4 109.3 all-gather.7
  171.7 108.7 all-gather.9
  382.3 53.7 reduce-scatter.19
  439.9 54.5 reduce-scatter.17
  498.3 76.7 reduce-scatter.15
  579.8 144.5 reduce-scatter.11
  729.1 144.6 reduce-scatter.13
  877.4 58.5 all-reduce.3

commit v2 on v1

--- a/solution.py
+++ b/solution.py
@@ -1,8 +1,11 @@
+import functools
 import math
 
 import jax
 import jax.numpy as jnp
 from jax import lax
+from jax.experimental import pallas as pl
+from jax.experimental.pallas import tpu as pltpu
 from jax.sharding import PartitionSpec as P
 
 HEADS = 12
@@ -75,6 +78,470 @@
     return jnp.where(valid_mask[:, None, None, :] > 0, raw * HDIM ** (-0.5), -1000000000.0)
 
 
+BF = jnp.bfloat16
+F32 = jnp.float32
+MESH = pl.DeviceIdType.MESH
+PLANE = 4
+
+
+def guarded(pred, run):
+    if pred is None:
+        run()
+    else:
+        pl.when(pred)(run)
+
+
+def both(first, second):
+    if first is None:
+        return second
+    return first if second is None else jnp.logical_and(first, second)
+
+
+def rows_at(start, count):
+    return pl.ds(start if isinstance(start, int) else pl.multiple_of(start, 16), count)
+
+
+class Links:
+    def __init__(self, depth, send_sem, recv_sem):
+        self.depth, self.send_sem, self.recv_sem = depth, send_sem, recv_sem
+        self.me, self.x = lax.axis_index("fsdp"), lax.axis_index("ns")
+        self.z, self.y, self.c = self.me // PLANE, lax.rem(self.me // 2, 2), lax.rem(self.me, 2)
+        self.up = (self.at(self.z + 1, self.y, self.c), self.x)
+        self.down = (self.at(self.z - 1, self.y, self.c), self.x)
+        self.y_peer = (self.at(self.z, 1 - self.y, self.c), self.x)
+        self.c_peer = (self.at(self.z, self.y, 1 - self.c), self.x)
+        self.x_peer = (self.me, 1 - self.x)
+        self.count, self.sent, self.waited = 0, [], set()
+
+    def at(self, z, y, c):
+        return PLANE * z + 2 * y + c
+
+    def slot(self):
+        self.count += 1
+        return self.count - 1
+
+    def greet(self):
+        barrier = pltpu.get_barrier_semaphore()
+
+        def signal(device):
+            pl.semaphore_signal(barrier, inc=1, device_id=device, device_id_type=MESH)
+
+        for device in (self.y_peer, self.x_peer, self.c_peer):
+            signal(device)
+        pl.when(self.z < self.depth - 1)(lambda: signal(self.up))
+        pl.when(self.z > 0)(lambda: signal(self.down))
+        inner = (self.z < self.depth - 1).astype(jnp.int32) + (self.z > 0).astype(jnp.int32)
+        pl.semaphore_wait(barrier, 3 + inner)
+
+    def copy(self, slot, source, target, device):
+        return pltpu.make_async_remote_copy(
+            src_ref=source,
+            dst_ref=target,
+            send_sem=self.send_sem.at[slot],
+            recv_sem=self.recv_sem.at[slot],
+            device_id=device,
+            device_id_type=MESH,
+        )
+
+    def send(self, slot, source, target, device, pred=None):
+        copy = self.copy(slot, source, target, device)
+        guarded(pred, copy.start)
+        self.sent.append((slot, pred, copy))
+
+    def receive(self, slot, target, pred=None):
+        guarded(pred, self.copy(slot, target, target, self.c_peer).wait_recv)
+
+    def finish(self, slot=None):
+        for number, pred, copy in self.sent:
+            if number not in self.waited and (slot is None or number == slot):
+                guarded(pred, copy.wait_send)
+        if slot is not None:
+            self.waited.add(slot)
+
+
+def gather_item(links, own, target, count):
+    depth, z, y, c, x = links.depth, links.z, links.y, links.c, links.x
+    third = count // 3
+    begin = x * third
+    origin = (0, 0)
+    keys = [(side, far) for far in range(1, depth) for side in (-1, 1)]
+    z_slot = {key: links.slot() for key in keys}
+    y_slot = {key: links.slot() for key in keys + [origin]}
+    x_slot = {(key, o): links.slot() for key in keys + [origin] for o in (0, 1)}
+    c_slot = {(key, o): links.slot() for key in keys + [origin] for o in (0, 1)}
+
+    def part(shard):
+        return target(shard).at[rows_at(begin, 2 * third)]
+
+    def own_part():
+        return own.at[rows_at(begin, 2 * third)]
+
+    def third_of(shard, side):
+        return target(shard).at[rows_at(side * 2 * third, third)]
+
+    def shard(key, other, core=None):
+        return links.at(z + key[0] * key[1], 1 - y if other else y, c if core is None else core)
+
+    def exists(key):
+        if key == origin:
+            return None
+        return z >= key[1] if key[0] < 0 else z + key[1] < depth
+
+    def z_send(key):
+        for side in (-1, 1) if key == origin else (key[0],):
+            if key[1] + 1 < depth:
+                source = own_part() if key == origin else part(shard(key, 0))
+                links.send(
+                    z_slot[(side, key[1] + 1)],
+                    source,
+                    part(shard(key, 0)),
+                    links.up if side < 0 else links.down,
+                    both(exists(key), z < depth - 1 if side < 0 else z > 0),
+                )
+
+    def y_send(key):
+        source = own_part() if key == origin else part(shard(key, 0))
+        links.send(y_slot[key], source, part(shard(key, 0)), links.y_peer, exists(key))
+
+    def x_send(key, other):
+        block = third_of(shard(key, other), x)
+        links.send(x_slot[(key, other)], block, block, links.x_peer, exists(key))
+
+    def c_send(key, other):
+        whole = target(shard(key, other))
+        source = own if (key, other) == (origin, 0) else whole
+        links.send(c_slot[(key, other)], source, whole, links.c_peer, exists(key))
+
+    order = []
+    for far in range(1, depth):
+        order += [((side, far), 0) for side in (-1, 1)]
+        order += [(key, 1) for key in ([origin] if far == 1 else [(-1, far - 1), (1, far - 1)])]
+    order += [((side, depth - 1), 1) for side in (-1, 1)]
+
+    def start():
+        z_send(origin)
+        y_send(origin)
+        c_send(origin, 0)
+
+    def cross(keys_now):
+        for key in keys_now:
+            links.receive(y_slot[key], part(shard(key, 1)), exists(key))
+            x_send(key, 1)
+
+    def step(far):
+        for side in (-1, 1):
+            key = (side, far)
+            links.receive(z_slot[key], part(shard(key, 0)), exists(key))
+            z_send(key)
+            y_send(key)
+            x_send(key, 0)
+        cross([origin] if far == 1 else [(-1, far - 1), (1, far - 1)])
+        if far == depth - 1:
+            cross([(-1, far), (1, far)])
+
+    def share():
+        for key, other in order:
+            links.receive(x_slot[(key, other)], third_of(shard(key, other), 1 - x), exists(key))
+            c_send(key, other)
+
+    def settle():
+        for key, other in [(origin, 0)] + order:
+            links.receive(c_slot[(key, other)], target(shard(key, other, 1 - c)), exists(key))
+
+    return start, step, share, settle
+
+
+def gather_kernel(depth, halves, rows, mats, all_rows, all_mats, send_sem, recv_sem, local_sem):
+    links = Links(depth, send_sem, recv_sem)
+    links.greet()
+    layers, count = mats.shape[:2]
+    size = count // halves
+    own = [pltpu.make_async_copy(rows, all_rows.at[links.me], local_sem.at[0])]
+    items = [gather_item(links, rows, lambda shard: all_rows.at[shard], rows.shape[0])]
+    for layer in range(layers):
+        own.append(
+            pltpu.make_async_copy(
+                mats.at[layer], all_mats.at[layer, links.me], local_sem.at[1 + layer]
+            )
+        )
+        for half in range(halves):
+            block = pl.ds(half * size, size)
+
+            def target(shard, layer=layer, block=block):
+                return all_mats.at[layer, shard, block]
+
+            items.append(gather_item(links, mats.at[layer, block], target, size))
+    for copy in own:
+        copy.start()
+    items[0][0]()
+    for number, (_, step, _, _) in enumerate(items):
+        step(1)
+        step(2)
+        if number + 1 < len(items):
+            items[number + 1][0]()
+        if number > 0:
+            items[number - 1][2]()
+        for far in range(3, depth):
+            step(far)
+    items[-1][2]()
+    for item in items:
+        item[3]()
+    links.finish()
+    for copy in own:
+        copy.wait()
+
+
+def gather(depth, rows, mats):
+    layers, count, width = mats.shape
+    shards = PLANE * depth
+    halves = 2
+    slots = (1 + layers * halves) * 60
+    any_space = pl.BlockSpec(memory_space=pl.ANY)
+    return pl.pallas_call(
+        functools.partial(gather_kernel, depth, halves),
+        out_shape=(
+            jax.ShapeDtypeStruct((shards,) + rows.shape, BF),
+            jax.ShapeDtypeStruct((layers, shards, count, width), BF),
+        ),
+        in_specs=[any_space] * 2,
+        out_specs=[any_space] * 2,
+        scratch_shapes=[
+            pltpu.SemaphoreType.DMA((slots,)),
+            pltpu.SemaphoreType.DMA((slots,)),
+            pltpu.SemaphoreType.DMA((1 + layers,)),
+        ],
+        name="gather_weights",
+        compiler_params=pltpu.CompilerParams(collective_id=1, has_side_effects=True),
+    )(rows, mats)
+
+
+def accumulate(target, start, source, begin, count, step):
+    @pl.loop(0, count // step)
+    def _(turn):
+        here = rows_at(start + turn * step, step)
+        there = rows_at(begin + turn * step, step)
+        target[here, :] = (target[here, :].astype(F32) + source[there, :].astype(F32)).astype(BF)
+
+
+def scatter_group(links, dest, load, sizes, bufs, emit):
+    depth, z, y, c, x = links.depth, links.z, links.y, links.c, links.x
+    n, p, q, step = sizes
+    mine, core_in, x_in, y_in, z_in, z_last, final = bufs
+    core_slot, x_slot = [links.slot(), links.slot()], [links.slot(), links.slot()]
+    q_slot, p_slot, low_slot, high_slot, last_slot = (links.slot() for _ in range(5))
+    m = p + q
+    first = x * p
+    own_p, peer_p = x * m, (1 - x) * m
+    sides = ((0, 1 - y), (1, y))
+
+    def begin():
+        for i, side in sides:
+            load(i, side, mine.at[side], core_in.at[side], core_slot[i])
+
+    def stage_core():
+        for i, side in sides:
+            load(i, side, mine.at[side], None, None)
+            links.receive(core_slot[i], core_in.at[side])
+            accumulate(mine.at[side], 0, core_in.at[side], 0, n, step)
+            links.send(x_slot[i], mine.at[side, rows_at(peer_p, p)], x_in.at[side], links.x_peer)
+            if i == 0:
+                links.send(q_slot, mine.at[side, pl.ds(p, q)], y_in.at[pl.ds(0, q)], links.y_peer)
+
+    def stage_x():
+        for i, side in sides:
+            links.receive(x_slot[i], x_in.at[side])
+            accumulate(mine.at[side], own_p, x_in.at[side], 0, p, step)
+            if i == 0:
+                links.send(
+                    p_slot, mine.at[side, rows_at(own_p, p)], y_in.at[pl.ds(q, p)], links.y_peer
+                )
+        links.receive(q_slot, y_in.at[pl.ds(0, q)])
+        accumulate(mine.at[y], p, y_in, 0, q, step)
+
+    def stage_y():
+        links.receive(p_slot, y_in.at[pl.ds(q, p)])
+        accumulate(mine.at[y], own_p, y_in, q, p, step)
+
+    def stage_z(hop):
+        block = mine.at[y, rows_at(first, m)]
+
+        def take(slot, source, pred):
+            @pl.when(pred)
+            def _():
+                links.receive(slot, source)
+                accumulate(mine.at[y], first, source, 0, m, step)
+
+        if dest > 0:
+            if 1 <= hop <= dest:
+                take(low_slot, z_in, z == hop)
+            if hop < dest:
+                links.send(low_slot, block, z_in, links.up, z == hop)
+        if dest < depth - 1:
+            turn = depth - 1 - hop
+            if hop >= 1 and turn > dest:
+                take(high_slot, z_in, z == turn)
+            if turn > dest + 1:
+                links.send(high_slot, block, z_in, links.down, z == turn)
+            if turn == dest + 1:
+                links.send(high_slot, block, z_last, links.down, z == turn)
+            if turn == dest and hop >= 1:
+                take(high_slot, z_last, z == dest)
+        if hop == max(dest, depth - 1 - dest):
+            links.send(last_slot, block, final, links.x_peer, z == dest)
+
+    def stage_last():
+        links.finish(x_slot[1])
+        links.finish(last_slot)
+
+        @pl.when(z == dest)
+        def _():
+            links.receive(last_slot, final)
+            accumulate(mine.at[y], p, final, jnp.where(x == 0, 0, p), q, step)
+
+            @pl.loop(0, p // 16)
+            def _(turn):
+                there = rows_at(jnp.where(x == 0, q, 0) + turn * 16, 16)
+                mine[y, rows_at(peer_p + turn * 16, 16), :] = final[there, :]
+
+            emit(mine.at[y])
+
+    hops = [functools.partial(stage_z, hop) for hop in range(depth)]
+    return begin, [stage_core, stage_x, stage_y] + hops + [stage_last]
+
+
+def scatter_kernel(depth, layers, sub, lags, *refs):
+    grads, row_grad = refs[: 4 * layers], refs[4 * layers]
+    out, row_out = refs[4 * layers + 1 : 4 * layers + 3]
+    big, small = refs[4 * layers + 3 : 4 * layers + 10], refs[4 * layers + 10 : 4 * layers + 17]
+    send_sem, recv_sem, local_sem = refs[4 * layers + 17 :]
+    links = Links(depth, send_sem, recv_sem)
+    links.greet()
+    y, c = links.y, links.c
+    count = out.shape[1]
+    n = count // sub
+    p = n // 4 // 16 * 16
+    groups = []
+
+    def block_of(layer, shard, part):
+        row = shard * count + part * n
+        for matrix in grads[4 * layer : 4 * layer + 4]:
+            if row < matrix.shape[0]:
+                return matrix.at[pl.ds(row, n)]
+            row -= matrix.shape[0]
+
+    def add_group(dest, source, sizes, bufs, emit):
+        number = len(groups)
+
+        def load(i, side, mine, core_in, slot):
+            sem = local_sem.at[2 * number + i]
+            if core_in is None:
+                pltpu.make_async_copy(source(0, 0), mine, sem).wait()
+                return
+            for y_now in (0, 1):
+                for core in (0, 1):
+
+                    @pl.when(jnp.logical_and(side == y_now, c == core))
+                    def _():
+                        pltpu.make_async_copy(source(y_now, core), mine, sem).start()
+                        links.copy(slot, source(y_now, 1 - core), core_in, links.c_peer).start()
+
+            links.sent.append((slot, None, links.copy(slot, source(0, 0), core_in, links.c_peer)))
+
+        groups.append(scatter_group(links, dest, load, sizes, bufs, emit))
+
+    def write(target, sem):
+        def emit(result):
+            copy = pltpu.make_async_copy(result, target, sem)
+            copy.start()
+            copy.wait()
+
+        return emit
+
+    end_sem = local_sem.at[local_sem.shape[0] - 1]
+    for layer in reversed(range(layers)):
+        for part in range(sub):
+            for dest in (3, 0, 2, 1) if depth == 4 else reversed(range(depth)):
+                number, spot = len(groups), layer * sub + part
+                add_group(
+                    dest,
+                    lambda y_now, core, layer=layer, part=part, dest=dest: block_of(
+                        layer, links.at(dest, y_now, core), part
+                    ),
+                    (n, p, n - 2 * p, 48),
+                    [ref.at[number] for ref in big[:5]] + [ref.at[spot] for ref in big[5:]],
+                    write(out.at[layer, pl.ds(part * n, n)], end_sem),
+                )
+    rows = row_out.shape[0]
+    for dest in reversed(range(depth)):
+        add_group(
+            dest,
+            lambda y_now, core, dest=dest: row_grad.at[links.at(dest, y_now, core)],
+            (rows, 16, rows - 32, 16),
+            [ref.at[dest] for ref in small[:5]] + list(small[5:]),
+            write(row_out, end_sem),
+        )
+    for begin, _ in groups:
+        begin()
+    for turn in range(len(groups) + max(lags)):
+        for place, lag in enumerate(lags):
+            if 0 <= turn - lag < len(groups):
+                groups[turn - lag][1][place]()
+    links.finish()
+
+
+def scatter(depth, grads, row_grad):
+    layers = len(grads)
+    shards = PLANE * depth
+    width = grads[0][0].shape[1]
+    count = sum(part.shape[0] for part in grads[0]) // shards
+    sub = 3
+    n = count // sub
+    p = n // 4 // 16 * 16
+    m = n - p
+    blocks = layers * depth * sub
+    rows, lanes = row_grad.shape[1:]
+    row_m = rows - 16
+    lags = [0, 3, 6] + [9 + 3 * hop for hop in range(depth)] + [9 + 3 * depth]
+
+    def room(*shape):
+        return pltpu.VMEM(shape, BF)
+
+    any_space = pl.BlockSpec(memory_space=pl.ANY)
+    slots = (blocks + depth) * 9
+    return pl.pallas_call(
+        functools.partial(scatter_kernel, depth, layers, sub, lags),
+        out_shape=(
+            jax.ShapeDtypeStruct((layers, count, width), BF),
+            jax.ShapeDtypeStruct((rows, lanes), BF),
+        ),
+        in_specs=[any_space] * (4 * layers + 1),
+        out_specs=[any_space] * 2,
+        scratch_shapes=[
+            room(blocks, 2, n, width),
+            room(blocks, 2, n, width),
+            room(blocks, 2, p, width),
+            room(blocks, m, width),
+            room(blocks, m, width),
+            room(layers * sub, m, width),
+            room(layers * sub, m, width),
+            room(depth, 2, rows, lanes),
+            room(depth, 2, rows, lanes),
+            room(depth, 2, 16, lanes),
+            room(depth, row_m, lanes),
+            room(depth, row_m, lanes),
+            room(row_m, lanes),
+            room(row_m, lanes),
+            pltpu.SemaphoreType.DMA((slots,)),
+            pltpu.SemaphoreType.DMA((slots,)),
+            pltpu.SemaphoreType.DMA((2 * (blocks + depth) + 1,)),
+        ],
+        name="scatter_gradients",
+        compiler_params=pltpu.CompilerParams(
+            collective_id=2, has_side_effects=True, vmem_limit_bytes=60 * 1024 * 1024
+        ),
+    )(*[part for layer in grads for part in layer], row_grad)
+
+
 def gather_layer(shard):
     return lax.all_gather(shard.astype(jnp.bfloat16), "fsdp", axis=0, tiled=True)
 
@@ -164,9 +631,7 @@
         resid, vector[0], matmul(project_grad, weight_tensors[: 3 * width])
     )
     residual_gradient = mixed_grad + first_in
-    grad_matrix = jnp.concatenate(
-        [part.astype(jnp.bfloat16) for part in (grad_qkv, grad_out, grad_up, grad_down)], 0
-    )
+    grad_matrix = [part.astype(BF) for part in (grad_qkv, grad_out, grad_up, grad_down)]
     grad_vector = jnp.concatenate(
         [
             jnp.stack(
@@ -188,26 +653,69 @@
     return (residual_gradient, grad_matrix, grad_vector)
 
 
-def gram_of(blocks):
-    return jnp.einsum("lcd,led->lce", blocks, blocks, precision=HIGHEST)
-
-
 def newton_schulz(blocks):
-    gram = gram_of(blocks)
-    frob = jnp.sqrt(jnp.trace(gram, axis1=1, axis2=2))[:, None, None] + 1e-07
+    frob = jnp.sqrt(jnp.sum(blocks * blocks, axis=(1, 2), keepdims=True)) + 1e-07
     blocks = blocks / frob
-    gram = gram / (frob * frob)
+    unit = jnp.eye(blocks.shape[1], dtype=jnp.float32)
     for turn in range(NS_STEPS):
-        poly = coeff_cubic * gram + coeff_quintic * jnp.einsum(
-            "lce,lef->lcf", gram, gram, precision=HIGHEST
+        shift = 1.0 if turn >= NS_STEPS - 2 else 0.0
+        short = blocks.astype(BF)
+        gram = jnp.einsum("lcd,led->lce", short, short, preferred_element_type=F32) - shift * unit
+        low = gram.astype(BF)
+        square = jnp.einsum("lce,lef->lcf", low, low, preferred_element_type=F32)
+        poly = (coeff_cubic + 2.0 * shift * coeff_quintic) * gram + coeff_quintic * square
+        stay = coeff_linear + shift * (coeff_cubic + shift * coeff_quintic)
+        blocks = stay * blocks + jnp.einsum(
+            "lce,led->lcd", poly.astype(BF), short, preferred_element_type=F32
         )
-        blocks = coeff_linear * blocks + jnp.einsum("lce,led->lcd", poly, blocks, precision=HIGHEST)
-        if turn + 1 < NS_STEPS:
-            gram = gram_of(blocks)
     return blocks
 
 
-def body(
+def updates(
+    clipped,
+    momentum,
+    orth,
+    layer_mats,
+    layer_zero,
+    layer_ema,
+    row_params,
+    row_zero,
+    row_ema,
+    row_first,
+    row_second,
+):
+    layers, _, width = layer_mats.shape
+    shard_width = row_params.shape[1]
+    front = PIX + EMB + SEQ + 4
+    new_first = first_decay * row_first + (1.0 - first_decay) * clipped
+    new_second = second_decay * row_second + (1.0 - second_decay) * clipped * clipped
+    down_bias_grad = clipped[front:].reshape(layers, 12, shard_width)[:, 7]
+    new_mats = layer_mats - muon_rate * (0.2 * math.sqrt(width) * orth + weight_decay * layer_mats)
+    ema_mats = ema_decay * layer_ema + (1.0 - ema_decay) * new_mats
+    mixed_mats = mix_share * new_mats + (1.0 - mix_share) * layer_zero
+    step_size = (
+        new_first
+        / (1.0 - first_decay**STEPS_DONE)
+        / (jnp.sqrt(new_second / (1.0 - second_decay**STEPS_DONE)) + adam_floor)
+    )
+    new_rows = row_params - adam_rate * (step_size + weight_decay * row_params)
+    ema_rows = ema_decay * row_ema + (1.0 - ema_decay) * new_rows
+    mixed_rows = mix_share * new_rows + (1.0 - mix_share) * row_zero
+    return (
+        new_mats,
+        momentum,
+        ema_mats,
+        mixed_mats,
+        new_rows,
+        new_first,
+        new_second,
+        ema_rows,
+        mixed_rows,
+        down_bias_grad,
+    )
+
+
+def plain_body(
     patches,
     pad_mask,
     labels,
@@ -294,7 +802,9 @@
             saved_activations[layer_number],
         )
         grad_mats[layer_number], grad_vecs[layer_number] = (
-            lax.psum_scatter(grad_matrix, "fsdp", scatter_dimension=0, tiled=True),
+            lax.psum_scatter(
+                jnp.concatenate(grad_matrix, 0), "fsdp", scatter_dimension=0, tiled=True
+            ),
             lax.psum_scatter(grad_vector, "fsdp", scatter_dimension=1, tiled=True),
         )
     embed_grad, gain_pre, shift_pre = norm_backward(embedded, head_vec[0], residual_gradient)
@@ -316,7 +826,6 @@
     side = lax.axis_index("ns")
     half_depth = width // pairs
     half_rows = row_grad.shape[0] // pairs
-    shard_width = row_grad.shape[1]
     mat_total, row_total = (
         lax.psum(mat_grad.astype(jnp.bfloat16), "ns").astype(jnp.float32),
         lax.psum(row_grad.astype(jnp.bfloat16), "ns").astype(jnp.float32),
@@ -328,36 +837,152 @@
     clip = jnp.minimum(1.0, clip_bound / (grad_norm + 1e-06))
     momentum = momentum_decay * layer_momentum + clip * mat_total
     orth = newton_schulz(momentum)
-    clipped = clip * row_total
-    new_first = first_decay * row_first + (1.0 - first_decay) * clipped
-    new_second = second_decay * row_second + (1.0 - second_decay) * clipped * clipped
-    down_bias_grad = clipped[front:].reshape(layers, 12, shard_width)[:, 7]
-    new_mats = layer_mats - muon_rate * (0.2 * math.sqrt(width) * orth + weight_decay * layer_mats)
-    ema_mats = ema_decay * layer_ema + (1.0 - ema_decay) * new_mats
-    mixed_mats = mix_share * new_mats + (1.0 - mix_share) * layer_zero
-    step_size = (
-        new_first
-        / (1.0 - first_decay**STEPS_DONE)
-        / (jnp.sqrt(new_second / (1.0 - second_decay**STEPS_DONE)) + adam_floor)
-    )
-    new_rows = row_params - adam_rate * (step_size + weight_decay * row_params)
-    ema_rows = ema_decay * row_ema + (1.0 - ema_decay) * new_rows
-    mixed_rows = mix_share * new_rows + (1.0 - mix_share) * row_zero
-    return (
-        loss_sum,
-        weight_sum,
-        grad_norm,
-        new_mats,
+    return (loss_sum, weight_sum, grad_norm) + updates(
+        clip * row_total,
         momentum,
-        ema_mats,
-        mixed_mats,
-        new_rows,
-        new_first,
-        new_second,
-        ema_rows,
-        mixed_rows,
-        down_bias_grad,
-    )
+        orth,
+        layer_mats,
+        layer_zero,
+        layer_ema,
+        row_params,
+        row_zero,
+        row_ema,
+        row_first,
+        row_second,
+    )
+
+
+def fast_body(
+    patches,
+    pad_mask,
+    labels,
+    loss_weights,
+    class_emb,
+    layer_mats,
+    layer_zero,
+    layer_ema,
+    layer_momentum,
+    row_params,
+    row_zero,
+    row_ema,
+    row_first,
+    row_second,
+):
+    layers, columns, width = layer_mats.shape
+    images, seq, pixels = patches.shape
+    shards = lax.axis_size("fsdp")
+    depth = shards // PLANE
+    rows, share = row_params.shape
+    front = PIX + EMB + SEQ + 4
+    lanes = -(-rows // 128) * 128
+    valid_mask = pad_mask.astype(F32)
+    sent_rows = jnp.pad(row_params.T.astype(BF), ((0, 0), (0, lanes - rows)))
+    all_rows, all_mats = gather(depth, sent_rows, layer_mats.astype(BF))
+    table = all_rows.reshape(width, lanes)
+    weights = all_mats.reshape(layers, shards * columns, width)
+    patch_weight, proj = table[:, :PIX], table[:, PIX : PIX + EMB]
+    position = table[:, PIX + EMB : PIX + EMB + SEQ].T.astype(F32)
+    vectors = table[:, PIX + EMB + SEQ : rows].T.astype(F32)
+    head_vec = vectors[:4]
+    layer_vector_params = vectors[4:].reshape(layers, 12, width)
+    flat_patches = patches.reshape(images * seq, pixels)
+    embedded = (
+        matmul_nt(flat_patches, patch_weight).reshape(images, seq, width) + position
+    ).reshape(images * seq, width)
+    resid = norm_forward(embedded, head_vec[0], head_vec[1])
+    saved_activations = []
+    for layer_number in range(layers):
+        resid, saved_activation = layer_forward(
+            resid, weights[layer_number], layer_vector_params[layer_number], valid_mask
+        )
+        saved_activations.append(saved_activation)
+    counts = jnp.sum(valid_mask, -1, keepdims=True)
+    pooled = jnp.sum(resid.reshape(images, seq, width) * valid_mask[..., None], 1) / counts
+    pooled_norm = norm_forward(pooled, head_vec[2], head_vec[3]).astype(BF)
+    feature = matmul(pooled_norm, proj)
+    inv_length = lax.rsqrt(jnp.sum(feature * feature, -1, keepdims=True) + unit_epsilon)
+    unit_feat = (feature * inv_length).astype(BF)
+    classes = class_emb.astype(F32)
+    class_unit = (
+        classes * lax.rsqrt(jnp.sum(classes * classes, -1, keepdims=True) + unit_epsilon)
+    ).astype(BF)
+    logits = logit_scale * matmul_nt(unit_feat, class_unit)
+    top_logit = jnp.max(logits, -1, keepdims=True)
+    shifted = jnp.exp(logits - top_logit)
+    total_exp = jnp.sum(shifted, -1, keepdims=True)
+    log_norm = top_logit + jnp.log(total_exp)
+    onehot = (jnp.arange(logits.shape[1])[None, :] == labels[:, None]).astype(F32)
+    losses = log_norm[:, 0] - jnp.sum(onehot * logits, -1)
+    weights_value = loss_weights.astype(F32)
+    logit_grad = weights_value[:, None] * (shifted / total_exp - onehot)
+    unit_grad = logit_scale * jnp.dot(logit_grad, class_unit.astype(F32), precision=HIGHEST)
+    feat_grad = inv_length * unit_grad - feature * inv_length**3 * jnp.sum(
+        unit_grad * feature, -1, keepdims=True
+    )
+    grad_proj = jnp.dot(pooled_norm.astype(F32).T, feat_grad, precision=HIGHEST)
+    pooled_grad, gain_post, shift_post = norm_backward(
+        pooled,
+        head_vec[2],
+        lax.dot_general(
+            feat_grad, proj.astype(F32), (((1,), (1,)), ((), ())), precision=HIGHEST
+        ),
+    )
+    upstream = (valid_mask[..., None] * (pooled_grad / counts)[:, None, :]).reshape(
+        images * seq, width
+    )
+    grad_mats = [None] * layers
+    grad_vecs = [None] * layers
+    for layer_number in reversed(range(layers)):
+        upstream, grad_mats[layer_number], grad_vecs[layer_number] = layer_backward(
+            upstream,
+            weights[layer_number],
+            layer_vector_params[layer_number],
+            valid_mask,
+            saved_activations[layer_number],
+        )
+    embed_grad, gain_pre, shift_pre = norm_backward(embedded, head_vec[0], upstream)
+    position_grad = jnp.sum(embed_grad.reshape(images, seq, width), 0)
+    patch_grad = matmul_tn(embed_grad.astype(BF), flat_patches)
+    vector_grad = jnp.concatenate(
+        [jnp.stack([gain_pre, shift_pre, gain_post, shift_post])] + grad_vecs, 0
+    )
+    row_grad = jnp.concatenate(
+        [patch_grad, grad_proj, position_grad.T, vector_grad.T, jnp.zeros((width, lanes - rows))], 1
+    )
+    mat_total, row_total = scatter(
+        depth, grad_mats, row_grad.astype(BF).reshape(shards, share, lanes)
+    )
+    mat_total = mat_total.astype(F32)
+    row_total = row_total.astype(F32)[:, :rows].T
+    squares = jnp.sum(mat_total * mat_total) + jnp.sum(row_total * row_total)
+    loss_sum, weight_sum, squares = lax.psum(
+        (jnp.sum(weights_value * losses), jnp.sum(weights_value), squares), ("fsdp", "ns")
+    )
+    grad_norm = jnp.sqrt(squares / lax.axis_size("ns")) / weight_sum
+    clip = jnp.minimum(1.0, clip_bound / (grad_norm + 1e-06)) / weight_sum
+    momentum = momentum_decay * layer_momentum + clip * mat_total
+    orth = newton_schulz(momentum)
+    return (loss_sum, weight_sum, grad_norm) + updates(
+        clip * row_total,
+        momentum,
+        orth,
+        layer_mats,
+        layer_zero,
+        layer_ema,
+        row_params,
+        row_zero,
+        row_ema,
+        row_first,
+        row_second,
+    )
+
+
+def body(*args):
+    count, share = args[5].shape[1], args[9].shape[1]
+    planes = lax.axis_size("fsdp") % PLANE == 0 and lax.axis_size("ns") == 2
+    if planes and count % 192 == 0 and share % 48 == 0:
+        return fast_body(*args)
+    return plain_body(*args)
 
 
 def solution(mesh):

time: 1150 us -> 708 us (0.62)
  waiting for transfers between devices: 600 us -> 0 us
  Pallas kernels: 0 us -> 301 us
  other arithmetic: 134 us -> 64.4 us
  blocking collectives: 83.9 us -> 38.3 us
  matrix products: 227 us -> 189 us
  local copies, waits for them, and re-layouts: 65.7 us -> 94.1 us
  between operations: 26.4 us -> 13.9 us
    pallas_call x0 -> x2, Pallas kernels: none -> 301 us  [the longest x1 169 us: scatter(): pl.pallas_call(functools.partial(scatter_kernel, depth, layers, sub, lags...]
    reduce_scatter x2 -> x0, waiting for transfers between devices: 297 us -> none  [body(): lax.psum_scatter(grad_matrix, 'fsdp', scatter_dimension=0, tiled=True)]
    all_gather x3 -> x0, waiting for transfers between devices: 187 us -> none  [the longest x2 187 us: gather_layer(): lax.all_gather(shard.astype(jnp.bfloat16), 'fsdp', axis=0, tiled=True)]
    concatenate x2 -> x0, other arithmetic: 84.8 us -> none  [layer_backward(): jnp.concatenate([part.astype(jnp.bfloat16) for part in (grad_qkv, grad_ou...]
    dot_general x17 -> x12, matrix products: 147 us -> 83.7 us  [the longest x5 53.2 us: newton_schulz(): jnp.einsum('lce,led->lcd', poly.astype(BF), short, preferred_element_type...]
    unnamed x12 -> x0, waiting for transfers between devices: 58.8 us -> none
    psum x1 -> x0, waiting for transfers between devices: 57.3 us -> none  [body(): lax.psum(mat_grad.astype(jnp.bfloat16), 'ns').astype(jnp.float32)]
    psum x2 -> x1, blocking collectives: 83.9 us -> 38.3 us  [fast_body(): lax.psum((jnp.sum(weights_value * losses), jnp.sum(weights_value), square...]
  transfers between devices with their start and end apart: 9 -> 0, of which waited for: 6 -> 0; matrix products, arithmetic and copies ran while one was open for 14% -> 0% of each run, Pallas kernels for 0% -> 0%
where the time goes in v2:
time: 708 us; the launch traced here: 700 us
  Pallas kernels  301 us (43%)
  matrix products  189 us (27%)
  local copies, waits for them, and re-layouts  94.1 us (13%)
  other arithmetic  64.4 us (9%)
  blocking collectives  38.3 us (5%)
  between operations  13.9 us (2%)
    pallas_call x1, Pallas kernels, scatter(): pl.pallas_call(functools.partial(scatter_kernel, depth, layers, sub, lags...  169 us
    pallas_call x1, Pallas kernels, gather(): pl.pallas_call(functools.partial(gather_kernel, depth, halves), out_shape...  132 us
    dot_general x5, matrix products, newton_schulz(): jnp.einsum('lce,led->lcd', poly.astype(BF), short, preferred_element_type...  53.2 us
    psum x1, blocking collectives, fast_body(): lax.psum((jnp.sum(weights_value * losses), jnp.sum(weights_value), square...  38.3 us
    dot_general x10, matrix products, matmul_nt(): lax.dot_general(left, right, (((1,), (1,)), ((), ())), preferred_element_...  31.3 us
    dot_general x9, matrix products, matmul(): return jnp.dot(left, right, preferred_element_type=jnp.float32)  30.7 us
    dot_general x9, matrix products, matmul_tn(): lax.dot_general(left, right, (((0,), (0,)), ((), ())), preferred_element_...  27.4 us
    dot_general x5, matrix products, newton_schulz(): jnp.einsum('lcd,led->lce', short, short, preferred_element_type=F32)  25.4 us

profile of v2, /device:TPU:0, one launch (start us, length us, event | category | flops | bytes accessed | tf_op | source)
XLA Modules:
  0.0 700.4 jit_solution(13285468603763998610)
XLA Ops:
  9.5 3.4 convert_element_type.325.mats
  12.9 131.8 %gather_weights.1 = (bf16[16,48,1664]{2,1,0:T(8,128)(2,1)}, bf16[2,16,576,768]{3,2,1,0:T(8,128)(2,1)}) custom-call(bf16[48,1664]{1,0:T(8,128)(2,1)} %pad.4.rows, bf16[2,576,768]{2,1,0:T(8,128)(2,1)} %convert_element_type.325.mats), custom_call_target="tpu_custom_call" | custom-call | tf_op jit(solution)/shard_map/gather_weights/pallas_call | solution.py:300
  151.0 5.3 fusion.188
  156.4 21.1 %fusion.187 = (bf16[1,16,576,768]{3,2,1,0:T(8,128)(2,1)}, bf16[1,16,576,768]{3,2,1,0:T(8,128)(2,1)}) fusion(bf16[2,16,576,768]{3,2,1,0:T(8,128)(2,1)} %get-tuple-element.18), kind=kLoop, calls=%fused_computation.328 | loop fusion | bytes 56623104 | tf_op jit(solution)/shard_map/slice | solution.py:896
  185.1 2.8 copy-done.13
  192.7 3.2 fusion.184
  197.4 2.5 fusion.35
  199.9 2.8 copy.95
  207.8 2.8 fusion.183
  211.9 4.1 fusion.22
  216.0 5.7 fusion.82
  246.5 3.1 fusion.177
  258.1 7.1 %fusion.200 = (bf16[3072]{0:T(1024)(128)(2,1)}, bf16[256,3072]{1,0:T(8,128)(2,1)}) fusion(f32[256,3072]{1,0:T(8,128)} %copy-done.143, bf16[9216,768]{1,0:T(8,128)(2,1)} %bitcast.258, f32[768]{0:T(1024)} %divide_reduce_fusion, f32[256]{0:T(256)} %bitcast.307), kind=kOutput, calls=%fused_computation.341 | convolution fusion | flops 1217000448 | bytes 9448448 | tf_op jit(solution)/shard_map/dot_general | solution.py:44
  266.5 5.1 fusion.199
  277.4 2.7 convert_reduce_fusion.3
  280.9 2.5 convolution_convert_fusion.10
  288.0 2.7 fusion.61
  292.4 4.0 convolution_convert_fusion.refs_7_
  296.5 3.9 convolution_convert_fusion.1.refs_6_
  303.9 2.6 fusion.198
  310.5 2.3 copy.104
  318.0 3.0 convolution_convert_fusion.2.refs_4_
  321.0 6.4 fusion.197
  328.7 5.1 fusion.196
  334.4 2.3 copy.105
  339.1 2.6 convert_reduce_fusion.1
  342.6 2.5 convolution_convert_fusion.9
  351.8 4.3 convolution_convert_fusion.3.refs_3_
  356.2 3.8 convolution_convert_fusion.4.refs_2_
  364.0 2.6 fusion.195
  378.3 2.5 fusion.111
  380.8 3.0 concatenate.37
  386.9 4.9 concatenate.39.refs_8_
  391.7 3.8 convolution_convert_fusion.5.refs_0_
  395.5 169.3 %scatter_gradients.1 = (bf16[2,576,768]{2,1,0:T(8,128)(2,1)}, bf16[48,1664]{1,0:T(8,128)(2,1)}) custom-call(bf16[2304,768]{1,0:T(8,128)(2,1)} %convolution_convert_fusion.5.refs_0_, bf16[768,768]{1,0:T(8,128)(2,1)} %convolution_convert_fusion.8.refs_1_, bf16[3072,768]{1,0:T(8,128)(2,1)} %convolution_convert_fusion.4.refs_2_, ...), custom_call_target="tpu_custom_call" | custom-call | tf_op jit(solution)/shard_map/scatter_gradients/pallas_call | solution.py:511
  566.6 3.0 fusion.36
  570.9 38.3 %all-reduce.1 = (f32[]{:T(128)}, f32[]{:T(128)}, f32[]{:T(128)}) all-reduce(f32[]{:T(128)} %bitcast.28, f32[]{:T(128)} %bitcast.29, f32[]{:T(128)S(6)} %add.476), channel_id=1, replica_groups=mesh['fsdp'=16,'ns'=2] {'fsdp','ns'}, use_global_device_ids=true, to_apply=%region_23.24 | all-reduce | flops 3 | bytes 24 | tf_op jit(solution)/shard_map/psum | solution.py:958
  613.0 2.4 add_multiply_fusion.1
  620.2 3.3 fusion.103
  623.4 10.3 %multiply_add_fusion.4 = f32[2,576,768]{2,1,0:T(8,128)} fusion(f32[2,576,576]{2,1,0:T(8,128)} %fusion.103, f32[2,576,768]{2,1,0:T(8,128)} %copy-done.37, f32[2]{0:T(128)S(1)} %sqrt_add_fusion), kind=kOutput, calls=%fused_computation.42 | convolution fusion | flops 1791369216 | bytes 9732104 | tf_op jit(solution)/shard_map/lce,led->lcd/dot_general | solution.py:668
  633.7 4.7 fusion.100
  638.4 7.8 %multiply_add_fusion.3 = f32[2,576,768]{2,1,0:T(8,128)} fusion(f32[2,576,768]{2,1,0:T(8,128)} %multiply_add_fusion.4, f32[2,576,576]{2,1,0:T(8,128)S(1)} %fusion.100), kind=kOutput, calls=%fused_computation.41 | convolution fusion | flops 1789599744 | bytes 9732096 | tf_op jit(solution)/shard_map/lce,led->lcd/dot_general | solution.py:668
  646.2 4.6 fusion.97
  650.8 7.8 %multiply_add_fusion.2 = f32[2,576,768]{2,1,0:T(8,128)} fusion(f32[2,576,768]{2,1,0:T(8,128)} %multiply_add_fusion.3, f32[2,576,576]{2,1,0:T(8,128)S(1)} %fusion.97), kind=kOutput, calls=%fused_computation.40 | convolution fusion | flops 1789599744 | bytes 9732096 | tf_op jit(solution)/shard_map/lce,led->lcd/dot_general | solution.py:668
  658.6 6.6 fusion.94
  665.2 10.3 %multiply_add_fusion.1 = f32[2,576,768]{2,1,0:T(8,128)} fusion(f32[2,576,768]{2,1,0:T(8,128)} %multiply_add_fusion.2, f32[2,576,576]{2,1,0:T(8,128)} %fusion.94, f32[576,576]{1,0:T(8,128)S(1)} %copy-done.14), kind=kOutput, calls=%fused_computation.39 | convolution fusion | flops 1790926848 | bytes 11059200 | tf_op jit(solution)/shard_map/lce,led->lcd/dot_general | solution.py:668
  675.6 6.3 fusion.91
  681.8 17.0 %add_multiply_fusion = (f32[2,576,768]{2,1,0:T(8,128)}, f32[2,576,768]{2,1,0:T(8,128)}, f32[2,576,768]{2,1,0:T(8,128)}) fusion(f32[2,576,768]{2,1,0:T(8,128)} %param.20, f32[2,576,768]{2,1,0:T(8,128)} %param.21, f32[2,576,768]{2,1,0:T(8,128)} %param.19, f32[2,576,768]{2,1,0:T(8,128)} %multiply_add_fusion.1, f32[2,576,576]{2,1,0:T(8,128)} %fusion.91, ...), kind=kOutput, calls=%fused_computation.36 | convolution fusion | flops 1799774208 | bytes 28753920 | tf_op jit(solution)/shard_map/lce,led->lcd/dot_general | solution.py:668
  (421 shorter events, 126.3 us)
Async XLA Ops:
  0.6 147.7 %copy-start = (bf16[1,256,768]{2,1,0:T(8,128)(2,1)S(1)}, bf16[1,256,768]{2,1,0:T(8,128)(2,1)}, u32[]{:S(2)}) copy-start(bf16[1,256,768]{2,1,0:T(8,128)(2,1)} %param.14) | copy-start | bytes 1179652
  4.5 176.1 %copy-start.139 = (pred[256]{0:T(512)(128)(4,1)}, pred[256]{0:T(512)(128)(4,1)S(1)}, u32[]{:S(2)}) copy-start(pred[256]{0:T(512)(128)(4,1)S(1)} %broadcast_compare_fusion) | copy-start | bytes 772
  147.7 29.7 %copy-start.55 = (f32[768]{0:T(1024)}, f32[768]{0:T(1024)S(1)}, u32[]{:S(2)}) copy-start(f32[768]{0:T(1024)S(1)} %get-tuple-element.53) | copy-start | bytes 9220
  147.7 29.7 %copy-start.58 = (f32[768]{0:T(1024)}, f32[768]{0:T(1024)S(1)}, u32[]{:S(2)}) copy-start(f32[768]{0:T(1024)S(1)} %get-tuple-element.54) | copy-start | bytes 9220
  147.7 29.7 %copy-start.67 = (f32[768]{0:T(1024)}, f32[768]{0:T(1024)S(1)}, u32[]{:S(2)}) copy-start(f32[768]{0:T(1024)S(1)} %get-tuple-element.52) | copy-start | bytes 9220
  147.7 29.8 %copy-start.113 = (f32[768]{0:T(1024)}, f32[768]{0:T(1024)S(1)}, u32[]{:S(2)}) copy-start(f32[768]{0:T(1024)S(1)} %get-tuple-element.51) | copy-start | bytes 9220
  150.2 27.3 %copy-start.3 = (f32[768,256]{1,0:T(8,128)}, f32[768,256]{1,0:T(8,128)S(1)}, u32[]{:S(2)}) copy-start(f32[768,256]{1,0:T(8,128)S(1)} %get-tuple-element.105) | copy-start | bytes 2359300
  150.3 27.3 %copy-start.73 = (f32[256]{0:T(256)}, f32[256]{0:T(256)S(1)}, u32[]{:S(2)}) copy-start(f32[256]{0:T(256)S(1)} %broadcast_multiply_fusion.14) | copy-start | bytes 3076
  150.4 27.1 %copy-start.80 = (f32[256]{0:T(256)}, f32[256]{0:T(256)S(1)}, u32[]{:S(2)}) copy-start(f32[256]{0:T(256)S(1)} %add_rsqrt_fusion.5) | copy-start | bytes 3076
  150.7 26.8 %copy-start.86 = (f32[256]{0:T(256)}, f32[256]{0:T(256)S(1)}, u32[]{:S(2)}) copy-start(f32[256]{0:T(256)S(1)} %broadcast_multiply_fusion.13) | copy-start | bytes 3076
  151.0 26.5 %copy-start.97 = (f32[256]{0:T(256)}, f32[256]{0:T(256)S(1)}, u32[]{:S(2)}) copy-start(f32[256]{0:T(256)S(1)} %add_rsqrt_fusion.4) | copy-start | bytes 3076
  156.4 21.2 %copy-start.32 = (bf16[1,4,576,768]{3,2,1,0:T(8,128)(2,1)}, bf16[1,4,576,768]{3,2,1,0:T(8,128)(2,1)S(1)}, u32[]{:S(2)}) copy-start(bf16[1,4,576,768]{3,2,1,0:T(8,128)(2,1)S(1)} %get-tuple-element.90) | copy-start | bytes 10616836
  182.6 5.3 copy-start.13
  185.0 5.8 copy-start.64
  185.0 5.8 copy-start.109
  185.0 5.7 copy-start.119
  210.7 5.3 copy-start.9
  216.0 5.8 copy-start.143
  285.4 5.3 copy-start.27
  285.4 5.4 copy-start.47
  312.8 5.2 copy-start.8
  312.8 5.2 copy-start.22
  312.8 5.2 copy-start.71
  312.8 5.2 copy-start.92
  312.8 5.2 copy-start.103
  312.8 5.2 copy-start.115
  338.5 6.7 copy-start.129
  338.5 6.6 copy-start.131
  364.0 9.1 %copy-start.5 = (f32[768,256]{1,0:T(8,128)S(1)}, f32[768,256]{1,0:T(8,128)}, u32[]{:S(2)}) copy-start(f32[768,256]{1,0:T(8,128)} %copy-done.3) | copy-start | bytes 2359300
  364.0 9.1 %copy-start.57 = (f32[768]{0:T(1024)S(1)}, f32[768]{0:T(1024)}, u32[]{:S(2)}) copy-start(f32[768]{0:T(1024)} %copy-done.55) | copy-start | bytes 9220
  364.0 9.1 %copy-start.60 = (f32[768]{0:T(1024)S(1)}, f32[768]{0:T(1024)}, u32[]{:S(2)}) copy-start(f32[768]{0:T(1024)} %copy-done.58) | copy-start | bytes 9220
  366.6 11.5 %copy-start.15 = (f32[256,768]{0,1:T(8,128)S(1)}, f32[256,768]{0,1:T(8,128)}, u32[]{:S(2)}) copy-start(f32[256,768]{0,1:T(8,128)} %copy.99) | copy-start | bytes 2359300
  366.6 11.5 %copy-start.16 = (f32[256,768]{0,1:T(8,128)S(1)}, f32[256,768]{0,1:T(8,128)}, u32[]{:S(2)}) copy-start(f32[256,768]{0,1:T(8,128)} %copy.104) | copy-start | bytes 2359300
  366.6 11.5 %copy-start.17 = (f32[256,768]{0,1:T(8,128)S(1)}, f32[256,768]{0,1:T(8,128)}, u32[]{:S(2)}) copy-start(f32[256,768]{0,1:T(8,128)} %copy.105) | copy-start | bytes 2359300
  366.6 11.5 %copy-start.63 = (f32[768]{0:T(1024)S(1)}, f32[768]{0:T(1024)}, u32[]{:S(2)}) copy-start(f32[768]{0:T(1024)} %get-tuple-element.37) | copy-start | bytes 9220
  366.6 11.5 %copy-start.66 = (f32[768]{0:T(1024)S(1)}, f32[768]{0:T(1024)}, u32[]{:S(2)}) copy-start(f32[768]{0:T(1024)} %get-tuple-element.47) | copy-start | bytes 9220
  373.0 5.0 copy-start.18
  373.1 5.0 copy-start.40
  373.1 5.0 copy-start.43
  373.1 5.0 copy-start.50
  386.1 5.6 copy-start.20
  386.1 5.6 copy-start.69
  386.1 5.6 copy-start.76
  395.5 217.5 %copy-start.48 = (f32[1564,48]{0,1:T(8,128)S(1)}, f32[1564,48]{0,1:T(8,128)}, u32[]{:S(2)}) copy-start(f32[1564,48]{0,1:T(8,128)} %param.23) | copy-start | bytes 900868
  395.5 217.5 %copy-start.52 = (f32[1564,48]{0,1:T(8,128)S(1)}, f32[1564,48]{0,1:T(8,128)}, u32[]{:S(2)}) copy-start(f32[1564,48]{0,1:T(8,128)} %param.24) | copy-start | bytes 900868
  395.5 217.5 %copy-start.53 = (f32[1564,48]{0,1:T(8,128)S(1)}, f32[1564,48]{0,1:T(8,128)}, u32[]{:S(2)}) copy-start(f32[1564,48]{0,1:T(8,128)} %param.26) | copy-start | bytes 900868
  564.8 52.5 %copy-start.25 = (bf16[2,576,768]{2,1,0:T(8,128)(2,1)S(1)}, bf16[2,576,768]{2,1,0:T(8,128)(2,1)}, u32[]{:S(2)}) copy-start(bf16[2,576,768]{2,1,0:T(8,128)(2,1)} %get-tuple-element.19) | copy-start | bytes 5308420
  658.6 6.6 copy-start.14
  (97 other events, 337.3 us)

commit v3 on v2

--- a/solution.py
+++ b/solution.py
@@ -542,6 +542,221 @@
     )(*[part for layer in grads for part in layer], row_grad)
 
 
+def finish_kernel(
+    shards,
+    sides,
+    hyper,
+    stats,
+    grad,
+    row_grad,
+    momentum,
+    mats,
+    zero,
+    ema,
+    totals,
+    new_momentum,
+    new_mats,
+    new_ema,
+    new_mixed,
+    grad_v,
+    row_v,
+    m_v,
+    mats_v,
+    zero_v,
+    ema_v,
+    x_v,
+    short_v,
+    low_v,
+    note,
+    inbox,
+    send_sem,
+    recv_sem,
+    in_sem,
+    out_sem,
+):
+    me = lax.axis_index("fsdp") * sides + lax.axis_index("ns")
+    everyone = shards * sides
+    layers, count, width = grad.shape
+    pairs = [(grad, grad_v), (row_grad, row_v), (momentum, m_v)]
+    pairs += [(mats, mats_v), (zero, zero_v), (ema, ema_v)]
+    loads = [pltpu.make_async_copy(a, b, in_sem.at[i]) for i, (a, b) in enumerate(pairs)]
+    for load in loads:
+        load.start()
+    barrier = pltpu.get_barrier_semaphore()
+
+    def others(run):
+        for number in range(everyone):
+            pl.when(me != number)(functools.partial(run, number))
+
+    def place(number):
+        return (number // sides, number % sides)
+
+    others(
+        lambda number: pl.semaphore_signal(
+            barrier, inc=1, device_id=place(number), device_id_type=MESH
+        )
+    )
+    loads[0].wait()
+    loads[1].wait()
+    part = count // 3
+
+    def blocks(run):
+        @pl.loop(0, layers * 3)
+        def _(turn):
+            run(turn // 3, rows_at(lax.rem(turn, 3) * part, part))
+
+    note[...] = stats[...]
+    lane = lax.broadcasted_iota(jnp.int32, (8, 128), 1)
+    sub = lax.broadcasted_iota(jnp.int32, (8, 128), 0)
+
+    def add_squares(block):
+        value = block.astype(F32)
+        total = jnp.sum(value * value)
+        note[...] += jnp.where((lane == 0) & (sub == 0), total, 0.0)
+
+    blocks(lambda layer, rows: add_squares(grad_v[layer, rows, :]))
+    add_squares(row_v[...])
+    pl.semaphore_wait(barrier, everyone - 1)
+
+    def mail(number):
+        return pltpu.make_async_remote_copy(
+            src_ref=note,
+            dst_ref=inbox.at[me],
+            send_sem=send_sem.at[number],
+            recv_sem=recv_sem.at[me],
+            device_id=place(number),
+            device_id_type=MESH,
+        )
+
+    def collect(number):
+        pltpu.make_async_remote_copy(
+            src_ref=note,
+            dst_ref=inbox.at[number],
+            send_sem=send_sem.at[number],
+            recv_sem=recv_sem.at[number],
+            device_id=place(number),
+            device_id_type=MESH,
+        ).wait_recv()
+
+    others(lambda number: mail(number).start())
+    inbox[pl.ds(me, 1)] = note[...][None]
+    others(collect)
+    summed = jnp.sum(inbox[...], 0)
+    others(lambda number: mail(number).wait_send())
+
+    def pick(index):
+        return jnp.sum(jnp.where((lane == index) & (sub == 0), summed, 0.0))
+
+    loss_sum, weight_sum = pick(1), pick(2)
+    norm = jnp.sqrt(jnp.full((8, 128), pick(0) / sides)) / weight_sum
+    clip = jnp.minimum(1.0, clip_bound / (norm + 1e-06)) / weight_sum
+    totals[...] = jnp.where(
+        lane == 0,
+        loss_sum,
+        jnp.where(lane == 1, weight_sum, jnp.where(lane == 2, norm, clip)),
+    )
+    factor = clip[:1, :1]
+    loads[2].wait()
+    stores = []
+    for layer in range(layers):
+        total = jnp.zeros((1, 1), F32)
+        for third in range(3):
+            rows = pl.ds(third * part, part)
+            value = momentum_decay * m_v[layer, rows, :] + factor * grad_v[layer, rows, :].astype(F32)
+            m_v[layer, rows, :] = value
+            total += jnp.sum(value * value, keepdims=True)
+        store = pltpu.make_async_copy(m_v.at[layer], new_momentum.at[layer], out_sem.at[layer])
+        store.start()
+        stores.append(store)
+        inverse = 1.0 / (jnp.sqrt(total) + 1e-07)
+        for third in range(3):
+            rows = pl.ds(third * part, part)
+            value = m_v[layer, rows, :] * inverse
+            x_v[layer, rows, :] = value
+            short_v[0, layer, rows, :] = value.astype(BF)
+
+    row_id = lax.broadcasted_iota(jnp.int32, (part, count), 0)
+    col_id = lax.broadcasted_iota(jnp.int32, (part, count), 1)
+
+    @pl.loop(0, NS_STEPS)
+    def _(turn):
+        now, later = lax.rem(turn, 2), 1 - lax.rem(turn, 2)
+        shift = jnp.where(turn >= NS_STEPS - 2, 1.0, 0.0)
+        linear = coeff_cubic + 2.0 * shift * coeff_quintic
+        stay = coeff_linear + shift * (coeff_cubic + shift * coeff_quintic)
+        for layer in range(layers):
+            for third in range(3):
+                rows = pl.ds(third * part, part)
+                gram = matmul_nt(short_v[now, layer, rows, :], short_v[now, layer])
+                gram -= jnp.where(row_id + third * part == col_id, shift, 0.0)
+                low_v[layer, rows, :] = gram.astype(BF)
+        for layer in range(layers):
+            for third in range(3):
+                rows = pl.ds(third * part, part)
+                low = low_v[layer, rows, :]
+                poly = linear * low.astype(F32) + coeff_quintic * matmul(low, low_v[layer])
+                value = stay * x_v[layer, rows, :] + matmul(poly.astype(BF), short_v[now, layer])
+                x_v[layer, rows, :] = value
+                short_v[later, layer, rows, :] = value.astype(BF)
+
+    for load in loads[3:]:
+        load.wait()
+    for layer in range(layers):
+        for third in range(3):
+            rows = pl.ds(third * part, part)
+            old = mats_v[layer, rows, :]
+            value = old - muon_rate * (
+                hyper * x_v[layer, rows, :] + weight_decay * old
+            )
+            mats_v[layer, rows, :] = value
+            ema_v[layer, rows, :] = ema_decay * ema_v[layer, rows, :] + (1.0 - ema_decay) * value
+            zero_v[layer, rows, :] = mix_share * value + (1.0 - mix_share) * zero_v[layer, rows, :]
+            for turn, (source, target) in enumerate(
+                ((mats_v, new_mats), (ema_v, new_ema), (zero_v, new_mixed))
+            ):
+                sem = out_sem.at[layers + (layer * 3 + third) * 3 + turn]
+                store = pltpu.make_async_copy(source.at[layer, rows], target.at[layer, rows], sem)
+                store.start()
+                stores.append(store)
+    for store in stores:
+        store.wait()
+
+
+def finish(shards, sides, stats, grad, row_grad, momentum, mats, zero, ema):
+    layers, count, width = grad.shape
+    everyone = shards * sides
+    full = jax.ShapeDtypeStruct(mats.shape, F32)
+    any_space = pl.BlockSpec(memory_space=pl.ANY)
+    vmem = pl.BlockSpec(memory_space=pltpu.VMEM)
+    return pl.pallas_call(
+        functools.partial(finish_kernel, shards, sides, 0.2 * math.sqrt(width)),
+        out_shape=(jax.ShapeDtypeStruct((8, 128), F32), full, full, full, full),
+        in_specs=[vmem] + [any_space] * 6,
+        out_specs=[vmem] + [any_space] * 4,
+        scratch_shapes=[
+            pltpu.VMEM(grad.shape, BF),
+            pltpu.VMEM(row_grad.shape, BF),
+            pltpu.VMEM(mats.shape, F32),
+            pltpu.VMEM(mats.shape, F32),
+            pltpu.VMEM(mats.shape, F32),
+            pltpu.VMEM(mats.shape, F32),
+            pltpu.VMEM(mats.shape, F32),
+            pltpu.VMEM((2,) + mats.shape, BF),
+            pltpu.VMEM((layers, count, count), BF),
+            pltpu.VMEM((8, 128), F32),
+            pltpu.VMEM((everyone, 8, 128), F32),
+            pltpu.SemaphoreType.DMA((everyone,)),
+            pltpu.SemaphoreType.DMA((everyone,)),
+            pltpu.SemaphoreType.DMA((6,)),
+            pltpu.SemaphoreType.DMA((layers * 10,)),
+        ],
+        name="clip_and_orthogonalize",
+        compiler_params=pltpu.CompilerParams(
+            collective_id=3, has_side_effects=True, vmem_limit_bytes=56 * 1024 * 1024
+        ),
+    )(stats, grad, row_grad, momentum, mats, zero, ema)
+
+
 def gather_layer(shard):
     return lax.all_gather(shard.astype(jnp.bfloat16), "fsdp", axis=0, tiled=True)
 
@@ -671,28 +886,11 @@
     return blocks
 
 
-def updates(
-    clipped,
-    momentum,
-    orth,
-    layer_mats,
-    layer_zero,
-    layer_ema,
-    row_params,
-    row_zero,
-    row_ema,
-    row_first,
-    row_second,
-):
-    layers, _, width = layer_mats.shape
-    shard_width = row_params.shape[1]
+def row_updates(clipped, layers, row_params, row_zero, row_ema, row_first, row_second):
     front = PIX + EMB + SEQ + 4
     new_first = first_decay * row_first + (1.0 - first_decay) * clipped
     new_second = second_decay * row_second + (1.0 - second_decay) * clipped * clipped
-    down_bias_grad = clipped[front:].reshape(layers, 12, shard_width)[:, 7]
-    new_mats = layer_mats - muon_rate * (0.2 * math.sqrt(width) * orth + weight_decay * layer_mats)
-    ema_mats = ema_decay * layer_ema + (1.0 - ema_decay) * new_mats
-    mixed_mats = mix_share * new_mats + (1.0 - mix_share) * layer_zero
+    down_bias_grad = clipped[front:].reshape(layers, 12, row_params.shape[1])[:, 7]
     step_size = (
         new_first
         / (1.0 - first_decay**STEPS_DONE)
@@ -701,18 +899,7 @@
     new_rows = row_params - adam_rate * (step_size + weight_decay * row_params)
     ema_rows = ema_decay * row_ema + (1.0 - ema_decay) * new_rows
     mixed_rows = mix_share * new_rows + (1.0 - mix_share) * row_zero
-    return (
-        new_mats,
-        momentum,
-        ema_mats,
-        mixed_mats,
-        new_rows,
-        new_first,
-        new_second,
-        ema_rows,
-        mixed_rows,
-        down_bias_grad,
-    )
+    return (new_rows, new_first, new_second, ema_rows, mixed_rows, down_bias_grad)
 
 
 def plain_body(
@@ -837,18 +1024,11 @@
     clip = jnp.minimum(1.0, clip_bound / (grad_norm + 1e-06))
     momentum = momentum_decay * layer_momentum + clip * mat_total
     orth = newton_schulz(momentum)
-    return (loss_sum, weight_sum, grad_norm) + updates(
-        clip * row_total,
-        momentum,
-        orth,
-        layer_mats,
-        layer_zero,
-        layer_ema,
-        row_params,
-        row_zero,
-        row_ema,
-        row_first,
-        row_second,
+    new_mats = layer_mats - muon_rate * (0.2 * math.sqrt(width) * orth + weight_decay * layer_mats)
+    ema_mats = ema_decay * layer_ema + (1.0 - ema_decay) * new_mats
+    mixed_mats = mix_share * new_mats + (1.0 - mix_share) * layer_zero
+    return (loss_sum, weight_sum, grad_norm, new_mats, momentum, ema_mats, mixed_mats) + row_updates(
+        clip * row_total, layers, row_params, row_zero, row_ema, row_first, row_second
     )
 
 
@@ -952,28 +1132,25 @@
     mat_total, row_total = scatter(
         depth, grad_mats, row_grad.astype(BF).reshape(shards, share, lanes)
     )
-    mat_total = mat_total.astype(F32)
-    row_total = row_total.astype(F32)[:, :rows].T
-    squares = jnp.sum(mat_total * mat_total) + jnp.sum(row_total * row_total)
-    loss_sum, weight_sum, squares = lax.psum(
-        (jnp.sum(weights_value * losses), jnp.sum(weights_value), squares), ("fsdp", "ns")
-    )
-    grad_norm = jnp.sqrt(squares / lax.axis_size("ns")) / weight_sum
-    clip = jnp.minimum(1.0, clip_bound / (grad_norm + 1e-06)) / weight_sum
-    momentum = momentum_decay * layer_momentum + clip * mat_total
-    orth = newton_schulz(momentum)
-    return (loss_sum, weight_sum, grad_norm) + updates(
-        clip * row_total,
-        momentum,
-        orth,
+    lane = lax.broadcasted_iota(jnp.int32, (8, 128), 1)
+    first = lax.broadcasted_iota(jnp.int32, (8, 128), 0) == 0
+    stats = jnp.where(first & (lane == 1), jnp.sum(weights_value * losses), 0.0)
+    stats = jnp.where(first & (lane == 2), jnp.sum(weights_value), stats)
+    totals, momentum, new_mats, ema_mats, mixed_mats = finish(
+        shards,
+        lax.axis_size("ns"),
+        stats,
+        mat_total,
+        row_total,
+        layer_momentum,
         layer_mats,
         layer_zero,
         layer_ema,
-        row_params,
-        row_zero,
-        row_ema,
-        row_first,
-        row_second,
+    )
+    loss_sum, weight_sum, grad_norm, clip = (totals[0, turn] for turn in range(4))
+    clipped = clip * row_total.astype(F32)[:, :rows].T
+    return (loss_sum, weight_sum, grad_norm, new_mats, momentum, ema_mats, mixed_mats) + row_updates(
+        clipped, layers, row_params, row_zero, row_ema, row_first, row_second
     )
 
 

time: 708 us -> 632 us (0.89)
  matrix products: 189 us -> 110 us
  Pallas kernels: 301 us -> 343 us
  blocking collectives: 38.3 us -> 0 us
  local copies, waits for them, and re-layouts: 94.1 us -> 104 us
    dot_general x10 -> x0, matrix products: 78.7 us -> none  [the longest x5 53.2 us: newton_schulz(): jnp.einsum('lce,led->lcd', poly.astype(BF), short, preferred_element_type...]
    pallas_call x0 -> x1, Pallas kernels: none -> 41.6 us  [finish(): pl.pallas_call(functools.partial(finish_kernel, shards, sides, 0.2 * math...]
    psum x1 -> x0, blocking collectives: 38.3 us -> none  [fast_body(): lax.psum((jnp.sum(weights_value * losses), jnp.sum(weights_value), square...]
    unnamed x291 -> x301, local copies, waits for them, and re-layouts: 14.5 us -> 23.8 us
where the time goes in v3:
time: 632 us; the launch traced here: 625 us
  Pallas kernels  343 us (54%)
  matrix products  110 us (17%)
  local copies, waits for them, and re-layouts  104 us (16%)
  other arithmetic  58.5 us (9%)
  between operations  9.32 us (1%)
    pallas_call x1, Pallas kernels, scatter(): pl.pallas_call(functools.partial(scatter_kernel, depth, layers, sub, lags...  169 us
    pallas_call x1, Pallas kernels, gather(): pl.pallas_call(functools.partial(gather_kernel, depth, halves), out_shape...  132 us
    pallas_call x1, Pallas kernels, finish(): pl.pallas_call(functools.partial(finish_kernel, shards, sides, 0.2 * math...  41.6 us
    dot_general x10, matrix products, matmul_nt(): lax.dot_general(left, right, (((1,), (1,)), ((), ())), preferred_element_...  31 us
    dot_general x9, matrix products, matmul(): return jnp.dot(left, right, preferred_element_type=jnp.float32)  30.7 us
    dot_general x9, matrix products, matmul_tn(): lax.dot_general(left, right, (((0,), (0,)), ((), ())), preferred_element_...  27.4 us
    unnamed x301, local copies, waits for them, and re-layouts  23.8 us
    slice x1, local copies, waits for them, and re-layouts, fast_body(): weights[layer_number]  21.1 us

profile of v3, /device:TPU:0, one launch (start us, length us, event | category | flops | bytes accessed | tf_op | source)
XLA Modules:
  0.0 624.5 jit_solution(6951082057110254195)
XLA Ops:
  8.9 3.4 convert_element_type.268.mats
  12.3 131.8 %gather_weights.1 = (bf16[16,48,1664]{2,1,0:T(8,128)(2,1)}, bf16[2,16,576,768]{3,2,1,0:T(8,128)(2,1)}) custom-call(bf16[48,1664]{1,0:T(8,128)(2,1)} %pad.4.rows, bf16[2,576,768]{2,1,0:T(8,128)(2,1)} %convert_element_type.268.mats), custom_call_target="tpu_custom_call" | custom-call | tf_op jit(solution)/shard_map/gather_weights/pallas_call | solution.py:300
  150.4 5.3 fusion.146
  155.7 21.1 %fusion.145 = (bf16[1,16,576,768]{3,2,1,0:T(8,128)(2,1)}, bf16[1,16,576,768]{3,2,1,0:T(8,128)(2,1)}) fusion(bf16[2,16,576,768]{3,2,1,0:T(8,128)(2,1)} %get-tuple-element.23), kind=kLoop, calls=%fused_computation.276 | loop fusion | bytes 56623104 | tf_op jit(solution)/shard_map/slice | solution.py:1076
  182.5 1.9 fusion.73
  184.4 2.8 copy-done.13
  191.9 3.2 fusion.142
  196.6 2.5 fusion.35
  199.1 2.6 copy.95
  206.8 2.8 fusion.141
  210.8 4.1 fusion.22
  215.0 5.7 fusion.74
  223.2 1.9 multiply_reduce_fusion.20
  238.6 1.9 subtract_multiply_fusion.5
  245.5 3.2 fusion.136
  251.4 1.9 divide_reduce_fusion
  258.4 7.1 %fusion.159 = (bf16[3072]{0:T(1024)(128)(2,1)}, bf16[256,3072]{1,0:T(8,128)(2,1)}) fusion(f32[256,3072]{1,0:T(8,128)} %copy-done.146, bf16[9216,768]{1,0:T(8,128)(2,1)} %bitcast.262, f32[768]{0:T(1024)} %divide_reduce_fusion, f32[256]{0:T(256)} %bitcast.311), kind=kOutput, calls=%fused_computation.290 | convolution fusion | flops 1217000448 | bytes 9448448 | tf_op jit(solution)/shard_map/dot_general | solution.py:44
  266.8 5.1 fusion.158
  272.5 2.3 copy.99
  277.7 2.9 convert_reduce_fusion.3
  281.5 2.5 convolution_convert_fusion.10
  284.0 1.9 copy.100
  288.6 2.7 fusion.53
  292.9 4.0 convolution_convert_fusion.refs_7_
  297.0 3.9 convolution_convert_fusion.1.refs_6_
  304.5 2.6 fusion.157
  311.0 2.3 copy.104
  315.9 2.0 convert_reduce_fusion.2
  318.6 3.0 convolution_convert_fusion.2.refs_4_
  321.6 6.1 fusion.156
  329.0 5.1 fusion.155
  334.7 2.3 copy.105
  339.4 2.6 convert_reduce_fusion.1
  342.9 2.5 convolution_convert_fusion.9
  345.4 1.9 copy.106
  352.1 4.3 convolution_convert_fusion.3.refs_3_
  356.5 3.8 convolution_convert_fusion.4.refs_2_
  364.3 2.6 fusion.154
  371.0 2.3 copy.110
  373.6 2.0 multiply_reduce_fusion.5
  375.6 2.2 fusion.101
  378.6 2.5 fusion.88
  381.2 3.0 concatenate.37
  387.2 4.9 concatenate.39.refs_8_
  392.0 3.8 convolution_convert_fusion.5.refs_0_
  395.8 169.3 %scatter_gradients.1 = (bf16[2,576,768]{2,1,0:T(8,128)(2,1)}, bf16[48,1664]{1,0:T(8,128)(2,1)}) custom-call(bf16[2304,768]{1,0:T(8,128)(2,1)} %convolution_convert_fusion.5.refs_0_, bf16[768,768]{1,0:T(8,128)(2,1)} %convolution_convert_fusion.8.refs_1_, bf16[3072,768]{1,0:T(8,128)(2,1)} %convolution_convert_fusion.4.refs_2_, ...), custom_call_target="tpu_custom_call" | custom-call | tf_op jit(solution)/shard_map/scatter_gradients/pallas_call | solution.py:511
  565.1 41.6 %clip_and_orthogonalize.1 = (f32[8,128]{1,0:T(8,128)}, f32[2,576,768]{2,1,0:T(8,128)}, f32[2,576,768]{2,1,0:T(8,128)}, f32[2,576,768]{2,1,0:T(8,128)}, f32[2,576,768]{2,1,0:T(8,128)}) custom-call(f32[8,128]{1,0:T(8,128)} %select_select_fusion.stats, bf16[2,576,768]{2,1,0:T(8,128)(2,1)} %get-tuple-element.24.grad, ...), custom_call_target="tpu_custom_call" | custom-call | tf_op jit(solution)/shard_map/clip_and_orthogonalize/pallas_call | solution.py:731
  609.6 2.1 add_multiply_fusion
  (420 shorter events, 111.9 us)
Async XLA Ops:
  0.6 147.1 %copy-start = (bf16[1,256,768]{2,1,0:T(8,128)(2,1)S(1)}, bf16[1,256,768]{2,1,0:T(8,128)(2,1)}, u32[]{:S(2)}) copy-start(bf16[1,256,768]{2,1,0:T(8,128)(2,1)} %param.14) | copy-start | bytes 1179652
  4.5 175.5 %copy-start.142 = (pred[256]{0:T(512)(128)(4,1)}, pred[256]{0:T(512)(128)(4,1)S(1)}, u32[]{:S(2)}) copy-start(pred[256]{0:T(512)(128)(4,1)S(1)} %broadcast_compare_fusion) | copy-start | bytes 772
  147.1 29.7 %copy-start.58 = (f32[768]{0:T(1024)}, f32[768]{0:T(1024)S(1)}, u32[]{:S(2)}) copy-start(f32[768]{0:T(1024)S(1)} %get-tuple-element.63) | copy-start | bytes 9220
  147.1 29.7 %copy-start.61 = (f32[768]{0:T(1024)}, f32[768]{0:T(1024)S(1)}, u32[]{:S(2)}) copy-start(f32[768]{0:T(1024)S(1)} %get-tuple-element.64) | copy-start | bytes 9220
  147.1 29.7 %copy-start.70 = (f32[768]{0:T(1024)}, f32[768]{0:T(1024)S(1)}, u32[]{:S(2)}) copy-start(f32[768]{0:T(1024)S(1)} %get-tuple-element.62) | copy-start | bytes 9220
  147.1 29.8 %copy-start.116 = (f32[768]{0:T(1024)}, f32[768]{0:T(1024)S(1)}, u32[]{:S(2)}) copy-start(f32[768]{0:T(1024)S(1)} %get-tuple-element.61) | copy-start | bytes 9220
  149.6 27.3 %copy-start.3 = (f32[768,256]{1,0:T(8,128)}, f32[768,256]{1,0:T(8,128)S(1)}, u32[]{:S(2)}) copy-start(f32[768,256]{1,0:T(8,128)S(1)} %get-tuple-element.112) | copy-start | bytes 2359300
  149.6 27.3 %copy-start.76 = (f32[256]{0:T(256)}, f32[256]{0:T(256)S(1)}, u32[]{:S(2)}) copy-start(f32[256]{0:T(256)S(1)} %broadcast_multiply_fusion.14) | copy-start | bytes 3076
  149.8 27.1 %copy-start.83 = (f32[256]{0:T(256)}, f32[256]{0:T(256)S(1)}, u32[]{:S(2)}) copy-start(f32[256]{0:T(256)S(1)} %add_rsqrt_fusion.5) | copy-start | bytes 3076
  150.1 26.8 %copy-start.89 = (f32[256]{0:T(256)}, f32[256]{0:T(256)S(1)}, u32[]{:S(2)}) copy-start(f32[256]{0:T(256)S(1)} %broadcast_multiply_fusion.13) | copy-start | bytes 3076
  150.4 26.5 %copy-start.100 = (f32[256]{0:T(256)}, f32[256]{0:T(256)S(1)}, u32[]{:S(2)}) copy-start(f32[256]{0:T(256)S(1)} %add_rsqrt_fusion.4) | copy-start | bytes 3076
  155.7 21.2 %copy-start.30 = (bf16[1,4,576,768]{3,2,1,0:T(8,128)(2,1)}, bf16[1,4,576,768]{3,2,1,0:T(8,128)(2,1)S(1)}, u32[]{:S(2)}) copy-start(bf16[1,4,576,768]{3,2,1,0:T(8,128)(2,1)S(1)} %get-tuple-element.95) | copy-start | bytes 10616836
  181.9 5.3 copy-start.13
  184.4 5.7 copy-start.67
  184.4 5.6 copy-start.112
  184.4 5.6 copy-start.122
  209.7 5.3 copy-start.9
  215.0 5.8 copy-start.146
  285.9 5.4 copy-start.25
  285.9 5.4 copy-start.47
  313.4 5.2 copy-start.8
  313.4 5.2 copy-start.21
  313.4 5.2 copy-start.74
  313.4 5.2 copy-start.95
  313.4 5.2 copy-start.106
  313.4 5.2 copy-start.118
  338.8 6.7 %copy-start.132 = (f32[256]{0:T(256)}, f32[256]{0:T(256)S(1)}, u32[]{:S(2)}) copy-start(f32[256]{0:T(256)S(1)} %broadcast_multiply_fusion.4) | copy-start | bytes 3076
  338.8 6.6 %copy-start.134 = (f32[256]{0:T(256)}, f32[256]{0:T(256)S(1)}, u32[]{:S(2)}) copy-start(f32[256]{0:T(256)S(1)} %broadcast_multiply_fusion.5) | copy-start | bytes 3076
  364.3 9.0 %copy-start.5 = (f32[768,256]{1,0:T(8,128)S(1)}, f32[768,256]{1,0:T(8,128)}, u32[]{:S(2)}) copy-start(f32[768,256]{1,0:T(8,128)} %copy-done.3) | copy-start | bytes 2359300
  364.3 9.0 %copy-start.60 = (f32[768]{0:T(1024)S(1)}, f32[768]{0:T(1024)}, u32[]{:S(2)}) copy-start(f32[768]{0:T(1024)} %copy-done.58) | copy-start | bytes 9220
  364.3 9.0 %copy-start.63 = (f32[768]{0:T(1024)S(1)}, f32[768]{0:T(1024)}, u32[]{:S(2)}) copy-start(f32[768]{0:T(1024)} %copy-done.61) | copy-start | bytes 9220
  366.9 11.5 %copy-start.14 = (f32[256,768]{0,1:T(8,128)S(1)}, f32[256,768]{0,1:T(8,128)}, u32[]{:S(2)}) copy-start(f32[256,768]{0,1:T(8,128)} %copy.99) | copy-start | bytes 2359300
  366.9 11.5 %copy-start.15 = (f32[256,768]{0,1:T(8,128)S(1)}, f32[256,768]{0,1:T(8,128)}, u32[]{:S(2)}) copy-start(f32[256,768]{0,1:T(8,128)} %copy.104) | copy-start | bytes 2359300
  366.9 11.5 %copy-start.16 = (f32[256,768]{0,1:T(8,128)S(1)}, f32[256,768]{0,1:T(8,128)}, u32[]{:S(2)}) copy-start(f32[256,768]{0,1:T(8,128)} %copy.105) | copy-start | bytes 2359300
  366.9 11.5 %copy-start.66 = (f32[768]{0:T(1024)S(1)}, f32[768]{0:T(1024)}, u32[]{:S(2)}) copy-start(f32[768]{0:T(1024)} %get-tuple-element.47) | copy-start | bytes 9220
  366.9 11.5 %copy-start.69 = (f32[768]{0:T(1024)S(1)}, f32[768]{0:T(1024)}, u32[]{:S(2)}) copy-start(f32[768]{0:T(1024)} %get-tuple-element.57) | copy-start | bytes 9220
  373.3 5.1 copy-start.17
  373.3 5.1 copy-start.40
  373.3 5.1 copy-start.43
  373.3 5.1 copy-start.51
  386.4 5.6 copy-start.19
  386.4 5.6 copy-start.72
  386.4 5.6 copy-start.79
  565.1 43.1 %copy-start.48 = (bf16[48,1664]{1,0:T(8,128)(2,1)S(1)}, bf16[48,1664]{1,0:T(8,128)(2,1)}, u32[]{:S(2)}) copy-start(bf16[48,1664]{1,0:T(8,128)(2,1)} %get-tuple-element.25.row_grad) | copy-start | bytes 479236
  565.1 44.5 %copy-start.49 = (f32[1564,48]{0,1:T(8,128)S(1)}, f32[1564,48]{0,1:T(8,128)}, u32[]{:S(2)}) copy-start(f32[1564,48]{0,1:T(8,128)} %param.23) | copy-start | bytes 900868
  565.1 44.5 %copy-start.53 = (f32[1564,48]{0,1:T(8,128)S(1)}, f32[1564,48]{0,1:T(8,128)}, u32[]{:S(2)}) copy-start(f32[1564,48]{0,1:T(8,128)} %param.24) | copy-start | bytes 900868
  565.1 44.5 %copy-start.54 = (f32[1564,48]{0,1:T(8,128)S(1)}, f32[1564,48]{0,1:T(8,128)}, u32[]{:S(2)}) copy-start(f32[1564,48]{0,1:T(8,128)} %param.26) | copy-start | bytes 900868
  565.1 44.5 %copy-start.55 = (f32[1564,48]{0,1:T(8,128)S(1)}, f32[1564,48]{0,1:T(8,128)}, u32[]{:S(2)}) copy-start(f32[1564,48]{0,1:T(8,128)} %param.27) | copy-start | bytes 900868
  (100 other events, 349.2 us)

commit v4 on v3

--- a/solution.py
+++ b/solution.py
@@ -1,5 +1,6 @@
 import functools
 import math
+from typing import NamedTuple
 
 import jax
 import jax.numpy as jnp
@@ -323,7 +324,13 @@
         target[here, :] = (target[here, :].astype(F32) + source[there, :].astype(F32)).astype(BF)
 
 
-def scatter_group(links, dest, load, sizes, bufs, emit):
+class Group(NamedTuple):
+    begin: object
+    stages: list
+    core_slot: list
+
+
+def scatter_group(links, dest, load, sizes, bufs, emit, used=None):
     depth, z, y, c, x = links.depth, links.z, links.y, links.c, links.x
     n, p, q, step = sizes
     mine, core_in, x_in, y_in, z_in, z_last, final = bufs
@@ -346,6 +353,8 @@
             links.send(x_slot[i], mine.at[side, rows_at(peer_p, p)], x_in.at[side], links.x_peer)
             if i == 0:
                 links.send(q_slot, mine.at[side, pl.ds(p, q)], y_in.at[pl.ds(0, q)], links.y_peer)
+        if used is not None:
+            used()
 
     def stage_x():
         for i, side in sides:
@@ -406,124 +415,543 @@
             emit(mine.at[y])
 
     hops = [functools.partial(stage_z, hop) for hop in range(depth)]
-    return begin, [stage_core, stage_x, stage_y] + hops + [stage_last]
-
-
-def scatter_kernel(depth, layers, sub, lags, *refs):
-    grads, row_grad = refs[: 4 * layers], refs[4 * layers]
-    out, row_out = refs[4 * layers + 1 : 4 * layers + 3]
-    big, small = refs[4 * layers + 3 : 4 * layers + 10], refs[4 * layers + 10 : 4 * layers + 17]
-    send_sem, recv_sem, local_sem = refs[4 * layers + 17 :]
+    return Group(begin, [stage_core, stage_x, stage_y] + hops + [stage_last], core_slot)
+
+def norm_back(value, gain, upstream):
+    center = value - jnp.mean(value, -1, keepdims=True)
+    scale = lax.rsqrt(jnp.mean(center * center, -1, keepdims=True) + norm_epsilon)
+    normal = center * scale
+    scaled = upstream * gain
+    inner = scale * (
+        scaled
+        - jnp.mean(scaled, -1, keepdims=True)
+        - normal * jnp.mean(scaled * normal, -1, keepdims=True)
+    )
+    return (
+        inner,
+        jnp.sum(upstream * normal, 0, keepdims=True),
+        jnp.sum(upstream, 0, keepdims=True),
+    )
+
+
+VMEM_LIMIT = 62 * 1024 * 1024
+SUB = 3
+IN_FLIGHT = 2 * SUB
+LAGS = (1, 3, 5, 7, 9, 11, 13, 15)
+
+
+def backward_kernel(
+    depth,
+    sides,
+    layers,
+    weights,
+    resid,
+    normed,
+    project,
+    log_total,
+    context,
+    mixed,
+    normed_two,
+    embedded,
+    patches,
+    vectors,
+    keep,
+    keep_column,
+    pooled_row,
+    z_column,
+    feature_row,
+    vector_start,
+    stats,
+    out,
+    row_out,
+    totals,
+    blocks_v,
+    core_in,
+    x_in,
+    y_in,
+    z_in,
+    z_last,
+    final,
+    rows_v,
+    row_mine,
+    row_core,
+    row_x,
+    row_y,
+    row_z,
+    row_z_last,
+    row_final,
+    resid_v,
+    normed_v,
+    project_v,
+    log_v,
+    context_v,
+    mixed_v,
+    two_v,
+    weight_v,
+    patch_v,
+    hidden_v,
+    pre_v,
+    up_v,
+    short_v,
+    total_v,
+    context_grad_v,
+    vector_v,
+    note,
+    inbox,
+    send_sem,
+    recv_sem,
+    local_sem,
+    weight_sem,
+    load_sem,
+    mail_send,
+    mail_recv,
+    free_sem,
+):
     links = Links(depth, send_sem, recv_sem)
-    links.greet()
-    y, c = links.y, links.c
+    y, c, z = links.y, links.c, links.z
+    me = links.me * sides + links.x
+    everyone = PLANE * depth * sides
+    width = up_v.shape[1]
     count = out.shape[1]
-    n = count // sub
+    n = count // SUB
     p = n // 4 // 16 * 16
-    groups = []
-
-    def block_of(layer, shard, part):
-        row = shard * count + part * n
-        for matrix in grads[4 * layer : 4 * layer + 4]:
-            if row < matrix.shape[0]:
-                return matrix.at[pl.ds(row, n)]
-            row -= matrix.shape[0]
-
-    def add_group(dest, source, sizes, bufs, emit):
-        number = len(groups)
-
-        def load(i, side, mine, core_in, slot):
-            sem = local_sem.at[2 * number + i]
-            if core_in is None:
-                pltpu.make_async_copy(source(0, 0), mine, sem).wait()
-                return
-            for y_now in (0, 1):
-                for core in (0, 1):
-
-                    @pl.when(jnp.logical_and(side == y_now, c == core))
-                    def _():
-                        pltpu.make_async_copy(source(y_now, core), mine, sem).start()
-                        links.copy(slot, source(y_now, 1 - core), core_in, links.c_peer).start()
-
-            links.sent.append((slot, None, links.copy(slot, source(0, 0), core_in, links.c_peer)))
-
-        groups.append(scatter_group(links, dest, load, sizes, bufs, emit))
-
-    def write(target, sem):
-        def emit(result):
-            copy = pltpu.make_async_copy(result, target, sem)
-            copy.start()
-            copy.wait()
-
-        return emit
-
-    end_sem = local_sem.at[local_sem.shape[0] - 1]
+    per_layer = depth * SUB
+    own = 2 * layers * per_layer
+    piece = 2 * n
+
+    saved = (
+        (normed_two, two_v),
+        (mixed, mixed_v),
+        (context, context_v),
+        (resid, resid_v),
+        (normed, normed_v),
+        (project, project_v),
+        (log_total, log_v),
+    )
+
+    def load(layer, which):
+        source, target = saved[which]
+        return pltpu.make_async_copy(source.at[layer], target, load_sem.at[which])
+
+    chunks = []
     for layer in reversed(range(layers)):
-        for part in range(sub):
-            for dest in (3, 0, 2, 1) if depth == 4 else reversed(range(depth)):
-                number, spot = len(groups), layer * sub + part
+        for turn in (3, 2, 1, 0):
+            chunks += [(layer, 8 + turn), (layer, 4 + turn)]
+        chunks += [(layer, 3), (layer, 0), (layer, 1), (layer, 2)]
+
+    def chunk_copy(number):
+        layer, index = chunks[number]
+        return pltpu.make_async_copy(
+            weights.at[layer, pl.ds(index * width, width)],
+            weight_v.at[number % 4],
+            weight_sem.at[number % 4],
+        )
+
+    def chunk(number):
+        chunk_copy(number).wait()
+        return weight_v[number % 4]
+
+    def refill(*numbers):
+        for number in numbers:
+            if number < len(chunks):
+                chunk_copy(number).start()
+
+    for which in range(len(saved)):
+        load(layers - 1, which).start()
+    refill(0, 1, 2, 3)
+    patch_load = pltpu.make_async_copy(patches, patch_v, load_sem.at[7])
+    patch_load.start()
+
+    def others(run):
+        for number in range(everyone):
+            pl.when(me != number)(functools.partial(run, number))
+
+    def place(number):
+        return (number // sides, number % sides)
+
+    barrier = pltpu.get_barrier_semaphore()
+    others(
+        lambda number: pl.semaphore_signal(
+            barrier, inc=1, device_id=place(number), device_id_type=MESH
+        )
+    )
+    note[...] = stats[...]
+    vector_v[...] = vector_start[...]
+    up_v[...] = keep_column[...] * pooled_row[...]
+    lane = lax.broadcasted_iota(jnp.int32, (8, 128), 1)
+    first = lax.broadcasted_iota(jnp.int32, (8, 128), 0) == 0
+
+    def add_squares(block):
+        value = block.astype(F32)
+        note[...] += jnp.where(first & (lane == 0), jnp.sum(value * value), 0.0)
+
+    groups, closers = [], []
+    starts = {}
+
+    def add_group(dest, send_out, take_in, sizes, bufs, emit, used=None):
+        def load_block(i, side, mine, target, slot):
+            if target is None:
+                take_in(i, side, mine)
+            else:
+                send_out(i, side, mine, target, slot)
+
+        groups.append(scatter_group(links, dest, load_block, sizes, bufs, emit, used))
+
+    for order, layer in enumerate(reversed(range(layers))):
+        for turn, dest in enumerate(reversed(range(depth))):
+            ring = own
+            for part in range(SUB):
+                number, spot = len(groups), layer * SUB + part
+                starts[(layer, dest, part)] = number
+                slot = number % IN_FLIGHT
+
+                def send_out(i, side, mine, target, sem_slot, ring=ring, part=part):
+                    source = blocks_v.at[ring + 2 * part + side]
+                    links.send(sem_slot, source, target, links.c_peer)
+
+                def write(source, layer=layer, part=part, spot=spot):
+                    target = out.at[layer, pl.ds(part * n, n)]
+                    return pltpu.make_async_copy(source, target, local_sem.at[spot])
+
+                def emit(result, write=write):
+                    add_squares(result[...])
+                    write(result).start()
+
+                closers.append((dest, write, blocks_v.at[2 * number]))
+
+                def used(number=number):
+                    if number < layers * per_layer - IN_FLIGHT:
+                        pl.semaphore_signal(
+                            free_sem, inc=1, device_id=links.c_peer, device_id_type=MESH
+                        )
+
                 add_group(
                     dest,
-                    lambda y_now, core, layer=layer, part=part, dest=dest: block_of(
-                        layer, links.at(dest, y_now, core), part
-                    ),
-                    (n, p, n - 2 * p, 48),
-                    [ref.at[number] for ref in big[:5]] + [ref.at[spot] for ref in big[5:]],
-                    write(out.at[layer, pl.ds(part * n, n)], end_sem),
+                    send_out,
+                    lambda i, side, mine: None,
+                    (n, p, n - 2 * p, n // 4),
+                    [blocks_v.at[pl.ds(2 * number, 2)], core_in.at[slot]]
+                    + [ref.at[number] for ref in (x_in, y_in, z_in)]
+                    + [z_last.at[spot], final.at[spot]],
+                    emit,
+                    used,
                 )
+    first_row_group = len(groups)
     rows = row_out.shape[0]
     for dest in reversed(range(depth)):
+        number = len(groups)
+
+        def row_copy(i, side, mine, dest=dest):
+            sem = local_sem.at[layers * SUB + 2 * dest + i]
+            return pltpu.make_async_copy(rows_v.at[links.at(dest, side, c)], mine, sem)
+
+        def row_send(i, side, mine, target, slot, dest=dest, row_copy=row_copy):
+            row_copy(i, side, mine).start()
+            source = rows_v.at[links.at(dest, side, 1 - c)]
+            links.send(slot, source, target, links.c_peer)
+
+        def row_emit(result, dest=dest):
+            add_squares(result[...])
+            row_out[...] = result[...]
+
         add_group(
             dest,
-            lambda y_now, core, dest=dest: row_grad.at[links.at(dest, y_now, core)],
+            row_send,
+            lambda i, side, mine, row_copy=row_copy: row_copy(i, side, mine).wait(),
             (rows, 16, rows - 32, 16),
-            [ref.at[dest] for ref in small[:5]] + list(small[5:]),
-            write(row_out, end_sem),
+            [ref.at[dest] for ref in (row_mine, row_core, row_x, row_y, row_z)]
+            + [row_z_last, row_final],
+            row_emit,
         )
-    for begin, _ in groups:
-        begin()
-    for turn in range(len(groups) + max(lags)):
-        for place, lag in enumerate(lags):
+
+    begun = []
+
+    def release(layer, dest):
+        for part in range(SUB):
+            number = starts[(layer, dest, part)]
+            if number >= IN_FLIGHT:
+                pl.semaphore_wait(free_sem, 1)
+            groups[number].begin()
+            begun.append(number)
+
+    def recycle(layer, dest):
+        for part in range(SUB):
+            number = starts[(layer, dest, part)]
+            if number >= SUB:
+                for slot in groups[number - SUB].core_slot:
+                    links.finish(slot)
+
+    last_turn = [0]
+
+    def advance():
+        turn = last_turn[0]
+        for stage, lag in enumerate(LAGS):
             if 0 <= turn - lag < len(groups):
-                groups[turn - lag][1][place]()
+                groups[turn - lag].stages[stage]()
+        last_turn[0] += 1
+
+    def grad_pieces(layer, dest, left, column, amount, right, begin):
+        number = starts[(layer, dest, 0)]
+        ring = own
+
+        @pl.loop(0, amount)
+        def _(turn):
+            columns = pl.ds(pl.multiple_of(column + turn * piece, 128), piece)
+            result = matmul_tn(left[:, columns], right[...])
+            for half in range(2):
+                block = 2 * (begin + turn) + half
+                shard = block // SUB
+                part = lax.rem(block, SUB)
+                side, core = shard // 2, lax.rem(shard, 2)
+                index = jnp.where(
+                    core == c, 2 * (number + part) + side, ring + 2 * part + side
+                )
+                blocks_v[index] = result[half * n : (half + 1) * n].astype(BF)
+
+    half_lane = lax.broadcasted_iota(jnp.int32, (1, 128), 1) < HDIM
+    scale = HDIM ** (-0.5)
+
+    def attention_pair(pair):
+        def lanes(base):
+            return pl.ds(pl.multiple_of(base + pair * 128, 128), 128)
+
+        query, key = project_v[:, lanes(0)], project_v[:, lanes(width)]
+        value, grad = project_v[:, lanes(2 * width)], context_grad_v[:, lanes(0)]
+        totals_now = log_v[...]
+        column = lax.broadcasted_iota(jnp.int32, totals_now.shape, 1)
+        query_grad = key_grad = value_grad = 0.0
+        zero = jnp.zeros_like(query)
+        for head in range(2):
+            here = half_lane if head == 0 else jnp.logical_not(half_lane)
+            query_h, key_h = jnp.where(here, query, zero), jnp.where(here, key, zero)
+            grad_h = jnp.where(here, grad, zero)
+            total = jnp.sum(
+                jnp.where(column == 2 * pair + head, totals_now, 0.0), -1, keepdims=True
+            )
+            scores = jnp.where(keep[...] > 0, matmul_nt(query_h, key) * scale, -1000000000.0)
+            probs = jnp.exp(scores - total)
+            prob_grad = matmul_nt(grad_h, value)
+            value_grad += matmul_tn(probs.astype(BF), grad_h)
+            score_grad = (
+                probs * (prob_grad - jnp.sum(prob_grad * probs, -1, keepdims=True))
+            ).astype(BF)
+            query_grad += matmul(score_grad, key_h)
+            key_grad += matmul_tn(score_grad, query_h)
+        pre_v[:, lanes(0)] = (query_grad * scale).astype(BF)
+        pre_v[:, lanes(width)] = (key_grad * scale).astype(BF)
+        pre_v[:, lanes(2 * width)] = value_grad.astype(BF)
+
+    def layer_steps(order, layer):
+        base = 4 + 12 * layer
+        chunk0 = 12 * order
+
+        def vector(index):
+            return vectors[pl.ds(base + index, 1), :]
+
+        def put(index, value):
+            vector_v[pl.ds(base + index, 1), :] = value
+
+        def column_sum(value):
+            return jnp.sum(value.astype(F32), 0, keepdims=True)
+
+        load(layer, 0).wait()
+        short_v[...] = up_v[...].astype(BF)
+        put(7, column_sum(short_v[...]))
+        total_v[...] = jnp.zeros_like(total_v)
+        recycle(layer, 3)
+        for turn, part in enumerate((3, 2, 1, 0)):
+            number = chunk0 + 2 * turn
+            down, up = chunk(number), chunk(number + 1)
+            pre = matmul_nt(two_v[...], up) + vector(8 + part)
+            gate = jax.nn.sigmoid(1.702 * pre)
+            hidden_v[...] = (pre * gate).astype(BF)
+            slope = gate + 1.702 * pre * gate * (1.0 - gate)
+            pre_grad = (matmul_nt(short_v[...], down) * slope).astype(BF)
+            pre_v[:, pl.ds(part * width, width)] = pre_grad
+            put(8 + part, column_sum(pre_grad))
+            total_v[...] += matmul(pre_grad, up)
+            refill(number + 4, number + 5)
+            yield None
+            if part == 0:
+                recycle(layer, 2)
+            if part > 0:
+                grad_pieces(layer, 3, hidden_v, 0, 2, short_v, 2 * (part - 1))
+            else:
+                grad_pieces(layer, 2, hidden_v, 0, 2, short_v, 4)
+            if part == 1:
+                release(layer, 3)
+                yield 3
+            else:
+                yield None
+        grad_pieces(layer, 2, pre_v, 2 * width, 2, two_v, 0)
+        yield None
+        grad_pieces(layer, 2, pre_v, 3 * width, 2, two_v, 2)
+        release(layer, 2)
+        yield 2
+        load(layer, 1).wait()
+        inner, gain, shift = norm_back(mixed_v[...], vector(5), total_v[...])
+        put(5, gain)
+        put(6, shift)
+        up_v[...] += inner
+        short_v[...] = up_v[...].astype(BF)
+        put(4, column_sum(short_v[...]))
+        yield None
+        load(layer, 2).wait()
+        recycle(layer, 1)
+        grad_pieces(layer, 1, short_v, 0, 2, context_v, 0)
+        context_grad_v[...] = matmul(short_v[...], chunk(chunk0 + 8)).astype(BF)
+        refill(chunk0 + 12)
+        yield None
+        grad_pieces(layer, 1, pre_v, 0, 2, two_v, 2)
+        yield None
+        grad_pieces(layer, 1, pre_v, width, 2, two_v, 4)
+        release(layer, 1)
+        if layer > 0:
+            for which in range(3):
+                load(layer - 1, which).start()
+        else:
+            embed_load.start()
+        yield 1
+        load(layer, 5).wait()
+        load(layer, 6).wait()
+        for third in range(3):
+
+            @pl.loop(0, 2)
+            def _(turn, third=third):
+                attention_pair(2 * third + turn)
+
+            yield None
+        load(layer, 4).wait()
+        recycle(layer, 0)
+        put(2, column_sum(pre_v[:, pl.ds(0, width)]))
+        put(3, column_sum(pre_v[:, pl.ds(2 * width, width)]))
+        for third in range(3):
+            grad_pieces(layer, 0, pre_v, third * width, 2, normed_v, 2 * third)
+            if third < 2:
+                yield None
+        release(layer, 0)
+        yield 0
+        load(layer, 3).wait()
+        back = matmul(pre_v[:, pl.ds(0, width)], chunk(chunk0 + 9))
+        back += matmul(pre_v[:, pl.ds(width, width)], chunk(chunk0 + 10))
+        back += matmul(pre_v[:, pl.ds(2 * width, width)], chunk(chunk0 + 11))
+        refill(chunk0 + 13, chunk0 + 14, chunk0 + 15)
+        inner, gain, shift = norm_back(resid_v[...], vector(0), back)
+        put(0, gain)
+        put(1, shift)
+        up_v[...] += inner
+        if layer > 0:
+            for which in range(3, len(saved)):
+                load(layer - 1, which).start()
+        yield None
+
+    embed_load = pltpu.make_async_copy(embedded, mixed_v, load_sem.at[8])
+    pl.semaphore_wait(barrier, everyone - 1)
+    pending = 0
+    for order, layer in enumerate(reversed(range(layers))):
+        for ready in layer_steps(order, layer):
+            if ready is not None:
+                pending += SUB
+            if pending > 0:
+                advance()
+                pending -= 1
+    embed_load.wait()
+    inner, gain, shift = norm_back(mixed_v[...], vectors[pl.ds(0, 1), :], up_v[...])
+    vector_v[pl.ds(0, 1), :] = gain
+    vector_v[pl.ds(1, 1), :] = shift
+    short_v[...] = inner.astype(BF)
+    total_v[...] = inner
+    patch_load.wait()
+    pixels, embeds, seq = patch_v.shape[1], feature_row.shape[1], inner.shape[0]
+    for turn in range(width // piece):
+        columns = pl.ds(turn * piece, piece)
+        patch_grad = matmul_tn(short_v[:, columns], patch_v[...])
+        position = total_v[:, columns].T
+        vector_grad = vector_v[:, columns].T
+        for part in range(piece // rows):
+            shard, inside = turn * (piece // rows) + part, slice(part * rows, (part + 1) * rows)
+            rows_v[shard, :, pl.ds(0, pixels)] = patch_grad[inside].astype(BF)
+            proj = z_column[pl.ds(shard * rows, rows), :] * feature_row[...]
+            rows_v[shard, :, pl.ds(pixels, embeds)] = proj.astype(BF)
+            rows_v[shard, :, pl.ds(pixels + embeds, seq)] = position[inside].astype(BF)
+            rows_v[shard, :, pl.ds(pixels + embeds + seq, 128)] = vector_grad[inside].astype(BF)
+    for number in range(first_row_group, len(groups)):
+        groups[number].begin()
+    while last_turn[0] < len(groups) + max(LAGS):
+        advance()
+
+    def mail(number, slot):
+        return pltpu.make_async_remote_copy(
+            src_ref=note,
+            dst_ref=inbox.at[slot],
+            send_sem=mail_send.at[number],
+            recv_sem=mail_recv.at[slot],
+            device_id=place(number),
+            device_id_type=MESH,
+        )
+
+    others(lambda number: mail(number, me).start())
+    inbox[pl.ds(me, 1)] = note[...][None]
     links.finish()
-
-
-def scatter(depth, grads, row_grad):
-    layers = len(grads)
+    for dest, write, source in closers:
+        pl.when(z == dest)(lambda write=write, source=source: write(source).wait())
+    others(lambda number: mail(number, number).wait_recv())
+    summed = jnp.sum(inbox[...], 0)
+    others(lambda number: mail(number, me).wait_send())
+
+    def pick(index):
+        return jnp.sum(jnp.where(first & (lane == index), summed, 0.0))
+
+    loss_sum, weight_sum = pick(1), pick(2)
+    norm = jnp.sqrt(jnp.full((8, 128), pick(0) / sides)) / weight_sum
+    clip = jnp.minimum(1.0, clip_bound / (norm + 1e-06)) / weight_sum
+    totals[...] = jnp.where(
+        lane == 0,
+        loss_sum,
+        jnp.where(lane == 1, weight_sum, jnp.where(lane == 2, norm, clip)),
+    )
+
+
+def backward(
+    depth, sides, weights, saved, embedded, patches, vectors, keep, keep_column, head, start, stats
+):
+    layers, rows_all, width = weights.shape
+    seq, pixels = patches.shape
     shards = PLANE * depth
-    width = grads[0][0].shape[1]
-    count = sum(part.shape[0] for part in grads[0]) // shards
-    sub = 3
-    n = count // sub
+    count, rows = rows_all // shards, width // shards
+    lanes = -(-(pixels + EMB + SEQ + 4 + 12 * layers) // 128) * 128
+    n = count // SUB
     p = n // 4 // 16 * 16
     m = n - p
-    blocks = layers * depth * sub
-    rows, lanes = row_grad.shape[1:]
+    per_layer = depth * SUB
+    blocks = layers * per_layer
     row_m = rows - 16
-    lags = [0, 3, 6] + [9 + 3 * hop for hop in range(depth)] + [9 + 3 * depth]
-
-    def room(*shape):
-        return pltpu.VMEM(shape, BF)
+    everyone = shards * sides
+
+    def room(*shape, dtype=BF):
+        return pltpu.VMEM(shape, dtype)
 
     any_space = pl.BlockSpec(memory_space=pl.ANY)
+    vmem = pl.BlockSpec(memory_space=pltpu.VMEM)
     slots = (blocks + depth) * 9
     return pl.pallas_call(
-        functools.partial(scatter_kernel, depth, layers, sub, lags),
+        functools.partial(backward_kernel, depth, sides, layers),
         out_shape=(
             jax.ShapeDtypeStruct((layers, count, width), BF),
             jax.ShapeDtypeStruct((rows, lanes), BF),
+            jax.ShapeDtypeStruct((8, 128), F32),
         ),
-        in_specs=[any_space] * (4 * layers + 1),
-        out_specs=[any_space] * 2,
+        in_specs=[any_space] * (1 + len(saved) + 2) + [vmem] * 8,
+        out_specs=[any_space, vmem, vmem],
         scratch_shapes=[
-            room(blocks, 2, n, width),
-            room(blocks, 2, n, width),
+            room(2 * blocks + 2 * SUB, n, width),
+            room(IN_FLIGHT, 2, n, width),
             room(blocks, 2, p, width),
             room(blocks, m, width),
             room(blocks, m, width),
-            room(layers * sub, m, width),
-            room(layers * sub, m, width),
+            room(layers * SUB, m, width),
+            room(layers * SUB, m, width),
+            room(shards, rows, lanes),
             room(depth, 2, rows, lanes),
             room(depth, 2, rows, lanes),
             room(depth, 2, 16, lanes),
@@ -531,35 +959,53 @@
             room(depth, row_m, lanes),
             room(row_m, lanes),
             room(row_m, lanes),
+            room(seq, width, dtype=F32),
+            room(seq, width),
+            room(seq, 3 * width),
+            room(seq, 128, dtype=F32),
+            room(seq, width),
+            room(seq, width, dtype=F32),
+            room(seq, width),
+            room(4, width, width),
+            room(seq, pixels),
+            room(seq, width),
+            room(seq, 4 * width),
+            room(seq, width, dtype=F32),
+            room(seq, width),
+            room(seq, width, dtype=F32),
+            room(seq, width),
+            room(128, width, dtype=F32),
+            room(8, 128, dtype=F32),
+            room(everyone, 8, 128, dtype=F32),
             pltpu.SemaphoreType.DMA((slots,)),
             pltpu.SemaphoreType.DMA((slots,)),
-            pltpu.SemaphoreType.DMA((2 * (blocks + depth) + 1,)),
+            pltpu.SemaphoreType.DMA((layers * SUB + 2 * depth,)),
+            pltpu.SemaphoreType.DMA((4,)),
+            pltpu.SemaphoreType.DMA((9,)),
+            pltpu.SemaphoreType.DMA((everyone,)),
+            pltpu.SemaphoreType.DMA((everyone,)),
+            pltpu.SemaphoreType.REGULAR,
         ],
-        name="scatter_gradients",
+        name="backward_and_sum",
         compiler_params=pltpu.CompilerParams(
-            collective_id=2, has_side_effects=True, vmem_limit_bytes=60 * 1024 * 1024
+            collective_id=2, has_side_effects=True, vmem_limit_bytes=VMEM_LIMIT
         ),
-    )(*[part for layer in grads for part in layer], row_grad)
+    )(weights, *saved, embedded, patches, vectors, keep, keep_column, *head, start, stats)
 
 
 def finish_kernel(
-    shards,
-    sides,
     hyper,
-    stats,
+    totals,
     grad,
-    row_grad,
     momentum,
     mats,
     zero,
     ema,
-    totals,
     new_momentum,
     new_mats,
     new_ema,
     new_mixed,
     grad_v,
-    row_v,
     m_v,
     mats_v,
     zero_v,
@@ -567,96 +1013,19 @@
     x_v,
     short_v,
     low_v,
-    note,
-    inbox,
-    send_sem,
-    recv_sem,
     in_sem,
     out_sem,
 ):
-    me = lax.axis_index("fsdp") * sides + lax.axis_index("ns")
-    everyone = shards * sides
     layers, count, width = grad.shape
-    pairs = [(grad, grad_v), (row_grad, row_v), (momentum, m_v)]
+    pairs = [(grad, grad_v), (momentum, m_v)]
     pairs += [(mats, mats_v), (zero, zero_v), (ema, ema_v)]
     loads = [pltpu.make_async_copy(a, b, in_sem.at[i]) for i, (a, b) in enumerate(pairs)]
     for load in loads:
         load.start()
-    barrier = pltpu.get_barrier_semaphore()
-
-    def others(run):
-        for number in range(everyone):
-            pl.when(me != number)(functools.partial(run, number))
-
-    def place(number):
-        return (number // sides, number % sides)
-
-    others(
-        lambda number: pl.semaphore_signal(
-            barrier, inc=1, device_id=place(number), device_id_type=MESH
-        )
-    )
+    part = count // 3
+    factor = totals[pl.ds(0, 1), pl.ds(3, 1)]
     loads[0].wait()
     loads[1].wait()
-    part = count // 3
-
-    def blocks(run):
-        @pl.loop(0, layers * 3)
-        def _(turn):
-            run(turn // 3, rows_at(lax.rem(turn, 3) * part, part))
-
-    note[...] = stats[...]
-    lane = lax.broadcasted_iota(jnp.int32, (8, 128), 1)
-    sub = lax.broadcasted_iota(jnp.int32, (8, 128), 0)
-
-    def add_squares(block):
-        value = block.astype(F32)
-        total = jnp.sum(value * value)
-        note[...] += jnp.where((lane == 0) & (sub == 0), total, 0.0)
-
-    blocks(lambda layer, rows: add_squares(grad_v[layer, rows, :]))
-    add_squares(row_v[...])
-    pl.semaphore_wait(barrier, everyone - 1)
-
-    def mail(number):
-        return pltpu.make_async_remote_copy(
-            src_ref=note,
-            dst_ref=inbox.at[me],
-            send_sem=send_sem.at[number],
-            recv_sem=recv_sem.at[me],
-            device_id=place(number),
-            device_id_type=MESH,
-        )
-
-    def collect(number):
-        pltpu.make_async_remote_copy(
-            src_ref=note,
-            dst_ref=inbox.at[number],
-            send_sem=send_sem.at[number],
-            recv_sem=recv_sem.at[number],
-            device_id=place(number),
-            device_id_type=MESH,
-        ).wait_recv()
-
-    others(lambda number: mail(number).start())
-    inbox[pl.ds(me, 1)] = note[...][None]
-    others(collect)
-    summed = jnp.sum(inbox[...], 0)
-    others(lambda number: mail(number).wait_send())
-
-    def pick(index):
-        return jnp.sum(jnp.where((lane == index) & (sub == 0), summed, 0.0))
-
-    loss_sum, weight_sum = pick(1), pick(2)
-    norm = jnp.sqrt(jnp.full((8, 128), pick(0) / sides)) / weight_sum
-    clip = jnp.minimum(1.0, clip_bound / (norm + 1e-06)) / weight_sum
-    totals[...] = jnp.where(
-        lane == 0,
-        loss_sum,
-        jnp.where(lane == 1, weight_sum, jnp.where(lane == 2, norm, clip)),
-    )
-    factor = clip[:1, :1]
-    loads[2].wait()
     stores = []
     for layer in range(layers):
         total = jnp.zeros((1, 1), F32)
@@ -699,7 +1068,7 @@
                 x_v[layer, rows, :] = value
                 short_v[later, layer, rows, :] = value.astype(BF)
 
-    for load in loads[3:]:
+    for load in loads[2:]:
         load.wait()
     for layer in range(layers):
         for third in range(3):
@@ -722,20 +1091,18 @@
         store.wait()
 
 
-def finish(shards, sides, stats, grad, row_grad, momentum, mats, zero, ema):
+def finish(totals, grad, momentum, mats, zero, ema):
     layers, count, width = grad.shape
-    everyone = shards * sides
     full = jax.ShapeDtypeStruct(mats.shape, F32)
     any_space = pl.BlockSpec(memory_space=pl.ANY)
     vmem = pl.BlockSpec(memory_space=pltpu.VMEM)
     return pl.pallas_call(
-        functools.partial(finish_kernel, shards, sides, 0.2 * math.sqrt(width)),
-        out_shape=(jax.ShapeDtypeStruct((8, 128), F32), full, full, full, full),
-        in_specs=[vmem] + [any_space] * 6,
-        out_specs=[vmem] + [any_space] * 4,
+        functools.partial(finish_kernel, 0.2 * math.sqrt(width)),
+        out_shape=(full, full, full, full),
+        in_specs=[vmem] + [any_space] * 5,
+        out_specs=[any_space] * 4,
         scratch_shapes=[
             pltpu.VMEM(grad.shape, BF),
-            pltpu.VMEM(row_grad.shape, BF),
             pltpu.VMEM(mats.shape, F32),
             pltpu.VMEM(mats.shape, F32),
             pltpu.VMEM(mats.shape, F32),
@@ -743,18 +1110,12 @@
             pltpu.VMEM(mats.shape, F32),
             pltpu.VMEM((2,) + mats.shape, BF),
             pltpu.VMEM((layers, count, count), BF),
-            pltpu.VMEM((8, 128), F32),
-            pltpu.VMEM((everyone, 8, 128), F32),
-            pltpu.SemaphoreType.DMA((everyone,)),
-            pltpu.SemaphoreType.DMA((everyone,)),
-            pltpu.SemaphoreType.DMA((6,)),
+            pltpu.SemaphoreType.DMA((5,)),
             pltpu.SemaphoreType.DMA((layers * 10,)),
         ],
-        name="clip_and_orthogonalize",
-        compiler_params=pltpu.CompilerParams(
-            collective_id=3, has_side_effects=True, vmem_limit_bytes=56 * 1024 * 1024
-        ),
-    )(stats, grad, row_grad, momentum, mats, zero, ema)
+        name="orthogonalize",
+        compiler_params=pltpu.CompilerParams(vmem_limit_bytes=56 * 1024 * 1024),
+    )(totals, grad, momentum, mats, zero, ema)
 
 
 def gather_layer(shard):
@@ -1075,7 +1436,12 @@
         resid, saved_activation = layer_forward(
             resid, weights[layer_number], layer_vector_params[layer_number], valid_mask
         )
-        saved_activations.append(saved_activation)
+        before, normed, project, log_total, context, mixed, normed_two, _, _ = saved_activation
+        log_total = jnp.pad(log_total.reshape(HEADS, seq).T, ((0, 0), (0, 128 - HEADS)))
+        saved_activations.append(
+            (before, normed, project, log_total, context, mixed, normed_two)
+        )
+    saved = [jnp.stack(parts) for parts in zip(*saved_activations)]
     counts = jnp.sum(valid_mask, -1, keepdims=True)
     pooled = jnp.sum(resid.reshape(images, seq, width) * valid_mask[..., None], 1) / counts
     pooled_norm = norm_forward(pooled, head_vec[2], head_vec[3]).astype(BF)
@@ -1099,7 +1465,6 @@
     feat_grad = inv_length * unit_grad - feature * inv_length**3 * jnp.sum(
         unit_grad * feature, -1, keepdims=True
     )
-    grad_proj = jnp.dot(pooled_norm.astype(F32).T, feat_grad, precision=HIGHEST)
     pooled_grad, gain_post, shift_post = norm_backward(
         pooled,
         head_vec[2],
@@ -1107,47 +1472,28 @@
             feat_grad, proj.astype(F32), (((1,), (1,)), ((), ())), precision=HIGHEST
         ),
     )
-    upstream = (valid_mask[..., None] * (pooled_grad / counts)[:, None, :]).reshape(
-        images * seq, width
-    )
-    grad_mats = [None] * layers
-    grad_vecs = [None] * layers
-    for layer_number in reversed(range(layers)):
-        upstream, grad_mats[layer_number], grad_vecs[layer_number] = layer_backward(
-            upstream,
-            weights[layer_number],
-            layer_vector_params[layer_number],
-            valid_mask,
-            saved_activations[layer_number],
-        )
-    embed_grad, gain_pre, shift_pre = norm_backward(embedded, head_vec[0], upstream)
-    position_grad = jnp.sum(embed_grad.reshape(images, seq, width), 0)
-    patch_grad = matmul_tn(embed_grad.astype(BF), flat_patches)
-    vector_grad = jnp.concatenate(
-        [jnp.stack([gain_pre, shift_pre, gain_post, shift_post])] + grad_vecs, 0
-    )
-    row_grad = jnp.concatenate(
-        [patch_grad, grad_proj, position_grad.T, vector_grad.T, jnp.zeros((width, lanes - rows))], 1
-    )
-    mat_total, row_total = scatter(
-        depth, grad_mats, row_grad.astype(BF).reshape(shards, share, lanes)
-    )
     lane = lax.broadcasted_iota(jnp.int32, (8, 128), 1)
     first = lax.broadcasted_iota(jnp.int32, (8, 128), 0) == 0
     stats = jnp.where(first & (lane == 1), jnp.sum(weights_value * losses), 0.0)
     stats = jnp.where(first & (lane == 2), jnp.sum(weights_value), stats)
-    totals, momentum, new_mats, ema_mats, mixed_mats = finish(
-        shards,
+    mat_total, row_total, totals = backward(
+        depth,
         lax.axis_size("ns"),
+        weights,
+        saved,
+        embedded,
+        flat_patches,
+        vectors,
+        valid_mask,
+        valid_mask.T,
+        (pooled_grad / counts, pooled_norm.astype(F32).T, feat_grad),
+        jnp.pad(jnp.stack([gain_post, shift_post]), ((2, 124), (0, 0))),
         stats,
-        mat_total,
-        row_total,
-        layer_momentum,
-        layer_mats,
-        layer_zero,
-        layer_ema,
     )
     loss_sum, weight_sum, grad_norm, clip = (totals[0, turn] for turn in range(4))
+    momentum, new_mats, ema_mats, mixed_mats = finish(
+        totals, mat_total, layer_momentum, layer_mats, layer_zero, layer_ema
+    )
     clipped = clip * row_total.astype(F32)[:, :rows].T
     return (loss_sum, weight_sum, grad_norm, new_mats, momentum, ema_mats, mixed_mats) + row_updates(
         clipped, layers, row_params, row_zero, row_ema, row_first, row_second
@@ -1156,8 +1502,8 @@
 
 def body(*args):
     count, share = args[5].shape[1], args[9].shape[1]
-    planes = lax.axis_size("fsdp") % PLANE == 0 and lax.axis_size("ns") == 2
-    if planes and count % 192 == 0 and share % 48 == 0:
+    planes = lax.axis_size("fsdp") == 4 * PLANE and lax.axis_size("ns") == 2
+    if planes and count % 192 == 0 and share % 48 == 0 and args[0].shape[0] == 1:
         return fast_body(*args)
     return plain_body(*args)
 

time: 632 us -> 480 us (0.76)
  matrix products: 110 us -> 34.9 us
  local copies, waits for them, and re-layouts: 104 us -> 39.2 us
  other arithmetic: 58.5 us -> 37.1 us
  Pallas kernels: 343 us -> 354 us
    dot_general x17 -> x0, matrix products: 35.4 us -> none  [the longest x9 27.4 us: matmul_tn(): lax.dot_general(left, right, (((0,), (0,)), ((), ())), preferred_element_...]
    dot_general x10 -> x6, matrix products: 31 us -> 9.35 us  [matmul_nt(): lax.dot_general(left, right, (((1,), (1,)), ((), ())), preferred_element_...]
    another operation x20 -> x2, local copies, waits for them, and re-layouts: 17.7 us -> 0.02 us  [the longest x1 0.02 us: fast_body(): saved = [jnp.stack(parts) for parts in zip(*saved_activations)]]
    unnamed x301 -> x126, local copies, waits for them, and re-layouts: 23.8 us -> 6.17 us
    dot_general x9 -> x3, matrix products: 30.7 us -> 14.7 us  [matmul(): return jnp.dot(left, right, preferred_element_type=jnp.float32)]
    reduce_sum x10 -> x2, other arithmetic: 17.7 us -> 2.5 us  [the longest x1 1.25 us: norm_backward(): jnp.mean(center * center, -1, keepdims=True) + norm_epsilon]
    pallas_call x2, Pallas kernels: 211 us -> 223 us  [the longest x1 187 us: backward(): pl.pallas_call(functools.partial(backward_kernel, depth, sides, layers),...]
    dot_general x4 -> x0, local copies, waits for them, and re-layouts: 9.23 us -> none  [matmul(): return jnp.dot(left, right, preferred_element_type=jnp.float32)]
where the time goes in v4:
time: 480 us; the launch traced here: 474 us
  Pallas kernels  354 us (74%)
  local copies, waits for them, and re-layouts  39.2 us (8%)
  other arithmetic  37.1 us (8%)
  matrix products  34.9 us (7%)
  between operations  8.71 us (2%)
    pallas_call x1, Pallas kernels, backward(): pl.pallas_call(functools.partial(backward_kernel, depth, sides, layers),...  187 us
    pallas_call x1, Pallas kernels, gather(): pl.pallas_call(functools.partial(gather_kernel, depth, halves), out_shape...  132 us
    pallas_call x1, Pallas kernels, finish(): pl.pallas_call(functools.partial(finish_kernel, 0.2 * math.sqrt(width)),...  35.6 us
    slice x1, local copies, waits for them, and re-layouts, fast_body(): weights[layer_number]  15.6 us
    dot_general x3, matrix products, matmul(): return jnp.dot(left, right, preferred_element_type=jnp.float32)  14.7 us
    another operation x8, other arithmetic, fast_body(): saved = [jnp.stack(parts) for parts in zip(*saved_activations)]  10.5 us

profile of v4, /device:TPU:0, one launch (start us, length us, event | category | flops | bytes accessed | tf_op | source)
XLA Modules:
  0.0 474.2 jit_solution(1919590436873410218)
XLA Ops:
  0.7 3.4 convert_element_type.139.mats
  4.8 131.8 %gather_weights.1 = (bf16[16,48,1664]{2,1,0:T(8,128)(2,1)}, bf16[2,16,576,768]{3,2,1,0:T(8,128)(2,1)}) custom-call(bf16[48,1664]{1,0:T(8,128)(2,1)} %pad.15.rows, bf16[2,576,768]{2,1,0:T(8,128)(2,1)} %convert_element_type.139.mats), custom_call_target="tpu_custom_call" | custom-call | tf_op jit(solution)/shard_map/gather_weights/pallas_call | solution.py:301
  136.6 1.0 slice.246
  137.8 1.9 fusion.130
  139.9 1.0 slice.247
  142.5 5.3 %fusion.127 = (bf16[1,4,576,768]{3,2,1,0:T(8,128)(2,1)}, bf16[1,4,576,768]{3,2,1,0:T(8,128)(2,1)S(1)}) fusion(bf16[2,16,576,768]{3,2,1,0:T(8,128)(2,1)} %get-tuple-element.22), kind=kLoop, calls=%fused_computation.187 | loop fusion | bytes 14155776 | tf_op jit(solution)/shard_map/slice | solution.py:1131
  147.8 1.3 fusion.14
  149.2 1.6 copy.79
  151.3 1.9 fusion.16
  153.2 0.7 fusion.18
  154.0 2.0 fusion.66
  156.0 15.6 %fusion.126 = (bf16[1,16,576,768]{3,2,1,0:T(8,128)(2,1)}, bf16[1,16,576,768]{3,2,1,0:T(8,128)(2,1)S(1)}) fusion(bf16[2,16,576,768]{3,2,1,0:T(8,128)(2,1)} %get-tuple-element.22), kind=kLoop, calls=%fused_computation.186 | loop fusion | bytes 56623104 | tf_op jit(solution)/shard_map/slice | solution.py:1437
  171.6 4.9 %copy-done.1 = bf16[1,16,576,768]{3,2,1,0:T(8,128)(2,1)} copy-done((bf16[1,16,576,768]{3,2,1,0:T(8,128)(2,1)}, bf16[1,16,576,768]{3,2,1,0:T(8,128)(2,1)S(1)}, u32[]{:S(2)}) %copy-start.1) | copy-done | bytes 14155800
  177.5 6.7 %fusion.132 = (f32[256]{0:T(256)S(1)}, f32[256,768]{1,0:T(8,128)S(1)}) fusion(f32[256,768]{1,0:T(8,128)S(1)} %get-tuple-element.80, f32[768]{0:T(1024)S(1)} %get-tuple-element.39, bf16[9216,768]{1,0:T(8,128)(2,1)} %bitcast.141, f32[3072]{0:T(1024)S(1)} %add.298, f32[768]{0:T(1024)S(1)} %get-tuple-element.40, f32[768]{0:T(1024)S(1)} %get-tuple-element.41, ...), kind=kOutput, calls=%fused_computation.192 | convolution fusion | flops 2422996736 | bytes 11824128 | tf_op jit(solution)/shard_map/dot_general | solution.py:41
  184.5 3.2 fusion.15
  187.7 1.6 copy.82
  189.3 1.9 fusion.17
  191.2 0.7 fusion.19
  192.0 2.0 fusion.65
  194.7 1.9 fusion.135
  196.9 6.7 %fusion.67 = f32[768]{0:T(1024)S(1)} fusion(f32[256,768]{1,0:T(8,128)S(1)} %get-tuple-element.86, bf16[9216,768]{1,0:T(8,128)(2,1)} %bitcast.139, f32[3072]{0:T(1024)S(1)} %add.324, f32[256]{0:T(256)S(1)} %bitcast.178, f32[768]{0:T(1024)S(1)} %copy-done.59, f32[768]{0:T(1024)S(1)} %copy-done.40, f32[768]{0:T(1024)S(1)} %copy-done.41, ...), kind=kOutput, calls=%fused_computation.53 | convolution fusion | flops 2423192832 | bytes 11040768 | tf_op jit(solution)/shard_map/dot_general | solution.py:41
  204.3 1.2 fusion.119
  206.2 1.3 multiply_reduce_fusion.5
  208.8 1.3 fusion.77
  213.6 1.3 select_reduce_fusion
  218.1 1.3 subtract_multiply_fusion
  221.3 2.5 fusion.124
  224.5 0.8 select_maximum_fusion.vector_start
  225.2 0.9 copy.88.z_column
  227.5 1.2 multiply_divide_fusion.pooled_row
  228.7 1.5 fusion.83
  230.2 1.0 pad_maximum_fusion.5.normed_two
  231.2 1.2 pad_maximum_fusion.2.mixed
  232.7 1.3 copy.85
  233.9 0.9 pad_maximum_fusion.4.context
  234.9 0.7 log_add_fusion.1
  235.8 0.7 log_add_fusion
  236.7 0.7 pad_maximum_fusion.6.log_total
  237.4 2.9 pad_maximum_fusion.project
  240.9 0.9 pad_maximum_fusion.3.normed
  241.8 1.2 pad_maximum_fusion.1.resid
  243.1 0.8 copy.87.keep_column
  243.9 187.0 %backward_and_sum.1 = (bf16[2,576,768]{2,1,0:T(8,128)(2,1)}, bf16[48,1664]{1,0:T(8,128)(2,1)}, f32[8,128]{1,0:T(8,128)}) custom-call(bf16[2,9216,768]{2,1,0:T(8,128)(2,1)} %bitcast.136, f32[2,256,768]{2,1,0:T(8,128)} %pad_maximum_fusion.1.resid, bf16[2,256,768]{2,1,0:T(8,128)(2,1)} %pad_maximum_fusion.3.normed, ...), custom_call_target="tpu_custom_call" | custom-call | tf_op jit(solution)/shard_map/backward_and_sum/pallas_call | solution.py:937
  430.9 1.4 fusion.129
  432.3 1.6 multiply_bitcast_fusion
  434.6 2.7 add_multiply_fusion
  437.3 0.8 multiply_add_fusion.1
  438.1 35.6 %orthogonalize.1 = (f32[2,576,768]{2,1,0:T(8,128)}, f32[2,576,768]{2,1,0:T(8,128)}, f32[2,576,768]{2,1,0:T(8,128)}, f32[2,576,768]{2,1,0:T(8,128)}) custom-call(f32[8,128]{1,0:T(8,128)} %get-tuple-element.24.totals, bf16[2,576,768]{2,1,0:T(8,128)(2,1)} %get-tuple-element.25.grad, f32[2,576,768]{2,1,0:T(8,128)} %momentum.1, f32[2,576,768]{2,1,0:T(8,128)} %mats.1, ...), custom_call_target="tpu_custom_call" | custom-call | tf_op jit(solution)/shard_map/orthogonalize/pallas_call | solution.py:1099
  (180 shorter events, 13.7 us)
Async XLA Ops:
  4.1 133.7 %copy-start.14 = (bf16[1,256,768]{2,1,0:T(8,128)(2,1)S(1)}, bf16[1,256,768]{2,1,0:T(8,128)(2,1)}, u32[]{:S(2)}) copy-start(bf16[1,256,768]{2,1,0:T(8,128)(2,1)} %param.14) | copy-start | bytes 1179652
  139.6 100.7 %copy-start = (f32[768,256]{0,1:T(8,128)}, f32[768,256]{0,1:T(8,128)S(1)}, u32[]{:S(2)}) copy-start(f32[768,256]{0,1:T(8,128)S(1)} %get-tuple-element.76) | copy-start | bytes 2359300
  139.7 31.9 %copy-start.27 = (f32[256]{0:T(256)}, f32[256]{0:T(256)S(1)}, u32[]{:S(2)}) copy-start(f32[256]{0:T(256)S(1)} %broadcast_multiply_fusion.4) | copy-start | bytes 3076
  139.9 31.6 %copy-start.30 = (f32[256]{0:T(256)}, f32[256]{0:T(256)S(1)}, u32[]{:S(2)}) copy-start(f32[256]{0:T(256)S(1)} %add_rsqrt_fusion.5) | copy-start | bytes 3076
  141.0 80.3 %copy-start.13 = (f32[28,768]{1,0:T(8,128)}, f32[28,768]{1,0:T(8,128)S(1)}, u32[]{:S(2)}) copy-start(f32[28,768]{1,0:T(8,128)S(1)} %convert_bitcast_fusion.1.vectors) | copy-start | bytes 258052
  141.7 6.1 %copy-start.36 = (f32[768]{0:T(1024)}, f32[768]{0:T(1024)S(1)}, u32[]{:S(2)}) copy-start(f32[768]{0:T(1024)S(1)} %get-tuple-element.45) | copy-start | bytes 9220
  141.7 6.1 %copy-start.38 = (f32[768]{0:T(1024)}, f32[768]{0:T(1024)S(1)}, u32[]{:S(2)}) copy-start(f32[768]{0:T(1024)S(1)} %get-tuple-element.46) | copy-start | bytes 9220
  141.7 29.8 %copy-start.21 = (f32[768]{0:T(1024)}, f32[768]{0:T(1024)S(1)}, u32[]{:S(2)}) copy-start(f32[768]{0:T(1024)S(1)} %get-tuple-element.47) | copy-start | bytes 9220
  141.7 29.8 %copy-start.23 = (f32[768]{0:T(1024)}, f32[768]{0:T(1024)S(1)}, u32[]{:S(2)}) copy-start(f32[768]{0:T(1024)S(1)} %get-tuple-element.48) | copy-start | bytes 9220
  141.7 35.7 %copy-start.42 = (f32[768]{0:T(1024)}, f32[768]{0:T(1024)S(1)}, u32[]{:S(2)}) copy-start(f32[768]{0:T(1024)S(1)} %get-tuple-element.40) | copy-start | bytes 9220
  141.7 35.7 %copy-start.43 = (f32[768]{0:T(1024)}, f32[768]{0:T(1024)S(1)}, u32[]{:S(2)}) copy-start(f32[768]{0:T(1024)S(1)} %get-tuple-element.41) | copy-start | bytes 9220
  141.8 42.7 %copy-start.32 = (f32[768]{0:T(1024)}, f32[768]{0:T(1024)S(1)}, u32[]{:S(2)}) copy-start(f32[768]{0:T(1024)S(1)} %get-tuple-element.37) | copy-start | bytes 9220
  141.8 42.7 %copy-start.34 = (f32[768]{0:T(1024)}, f32[768]{0:T(1024)S(1)}, u32[]{:S(2)}) copy-start(f32[768]{0:T(1024)S(1)} %get-tuple-element.38) | copy-start | bytes 9220
  142.1 5.7 %copy-start.44 = (f32[256]{0:T(256)}, f32[256]{0:T(256)S(1)}, u32[]{:S(2)}) copy-start(f32[256]{0:T(256)S(1)} %broadcast_multiply_fusion.3) | copy-start | bytes 3076
  142.4 5.4 %copy-start.53 = (f32[256]{0:T(256)}, f32[256]{0:T(256)S(1)}, u32[]{:S(2)}) copy-start(f32[256]{0:T(256)S(1)} %add_rsqrt_fusion.4) | copy-start | bytes 3076
  149.1 4.1 copy-start.5
  156.0 15.6 %copy-start.15 = (bf16[12,64,256]{2,1,0:T(8,128)(2,1)}, bf16[12,64,256]{2,1,0:T(8,128)(2,1)S(1)}, u32[]{:S(2)}) copy-start(bf16[12,64,256]{2,1,0:T(8,128)(2,1)S(1)} %fusion.66) | copy-start | bytes 1179652
  171.5 4.9 %copy-start.1 = (bf16[1,16,576,768]{3,2,1,0:T(8,128)(2,1)}, bf16[1,16,576,768]{3,2,1,0:T(8,128)(2,1)S(1)}, u32[]{:S(2)}) copy-start(bf16[1,16,576,768]{3,2,1,0:T(8,128)(2,1)S(1)} %get-tuple-element.59) | copy-start | bytes 42467332
  177.2 7.0 %copy-start.3 = (f32[256,768]{1,0:T(8,128)}, f32[256,768]{1,0:T(8,128)S(1)}, u32[]{:S(2)}) copy-start(f32[256,768]{1,0:T(8,128)S(1)} %get-tuple-element.80) | copy-start | bytes 2359300
  177.2 7.0 %copy-start.48 = (f32[256]{0:T(256)}, f32[256]{0:T(256)S(1)}, u32[]{:S(2)}) copy-start(f32[256]{0:T(256)S(1)} %broadcast_multiply_fusion.2) | copy-start | bytes 3076
  177.4 6.8 %copy-start.57 = (f32[256]{0:T(256)}, f32[256]{0:T(256)S(1)}, u32[]{:S(2)}) copy-start(f32[256]{0:T(256)S(1)} %add_rsqrt_fusion.3) | copy-start | bytes 3076
  187.7 3.5 copy-start.7
  196.6 7.0 %copy-start.49 = (f32[256]{0:T(256)}, f32[256]{0:T(256)S(1)}, u32[]{:S(2)}) copy-start(f32[256]{0:T(256)S(1)} %broadcast_multiply_fusion) | copy-start | bytes 3076
  196.8 6.8 %copy-start.58 = (f32[256]{0:T(256)}, f32[256]{0:T(256)S(1)}, u32[]{:S(2)}) copy-start(f32[256]{0:T(256)S(1)} %add_rsqrt_fusion.1) | copy-start | bytes 3076
  196.9 6.8 %copy-start.61 = (s32[1,256]{1,0:T(1,128)S(1)}, s32[1,256]{1,0:T(1,128)}, u32[]{:S(2)}) copy-start(s32[1,256]{1,0:T(1,128)} %param.15) | copy-start | bytes 3076
  196.9 14.5 %copy-start.2 = (bf16[1000,512]{1,0:T(8,128)(2,1)S(1)}, bf16[1000,512]{1,0:T(8,128)(2,1)}, u32[]{:S(2)}) copy-start(bf16[1000,512]{1,0:T(8,128)(2,1)} %param.18) | copy-start | bytes 3072004
  220.0 11.2 %copy-start.4 = (f32[256,768]{1,0:T(8,128)S(1)}, f32[256,768]{1,0:T(8,128)}, u32[]{:S(2)}) copy-start(f32[256,768]{1,0:T(8,128)} %copy-done.3) | copy-start | bytes 2359300
  221.3 7.4 %copy-start.29 = (f32[512]{0:T(512)}, f32[512]{0:T(512)S(1)}, u32[]{:S(2)}) copy-start(f32[512]{0:T(512)S(1)} %multiply_subtract_fusion.1) | copy-start | bytes 6148
  228.7 3.8 copy-start.9
  232.5 4.9 %copy-start.6 = (bf16[256,2304]{1,0:T(8,128)(2,1)S(1)}, bf16[256,2304]{1,0:T(8,128)(2,1)}, u32[]{:S(2)}) copy-start(bf16[256,2304]{1,0:T(8,128)(2,1)} %copy-done.5) | copy-start | bytes 3538948
  234.9 5.5 %copy-start.22 = (f32[768]{0:T(1024)S(1)}, f32[768]{0:T(1024)}, u32[]{:S(2)}) copy-start(f32[768]{0:T(1024)} %copy-done.21) | copy-start | bytes 9220
  234.9 5.5 %copy-start.24 = (f32[768]{0:T(1024)S(1)}, f32[768]{0:T(1024)}, u32[]{:S(2)}) copy-start(f32[768]{0:T(1024)} %copy-done.23) | copy-start | bytes 9220
  234.9 5.5 %copy-start.28 = (f32[256]{0:T(256)S(1)}, f32[256]{0:T(256)}, u32[]{:S(2)}) copy-start(f32[256]{0:T(256)} %copy-done.27) | copy-start | bytes 3076
  234.9 5.5 %copy-start.31 = (f32[256]{0:T(256)S(1)}, f32[256]{0:T(256)}, u32[]{:S(2)}) copy-start(f32[256]{0:T(256)} %copy-done.30) | copy-start | bytes 3076
  234.9 5.5 %copy-start.33 = (f32[768]{0:T(1024)S(1)}, f32[768]{0:T(1024)}, u32[]{:S(2)}) copy-start(f32[768]{0:T(1024)} %copy-done.32) | copy-start | bytes 9220
  234.9 5.5 %copy-start.35 = (f32[768]{0:T(1024)S(1)}, f32[768]{0:T(1024)}, u32[]{:S(2)}) copy-start(f32[768]{0:T(1024)} %copy-done.34) | copy-start | bytes 9220
  234.9 5.5 %copy-start.37 = (f32[768]{0:T(1024)S(1)}, f32[768]{0:T(1024)}, u32[]{:S(2)}) copy-start(f32[768]{0:T(1024)} %copy-done.36) | copy-start | bytes 9220
  234.9 5.5 %copy-start.39 = (f32[768]{0:T(1024)S(1)}, f32[768]{0:T(1024)}, u32[]{:S(2)}) copy-start(f32[768]{0:T(1024)} %copy-done.38) | copy-start | bytes 9220
  234.9 5.5 %copy-start.45 = (f32[256]{0:T(256)S(1)}, f32[256]{0:T(256)}, u32[]{:S(2)}) copy-start(f32[256]{0:T(256)} %copy-done.44) | copy-start | bytes 3076
  234.9 5.5 %copy-start.47 = (f32[256]{0:T(256)S(1)}, f32[256]{0:T(256)}, u32[]{:S(2)}) copy-start(f32[256]{0:T(256)} %copy-done.46) | copy-start | bytes 3076
  234.9 5.5 %copy-start.54 = (f32[256]{0:T(256)S(1)}, f32[256]{0:T(256)}, u32[]{:S(2)}) copy-start(f32[256]{0:T(256)} %copy-done.53) | copy-start | bytes 3076
  234.9 5.5 %copy-start.56 = (f32[256]{0:T(256)S(1)}, f32[256]{0:T(256)}, u32[]{:S(2)}) copy-start(f32[256]{0:T(256)} %copy-done.55) | copy-start | bytes 3076
  243.9 190.8 %copy-start.11 = (f32[1564,48]{0,1:T(8,128)S(1)}, f32[1564,48]{0,1:T(8,128)}, u32[]{:S(2)}) copy-start(f32[1564,48]{0,1:T(8,128)} %param.23) | copy-start | bytes 900868
  243.9 190.8 %copy-start.16 = (f32[1564,48]{0,1:T(8,128)S(1)}, f32[1564,48]{0,1:T(8,128)}, u32[]{:S(2)}) copy-start(f32[1564,48]{0,1:T(8,128)} %param.24) | copy-start | bytes 900868
  243.9 190.8 %copy-start.17 = (f32[1564,48]{0,1:T(8,128)S(1)}, f32[1564,48]{0,1:T(8,128)}, u32[]{:S(2)}) copy-start(f32[1564,48]{0,1:T(8,128)} %param.26) | copy-start | bytes 900868
  243.9 190.8 %copy-start.18 = (f32[1564,48]{0,1:T(8,128)S(1)}, f32[1564,48]{0,1:T(8,128)}, u32[]{:S(2)}) copy-start(f32[1564,48]{0,1:T(8,128)} %param.27) | copy-start | bytes 900868
  430.9 6.4 %copy-start.19 = (f32[1564,48]{0,1:T(8,128)S(1)}, f32[1564,48]{0,1:T(8,128)}, u32[]{:S(2)}) copy-start(f32[1564,48]{0,1:T(8,128)} %param.25) | copy-start | bytes 900868
  437.3 36.4 %copy-start.12 = (f32[1564,48]{0,1:T(8,128)}, f32[1564,48]{0,1:T(8,128)S(1)}, u32[]{:S(2)}) copy-start(f32[1564,48]{0,1:T(8,128)S(1)} %get-tuple-element.54) | copy-start | bytes 900868
  (14 other events, 36.9 us)

commit v5 on v4

--- a/solution.py
+++ b/solution.py
@@ -13,6 +13,7 @@
 HDIM = 64
 PIX = 768
 EMB = 512
+CLASSES = 1000
 SEQ = 256
 NS_STEPS = 5
 STEPS_DONE = 10
@@ -251,69 +252,352 @@
 
     return start, step, share, settle
 
-
-def gather_kernel(depth, halves, rows, mats, all_rows, all_mats, send_sem, recv_sem, local_sem):
+def split(value):
+    high = value.astype(BF)
+    return high, (value - high.astype(F32)).astype(BF)
+
+
+def forward_kernel(
+    depth,
+    halves,
+    rows,
+    mats,
+    patches,
+    keep,
+    keep_column,
+    classes,
+    label,
+    weight,
+    all_mats,
+    resid,
+    normed,
+    project,
+    log_total,
+    context,
+    mixed,
+    normed_two,
+    embedded,
+    vectors,
+    pooled_row,
+    z_rows,
+    feature_rows,
+    vector_start,
+    stats,
+    rows_v,
+    resid_v,
+    normed_v,
+    project_v,
+    log_v,
+    context_v,
+    mixed_v,
+    two_v,
+    embed_v,
+    weight_v,
+    total_v,
+    class_v,
+    send_sem,
+    recv_sem,
+    local_sem,
+    weight_sem,
+    save_sem,
+):
     links = Links(depth, send_sem, recv_sem)
     links.greet()
-    layers, count = mats.shape[:2]
+    layers, count, width = mats.shape
     size = count // halves
-    own = [pltpu.make_async_copy(rows, all_rows.at[links.me], local_sem.at[0])]
-    items = [gather_item(links, rows, lambda shard: all_rows.at[shard], rows.shape[0])]
+    own = [pltpu.make_async_copy(rows, rows_v.at[links.me], local_sem.at[0])]
+    items = [gather_item(links, rows, lambda shard: rows_v.at[shard], rows.shape[0])]
     for layer in range(layers):
         own.append(
             pltpu.make_async_copy(
-                mats.at[layer], all_mats.at[layer, links.me], local_sem.at[1 + layer]
+                mats.at[layer],
+                all_mats.at[layer, pl.ds(links.me * count, count)],
+                local_sem.at[1 + layer],
             )
         )
         for half in range(halves):
-            block = pl.ds(half * size, size)
-
-            def target(shard, layer=layer, block=block):
-                return all_mats.at[layer, shard, block]
-
-            items.append(gather_item(links, mats.at[layer, block], target, size))
+
+            def target(shard, layer=layer, half=half):
+                return all_mats.at[layer, rows_at(shard * count + half * size, size)]
+
+            items.append(gather_item(links, mats.at[layer, pl.ds(half * size, size)], target, size))
     for copy in own:
         copy.start()
+    saves = []
+
+    def save(source, target):
+        copy = pltpu.make_async_copy(source, target, save_sem.at[len(saves)])
+        copy.start()
+        saves.append(copy)
+
+    def table(begin, amount):
+        return rows_v[:, :, pl.ds(begin, amount)].reshape(width, amount)
+
+    pixels, seq = patches.shape[1], patches.shape[0]
+
+    def column(index):
+        return vectors[pl.ds(index, 1), :]
+
+    def embed():
+        own[0].wait()
+        vectors[...] = table(pixels + EMB + SEQ, 128).astype(F32).T
+        position = table(pixels + EMB, SEQ).astype(F32).T
+        embed_v[...] = matmul_nt(patches[...], table(0, pixels)) + position
+        save(embed_v, embedded)
+        resid_v[0] = norm_forward(embed_v[...], column(0), column(1))
+
+    order = []
+    for layer in range(layers):
+        order += [(layer, index) for index in (0, 1, 2, 3, 4, 8, 5, 9, 6, 10, 7, 11)]
+
+    def chunk_copy(number):
+        layer, index = order[number]
+        return pltpu.make_async_copy(
+            all_mats.at[layer, pl.ds(index * width, width)],
+            weight_v.at[number % 4],
+            weight_sem.at[number % 4],
+        )
+
+    def chunk(number):
+        chunk_copy(number).wait()
+        return weight_v[number % 4]
+
+    half_lane = lax.broadcasted_iota(jnp.int32, (1, 128), 1) < HDIM
+    scale = HDIM ** (-0.5)
+
+    def attention_pair(layer, pair):
+        def lanes(base):
+            return pl.ds(pl.multiple_of(base + pair * 128, 128), 128)
+
+        query, key = project_v[layer, :, lanes(0)], project_v[layer, :, lanes(width)]
+        value = project_v[layer, :, lanes(2 * width)]
+        results = []
+        kept = log_v[layer]
+        lane = lax.broadcasted_iota(jnp.int32, kept.shape, 1)
+        for head in range(2):
+            here = half_lane if head == 0 else jnp.logical_not(half_lane)
+            query_h = jnp.where(here, query, jnp.zeros_like(query))
+            scores = jnp.where(keep[...] > 0, matmul_nt(query_h, key) * scale, -1000000000.0)
+            top = jnp.max(scores, -1, keepdims=True)
+            expo = jnp.exp(scores - top)
+            total = jnp.sum(expo, -1, keepdims=True)
+            kept = jnp.where(lane == 2 * pair + head, top + jnp.log(total), kept)
+            results.append(matmul((expo / total).astype(BF), value))
+        log_v[layer] = kept
+        context_v[layer, :, lanes(0)] = jnp.where(half_lane, results[0], results[1]).astype(BF)
+
+    def layer_steps(layer):
+        base, first = 4 + 12 * layer, 12 * layer
+
+        def vector(index):
+            return column(base + index)
+
+        for number in range(first, first + 4):
+            chunk_copy(number).start()
+        log_v[layer] = jnp.zeros_like(log_v[layer])
+        save(resid_v.at[layer], resid.at[layer])
+        normed_v[layer] = norm_forward(resid_v[layer], vector(0), vector(1)).astype(BF)
+        save(normed_v.at[layer], normed.at[layer])
+        for part in range(3):
+            result = matmul_nt(normed_v[layer], chunk(first + part))
+            if part != 1:
+                result += vector(2 if part == 0 else 3)
+            project_v[layer, :, pl.ds(part * width, width)] = result.astype(BF)
+            chunk_copy(first + 4 + part).start()
+        save(project_v.at[layer], project.at[layer])
+        yield
+        for third in range(3):
+
+            @pl.loop(0, 2)
+            def _(turn, third=third):
+                attention_pair(layer, 2 * third + turn)
+
+            yield
+        save(context_v.at[layer], context.at[layer])
+        save(log_v.at[layer], log_total.at[layer])
+        mixed_v[layer] = resid_v[layer] + (
+            matmul_nt(context_v[layer], chunk(first + 3)) + vector(4)
+        )
+        chunk_copy(first + 7).start()
+        save(mixed_v.at[layer], mixed.at[layer])
+        two_v[layer] = norm_forward(mixed_v[layer], vector(5), vector(6)).astype(BF)
+        save(two_v.at[layer], normed_two.at[layer])
+        yield
+        total_v[...] = mixed_v[layer] + vector(7)
+        for part in range(4):
+            number = first + 4 + 2 * part
+            pre = matmul_nt(two_v[layer], chunk(number)) + vector(8 + part)
+            hidden = (pre * jax.nn.sigmoid(1.702 * pre)).astype(BF)
+            total_v[...] += matmul(hidden, chunk(number + 1))
+            for ahead in (number + 4, number + 5):
+                if ahead < first + 12:
+                    chunk_copy(ahead).start()
+            if part < 3:
+                yield
+        resid_v[layer + 1] = total_v[...]
+        yield
+
+    def class_units():
+        value = classes[...].astype(F32)
+        length = lax.rsqrt(jnp.sum(value * value, -1, keepdims=True) + unit_epsilon)
+        class_v[...] = (value * length).astype(BF)
+
+    def head():
+        number = jnp.sum(keep[...], -1, keepdims=True)
+        pooled = jnp.sum(resid_v[layers] * keep_column[...], 0, keepdims=True) / number
+        center = pooled - jnp.mean(pooled, -1, keepdims=True)
+        spread = lax.rsqrt(jnp.mean(center * center, -1, keepdims=True) + norm_epsilon)
+        normal = center * spread
+        z_value = jnp.broadcast_to(normal * column(2) + column(3), (16, width)).astype(BF)
+        proj = table(pixels, EMB)
+        feature = matmul(z_value, proj)
+        inverse = lax.rsqrt(jnp.sum(feature * feature, -1, keepdims=True) + unit_epsilon)
+        unit = (feature * inverse).astype(BF)
+        logits = logit_scale * matmul_nt(unit, class_v[...])
+        lane = lax.broadcasted_iota(jnp.int32, logits.shape, 1)
+        logits = jnp.where(lane < CLASSES, logits, -1e30)
+        top = jnp.max(logits, -1, keepdims=True)
+        shifted = jnp.exp(logits - top)
+        total = jnp.sum(shifted, -1, keepdims=True)
+        chosen = lane == label[...]
+        loss = top + jnp.log(total) - jnp.sum(jnp.where(chosen, logits, 0.0), -1, keepdims=True)
+        logit_grad = weight[...] * (shifted / total - chosen.astype(F32))
+        high, low = split(logit_grad)
+        unit_grad = logit_scale * (matmul(high, class_v[...]) + matmul(low, class_v[...]))
+        feature_grad = inverse * unit_grad - feature * inverse**3 * jnp.sum(
+            unit_grad * feature, -1, keepdims=True
+        )
+        high, low = split(feature_grad)
+        z_grad = (matmul_nt(high, proj) + matmul_nt(low, proj))[:1]
+        scaled = z_grad * column(2)
+        inner = spread * (
+            scaled
+            - jnp.mean(scaled, -1, keepdims=True)
+            - normal * jnp.mean(scaled * normal, -1, keepdims=True)
+        )
+        pooled_row[...] = jnp.broadcast_to(inner / number, pooled_row.shape)
+        spot = lax.broadcasted_iota(jnp.int32, (16, 1), 0)
+        z_rows[...] = jnp.where(spot < 2, z_value, jnp.zeros_like(z_value))
+        picked = jnp.where(spot == 0, high, jnp.where(spot == 1, low, jnp.zeros_like(low)))
+        feature_rows[...] = picked
+        vector_start[...] = jnp.zeros_like(vector_start)
+        vector_start[pl.ds(2, 1), :] = z_grad * normal
+        vector_start[pl.ds(3, 1), :] = z_grad
+        here = lax.broadcasted_iota(jnp.int32, (8, 128), 1)
+        first = lax.broadcasted_iota(jnp.int32, (8, 128), 0) == 0
+        value = jnp.where(first & (here == 1), (loss * weight[...])[:8], 0.0)
+        stats[...] = jnp.where(first & (here == 2), jnp.broadcast_to(weight[...], (8, 128)), value)
+
+    running = None
+
+    def work(amount):
+        nonlocal running
+        for _ in range(amount):
+            if running is None:
+                return
+            if next(running, 0) == 0:
+                running = None
+
     items[0][0]()
+    class_units()
     for number, (_, step, _, _) in enumerate(items):
         step(1)
+        work(1)
         step(2)
         if number + 1 < len(items):
             items[number + 1][0]()
+        work(1)
         if number > 0:
             items[number - 1][2]()
+        work(1)
         for far in range(3, depth):
             step(far)
+        work(1)
+        if number > 0:
+            items[number - 1][3]()
+            if number == 1:
+                embed()
+            for layer in range(layers - 1):
+                if number - 1 == halves * (layer + 1):
+                    own[1 + layer].wait()
+                    work(1000)
+                    running = counted(layer_steps(layer))
+        work(1)
     items[-1][2]()
-    for item in items:
-        item[3]()
+    work(2)
+    items[-1][3]()
+    work(1000)
+    own[layers].wait()
+    for _ in layer_steps(layers - 1):
+        pass
+    head()
     links.finish()
-    for copy in own:
+    for copy in saves:
         copy.wait()
 
 
-def gather(depth, rows, mats):
+def counted(steps):
+    for _ in steps:
+        yield 1
+
+
+def forward(depth, rows, mats, patches, keep, keep_column, classes, label, weight):
     layers, count, width = mats.shape
     shards = PLANE * depth
     halves = 2
+    seq = patches.shape[0]
     slots = (1 + layers * halves) * 60
     any_space = pl.BlockSpec(memory_space=pl.ANY)
+    vmem = pl.BlockSpec(memory_space=pltpu.VMEM)
+
+    def shape(*sizes, dtype=F32):
+        return jax.ShapeDtypeStruct(sizes, dtype)
+
+    saved = (
+        shape(layers, seq, width),
+        shape(layers, seq, width, dtype=BF),
+        shape(layers, seq, 3 * width, dtype=BF),
+        shape(layers, seq, 128),
+        shape(layers, seq, width, dtype=BF),
+        shape(layers, seq, width),
+        shape(layers, seq, width, dtype=BF),
+    )
     return pl.pallas_call(
-        functools.partial(gather_kernel, depth, halves),
-        out_shape=(
-            jax.ShapeDtypeStruct((shards,) + rows.shape, BF),
-            jax.ShapeDtypeStruct((layers, shards, count, width), BF),
+        functools.partial(forward_kernel, depth, halves),
+        out_shape=(shape(layers, shards * count, width, dtype=BF),)
+        + saved
+        + (
+            shape(seq, width),
+            shape(128, width),
+            shape(8, width),
+            shape(16, width, dtype=BF),
+            shape(16, EMB, dtype=BF),
+            shape(128, width),
+            shape(8, 128),
         ),
-        in_specs=[any_space] * 2,
-        out_specs=[any_space] * 2,
+        in_specs=[any_space] * 2 + [vmem] * 6,
+        out_specs=[any_space] * 9 + [vmem] * 6,
         scratch_shapes=[
+            pltpu.VMEM((shards,) + rows.shape, BF),
+            pltpu.VMEM((layers + 1, seq, width), F32),
+        ]
+        + [pltpu.VMEM(array.shape, array.dtype) for array in saved[1:]]
+        + [
+            pltpu.VMEM((seq, width), F32),
+            pltpu.VMEM((4, width, width), BF),
+            pltpu.VMEM((seq, width), F32),
+            pltpu.VMEM(classes.shape, BF),
             pltpu.SemaphoreType.DMA((slots,)),
             pltpu.SemaphoreType.DMA((slots,)),
             pltpu.SemaphoreType.DMA((1 + layers,)),
+            pltpu.SemaphoreType.DMA((4,)),
+            pltpu.SemaphoreType.DMA((1 + 7 * layers,)),
         ],
-        name="gather_weights",
-        compiler_params=pltpu.CompilerParams(collective_id=1, has_side_effects=True),
-    )(rows, mats)
+        name="gather_and_forward",
+        compiler_params=pltpu.CompilerParams(
+            collective_id=1, has_side_effects=True, vmem_limit_bytes=56 * 1024 * 1024
+        ),
+    )(rows, mats, patches, keep, keep_column, classes, label, weight)
 
 
 def accumulate(target, start, source, begin, count, step):
@@ -458,8 +742,8 @@
     keep,
     keep_column,
     pooled_row,
-    z_column,
-    feature_row,
+    z_rows,
+    feature_rows,
     vector_start,
     stats,
     out,
@@ -577,7 +861,7 @@
     )
     note[...] = stats[...]
     vector_v[...] = vector_start[...]
-    up_v[...] = keep_column[...] * pooled_row[...]
+    up_v[...] = keep_column[...] * pooled_row[pl.ds(0, 1), :]
     lane = lax.broadcasted_iota(jnp.int32, (8, 128), 1)
     first = lax.broadcasted_iota(jnp.int32, (8, 128), 0) == 0
 
@@ -862,17 +1146,17 @@
     short_v[...] = inner.astype(BF)
     total_v[...] = inner
     patch_load.wait()
-    pixels, embeds, seq = patch_v.shape[1], feature_row.shape[1], inner.shape[0]
+    pixels, embeds, seq = patch_v.shape[1], feature_rows.shape[1], inner.shape[0]
     for turn in range(width // piece):
         columns = pl.ds(turn * piece, piece)
         patch_grad = matmul_tn(short_v[:, columns], patch_v[...])
+        proj_grad = matmul_tn(z_rows[:, columns], feature_rows[...])
         position = total_v[:, columns].T
         vector_grad = vector_v[:, columns].T
         for part in range(piece // rows):
             shard, inside = turn * (piece // rows) + part, slice(part * rows, (part + 1) * rows)
             rows_v[shard, :, pl.ds(0, pixels)] = patch_grad[inside].astype(BF)
-            proj = z_column[pl.ds(shard * rows, rows), :] * feature_row[...]
-            rows_v[shard, :, pl.ds(pixels, embeds)] = proj.astype(BF)
+            rows_v[shard, :, pl.ds(pixels, embeds)] = proj_grad[inside].astype(BF)
             rows_v[shard, :, pl.ds(pixels + embeds, seq)] = position[inside].astype(BF)
             rows_v[shard, :, pl.ds(pixels + embeds + seq, 128)] = vector_grad[inside].astype(BF)
     for number in range(first_row_group, len(groups)):
@@ -1410,84 +1694,36 @@
     row_second,
 ):
     layers, columns, width = layer_mats.shape
-    images, seq, pixels = patches.shape
     shards = lax.axis_size("fsdp")
     depth = shards // PLANE
     rows, share = row_params.shape
-    front = PIX + EMB + SEQ + 4
     lanes = -(-rows // 128) * 128
     valid_mask = pad_mask.astype(F32)
     sent_rows = jnp.pad(row_params.T.astype(BF), ((0, 0), (0, lanes - rows)))
-    all_rows, all_mats = gather(depth, sent_rows, layer_mats.astype(BF))
-    table = all_rows.reshape(width, lanes)
-    weights = all_mats.reshape(layers, shards * columns, width)
-    patch_weight, proj = table[:, :PIX], table[:, PIX : PIX + EMB]
-    position = table[:, PIX + EMB : PIX + EMB + SEQ].T.astype(F32)
-    vectors = table[:, PIX + EMB + SEQ : rows].T.astype(F32)
-    head_vec = vectors[:4]
-    layer_vector_params = vectors[4:].reshape(layers, 12, width)
-    flat_patches = patches.reshape(images * seq, pixels)
-    embedded = (
-        matmul_nt(flat_patches, patch_weight).reshape(images, seq, width) + position
-    ).reshape(images * seq, width)
-    resid = norm_forward(embedded, head_vec[0], head_vec[1])
-    saved_activations = []
-    for layer_number in range(layers):
-        resid, saved_activation = layer_forward(
-            resid, weights[layer_number], layer_vector_params[layer_number], valid_mask
-        )
-        before, normed, project, log_total, context, mixed, normed_two, _, _ = saved_activation
-        log_total = jnp.pad(log_total.reshape(HEADS, seq).T, ((0, 0), (0, 128 - HEADS)))
-        saved_activations.append(
-            (before, normed, project, log_total, context, mixed, normed_two)
-        )
-    saved = [jnp.stack(parts) for parts in zip(*saved_activations)]
-    counts = jnp.sum(valid_mask, -1, keepdims=True)
-    pooled = jnp.sum(resid.reshape(images, seq, width) * valid_mask[..., None], 1) / counts
-    pooled_norm = norm_forward(pooled, head_vec[2], head_vec[3]).astype(BF)
-    feature = matmul(pooled_norm, proj)
-    inv_length = lax.rsqrt(jnp.sum(feature * feature, -1, keepdims=True) + unit_epsilon)
-    unit_feat = (feature * inv_length).astype(BF)
-    classes = class_emb.astype(F32)
-    class_unit = (
-        classes * lax.rsqrt(jnp.sum(classes * classes, -1, keepdims=True) + unit_epsilon)
-    ).astype(BF)
-    logits = logit_scale * matmul_nt(unit_feat, class_unit)
-    top_logit = jnp.max(logits, -1, keepdims=True)
-    shifted = jnp.exp(logits - top_logit)
-    total_exp = jnp.sum(shifted, -1, keepdims=True)
-    log_norm = top_logit + jnp.log(total_exp)
-    onehot = (jnp.arange(logits.shape[1])[None, :] == labels[:, None]).astype(F32)
-    losses = log_norm[:, 0] - jnp.sum(onehot * logits, -1)
-    weights_value = loss_weights.astype(F32)
-    logit_grad = weights_value[:, None] * (shifted / total_exp - onehot)
-    unit_grad = logit_scale * jnp.dot(logit_grad, class_unit.astype(F32), precision=HIGHEST)
-    feat_grad = inv_length * unit_grad - feature * inv_length**3 * jnp.sum(
-        unit_grad * feature, -1, keepdims=True
-    )
-    pooled_grad, gain_post, shift_post = norm_backward(
-        pooled,
-        head_vec[2],
-        lax.dot_general(
-            feat_grad, proj.astype(F32), (((1,), (1,)), ((), ())), precision=HIGHEST
-        ),
-    )
-    lane = lax.broadcasted_iota(jnp.int32, (8, 128), 1)
-    first = lax.broadcasted_iota(jnp.int32, (8, 128), 0) == 0
-    stats = jnp.where(first & (lane == 1), jnp.sum(weights_value * losses), 0.0)
-    stats = jnp.where(first & (lane == 2), jnp.sum(weights_value), stats)
+    classes = jnp.pad(class_emb, ((0, -class_emb.shape[0] % 128), (0, 0)))
+    weights, *saved, embedded, vectors, pooled_row, z_rows, feature_rows, start, stats = forward(
+        depth,
+        sent_rows,
+        layer_mats.astype(BF),
+        patches[0],
+        valid_mask,
+        valid_mask.T,
+        classes,
+        labels[:, None],
+        loss_weights.astype(F32)[:, None],
+    )
     mat_total, row_total, totals = backward(
         depth,
         lax.axis_size("ns"),
         weights,
         saved,
         embedded,
-        flat_patches,
+        patches[0],
         vectors,
         valid_mask,
         valid_mask.T,
-        (pooled_grad / counts, pooled_norm.astype(F32).T, feat_grad),
-        jnp.pad(jnp.stack([gain_post, shift_post]), ((2, 124), (0, 0))),
+        (pooled_row, z_rows, feature_rows),
+        start,
         stats,
     )
     loss_sum, weight_sum, grad_norm, clip = (totals[0, turn] for turn in range(4))

time: 480 us -> 404 us (0.84)
  matrix products: 34.9 us -> 0 us
  local copies, waits for them, and re-layouts: 39.2 us -> 5.92 us
  other arithmetic: 37.1 us -> 10.7 us
  Pallas kernels: 354 us -> 380 us
  between operations: 8.71 us -> 2.48 us
    dot_general x15 -> x0, matrix products: 34.9 us -> none  [the longest x3 14.7 us: matmul(): return jnp.dot(left, right, preferred_element_type=jnp.float32)]
    pallas_call x1, Pallas kernels: 132 us -> 156 us  [forward(): pl.pallas_call(functools.partial(forward_kernel, depth, halves), out_shap...]
    slice x6 -> x0, local copies, waits for them, and re-layouts: 23.6 us -> none  [the longest x1 15.6 us: fast_body(): weights[layer_number]]
    another operation x10 -> x0, other arithmetic: 11.3 us -> none  [the longest x8 10.5 us: fast_body(): saved = [jnp.stack(parts) for parts in zip(*saved_activations)]]
    reduce_sum x15 -> x0, other arithmetic: 8.84 us -> none  [the longest x2 1.46 us: layer_forward(): totals = jnp.sum(expo, -1, keepdims=True)]
    unnamed x126 -> x12, local copies, waits for them, and re-layouts: 6.17 us -> 0.04 us
where the time goes in v5:
time: 404 us; the launch traced here: 399 us
  Pallas kernels  380 us (94%)
  other arithmetic  10.7 us (3%)
  local copies, waits for them, and re-layouts  5.92 us (1%)
    pallas_call x1, Pallas kernels, backward(): pl.pallas_call(functools.partial(backward_kernel, depth, sides, layers),...  188 us
    pallas_call x1, Pallas kernels, forward(): pl.pallas_call(functools.partial(forward_kernel, depth, halves), out_shap...  156 us
    pallas_call x1, Pallas kernels, finish(): pl.pallas_call(functools.partial(finish_kernel, 0.2 * math.sqrt(width)),...  35.6 us

profile of v5, /device:TPU:0, one launch (start us, length us, event | category | flops | bytes accessed | tf_op | source)
XLA Modules:
  0.0 399.4 jit_solution(14550133353104326172)
XLA Ops:
  1.9 1.2 convert_bitcast_fusion.1
  3.2 0.8 copy.28.keep_column
  4.0 1.0 convert_bitcast_fusion
  5.0 0.7 pad.8.rows
  5.7 2.3 pad.9.classes
  7.9 3.4 convert_element_type.22.mats
  11.3 156.4 %gather_and_forward.1 = (bf16[2,9216,768]{2,1,0:T(8,128)(2,1)}, f32[2,256,768]{2,1,0:T(8,128)}, bf16[2,256,768]{2,1,0:T(8,128)(2,1)}, bf16[2,256,2304]{2,1,0:T(8...) custom-call(bf16[48,1664]{1,0:T(8,128)(2,1)} %pad.8.rows, ...), custom_call_target="tpu_custom_call" | custom-call | tf_op jit(solution)/shard_map/gather_and_forward/pallas_call | solution.py:565
  167.7 0.0 copy-start
  167.8 0.0 copy-start.2
  167.8 0.0 copy-start.3
  167.8 0.0 copy-start.4
  167.8 188.3 %backward_and_sum.1 = (bf16[2,576,768]{2,1,0:T(8,128)(2,1)}, bf16[48,1664]{1,0:T(8,128)(2,1)}, f32[8,128]{1,0:T(8,128)}) custom-call(bf16[2,9216,768]{2,1,0:T(8,128)(2,1)} %get-tuple-element.35.weights, f32[2,256,768]{2,1,0:T(8,128)} %get-tuple-element.36.resid, bf16[2,256,768]{2,1,0:T(8,128)(2,1)} %get-tuple-element.37.normed, ...), custom_call_target="tpu_custom_call" | custom-call | tf_op jit(solution)/shard_map/backward_and_sum/pallas_call | solution.py:1221
  356.1 0.0 copy-start.5
  356.1 1.4 fusion.2
  357.5 1.6 multiply_bitcast_fusion
  359.1 0.1 slice.32
  359.2 0.1 copy.30
  359.3 0.6 slice.33
  359.8 0.0 copy-done
  359.8 0.0 copy-done.2
  359.8 0.0 copy-done.3
  359.8 0.0 copy-done.4
  359.8 2.7 add_multiply_fusion
  362.5 0.0 copy-start.1
  362.5 0.0 copy-done.5
  362.5 0.8 multiply_add_fusion
  363.4 35.6 %orthogonalize.1 = (f32[2,576,768]{2,1,0:T(8,128)}, f32[2,576,768]{2,1,0:T(8,128)}, f32[2,576,768]{2,1,0:T(8,128)}, f32[2,576,768]{2,1,0:T(8,128)}) custom-call(f32[8,128]{1,0:T(8,128)} %get-tuple-element.50.totals, bf16[2,576,768]{2,1,0:T(8,128)(2,1)} %get-tuple-element.51.grad, f32[2,576,768]{2,1,0:T(8,128)} %momentum.1, f32[2,576,768]{2,1,0:T(8,128)} %mats.1, ...), custom_call_target="tpu_custom_call" | custom-call | tf_op jit(solution)/shard_map/orthogonalize/pallas_call | solution.py:1383
  399.0 0.0 copy-done.1
  (1 shorter events, 0.0 us)
Async XLA Ops:
  167.7 192.1 %copy-start = (f32[1564,48]{0,1:T(8,128)S(1)}, f32[1564,48]{0,1:T(8,128)}, u32[]{:S(2)}) copy-start(f32[1564,48]{0,1:T(8,128)} %param.23) | copy-start | bytes 900868
  167.8 192.1 %copy-start.2 = (f32[1564,48]{0,1:T(8,128)S(1)}, f32[1564,48]{0,1:T(8,128)}, u32[]{:S(2)}) copy-start(f32[1564,48]{0,1:T(8,128)} %param.24) | copy-start | bytes 900868
  167.8 192.1 %copy-start.3 = (f32[1564,48]{0,1:T(8,128)S(1)}, f32[1564,48]{0,1:T(8,128)}, u32[]{:S(2)}) copy-start(f32[1564,48]{0,1:T(8,128)} %param.26) | copy-start | bytes 900868
  167.8 192.1 %copy-start.4 = (f32[1564,48]{0,1:T(8,128)S(1)}, f32[1564,48]{0,1:T(8,128)}, u32[]{:S(2)}) copy-start(f32[1564,48]{0,1:T(8,128)} %param.27) | copy-start | bytes 900868
  356.1 6.5 %copy-start.5 = (f32[1564,48]{0,1:T(8,128)S(1)}, f32[1564,48]{0,1:T(8,128)}, u32[]{:S(2)}) copy-start(f32[1564,48]{0,1:T(8,128)} %param.25) | copy-start | bytes 900868
  362.5 36.4 %copy-start.1 = (f32[1564,48]{0,1:T(8,128)}, f32[1564,48]{0,1:T(8,128)S(1)}, u32[]{:S(2)}) copy-start(f32[1564,48]{0,1:T(8,128)S(1)} %get-tuple-element.58) | copy-start | bytes 900868

commit v6 on v5

--- a/solution.py
+++ b/solution.py
@@ -13,7 +13,6 @@
 HDIM = 64
 PIX = 768
 EMB = 512
-CLASSES = 1000
 SEQ = 256
 NS_STEPS = 5
 STEPS_DONE = 10
@@ -164,19 +163,26 @@
 def gather_item(links, own, target, count):
     depth, z, y, c, x = links.depth, links.z, links.y, links.c, links.x
     third = count // 3
-    begin = x * third
+    early = count // 9 // 16 * 16
+    begin, amount = x * (third + early), 2 * third - early
+    early_begin = amount - x * (third - early)
     origin = (0, 0)
     keys = [(side, far) for far in range(1, depth) for side in (-1, 1)]
     z_slot = {key: links.slot() for key in keys}
     y_slot = {key: links.slot() for key in keys + [origin]}
+    e_slot = {(key, o): links.slot() for key in keys for o in (0, 1)}
+    pair_slot = links.slot()
     x_slot = {(key, o): links.slot() for key in keys + [origin] for o in (0, 1)}
     c_slot = {(key, o): links.slot() for key in keys + [origin] for o in (0, 1)}
 
     def part(shard):
-        return target(shard).at[rows_at(begin, 2 * third)]
+        return target(shard).at[rows_at(begin, amount)]
 
     def own_part():
-        return own.at[rows_at(begin, 2 * third)]
+        return own.at[rows_at(begin, amount)]
+
+    def early_part(shard):
+        return target(shard).at[rows_at(early_begin, early)]
 
     def third_of(shard, side):
         return target(shard).at[rows_at(side * 2 * third, third)]
@@ -201,6 +207,23 @@
                     both(exists(key), z < depth - 1 if side < 0 else z > 0),
                 )
 
+    def e_send(key, other):
+        for side in (-1, 1) if key == origin else (key[0],):
+            if early and key[1] + 1 < depth:
+                block = early_part(shard(key, other))
+                mine = key == origin and other == 0
+                links.send(
+                    e_slot[((side, key[1] + 1), other)],
+                    own.at[rows_at(early_begin, early)] if mine else block,
+                    block,
+                    links.up if side < 0 else links.down,
+                    both(exists(key), z < depth - 1 if side < 0 else z > 0),
+                )
+
+    def e_receive(key, other):
+        if early:
+            links.receive(e_slot[(key, other)], early_part(shard(key, other)), exists(key))
+
     def y_send(key):
         source = own_part() if key == origin else part(shard(key, 0))
         links.send(y_slot[key], source, part(shard(key, 0)), links.y_peer, exists(key))
@@ -221,7 +244,11 @@
     order += [((side, depth - 1), 1) for side in (-1, 1)]
 
     def start():
+        if early:
+            source = own.at[rows_at(early_begin, early)]
+            links.send(pair_slot, source, early_part(shard(origin, 0)), links.y_peer)
         z_send(origin)
+        e_send(origin, 0)
         y_send(origin)
         c_send(origin, 0)
 
@@ -231,6 +258,9 @@
             x_send(key, 1)
 
     def step(far):
+        if far == 1 and early:
+            links.receive(pair_slot, early_part(shard(origin, 1)))
+            e_send(origin, 1)
         for side in (-1, 1):
             key = (side, far)
             links.receive(z_slot[key], part(shard(key, 0)), exists(key))
@@ -238,6 +268,10 @@
             y_send(key)
             x_send(key, 0)
         cross([origin] if far == 1 else [(-1, far - 1), (1, far - 1)])
+        for side in (-1, 1):
+            for other in (0, 1):
+                e_receive((side, far), other)
+                e_send((side, far), other)
         if far == depth - 1:
             cross([(-1, far), (1, far)])
 
@@ -284,6 +318,8 @@
     vector_start,
     stats,
     rows_v,
+    mats_v,
+    own_v,
     resid_v,
     normed_v,
     project_v,
@@ -302,16 +338,17 @@
     save_sem,
 ):
     links = Links(depth, send_sem, recv_sem)
-    links.greet()
     layers, count, width = mats.shape
     size = count // halves
-    own = [pltpu.make_async_copy(rows, rows_v.at[links.me], local_sem.at[0])]
+    rows_v[pl.ds(links.me, 1)] = rows[...][None]
     items = [gather_item(links, rows, lambda shard: rows_v.at[shard], rows.shape[0])]
+    own, loads = [], []
     for layer in range(layers):
+        loads.append(pltpu.make_async_copy(mats.at[layer], mats_v, local_sem.at[0]))
         own.append(
             pltpu.make_async_copy(
-                mats.at[layer],
-                all_mats.at[layer, pl.ds(links.me * count, count)],
+                own_v.at[layer],
+                all_mats.at[layer, rows_at(links.me * count, count)],
                 local_sem.at[1 + layer],
             )
         )
@@ -320,10 +357,19 @@
             def target(shard, layer=layer, half=half):
                 return all_mats.at[layer, rows_at(shard * count + half * size, size)]
 
-            items.append(gather_item(links, mats.at[layer, pl.ds(half * size, size)], target, size))
-    for copy in own:
-        copy.start()
+            block = own_v.at[layer, pl.ds(half * size, size)]
+            items.append(gather_item(links, block, target, size))
     saves = []
+
+    def take(layer):
+        loads[layer].wait()
+        own_v[layer] = mats_v[...].astype(BF)
+        own[layer].start()
+        if layer + 1 < layers:
+            loads[layer + 1].start()
+
+    loads[0].start()
+    links.greet()
 
     def save(source, target):
         copy = pltpu.make_async_copy(source, target, save_sem.at[len(saves)])
@@ -339,7 +385,6 @@
         return vectors[pl.ds(index, 1), :]
 
     def embed():
-        own[0].wait()
         vectors[...] = table(pixels + EMB + SEQ, 128).astype(F32).T
         position = table(pixels + EMB, SEQ).astype(F32).T
         embed_v[...] = matmul_nt(patches[...], table(0, pixels)) + position
@@ -455,7 +500,6 @@
         unit = (feature * inverse).astype(BF)
         logits = logit_scale * matmul_nt(unit, class_v[...])
         lane = lax.broadcasted_iota(jnp.int32, logits.shape, 1)
-        logits = jnp.where(lane < CLASSES, logits, -1e30)
         top = jnp.max(logits, -1, keepdims=True)
         shifted = jnp.exp(logits - top)
         total = jnp.sum(shifted, -1, keepdims=True)
@@ -499,12 +543,15 @@
                 running = None
 
     items[0][0]()
+    take(0)
     class_units()
     for number, (_, step, _, _) in enumerate(items):
         step(1)
         work(1)
         step(2)
         if number + 1 < len(items):
+            if number > 0 and number % halves == 0:
+                take(number // halves)
             items[number + 1][0]()
         work(1)
         if number > 0:
@@ -519,7 +566,7 @@
                 embed()
             for layer in range(layers - 1):
                 if number - 1 == halves * (layer + 1):
-                    own[1 + layer].wait()
+                    own[layer].wait()
                     work(1000)
                     running = counted(layer_steps(layer))
         work(1)
@@ -527,7 +574,7 @@
     work(2)
     items[-1][3]()
     work(1000)
-    own[layers].wait()
+    own[layers - 1].wait()
     for _ in layer_steps(layers - 1):
         pass
     head()
@@ -575,10 +622,12 @@
             shape(128, width),
             shape(8, 128),
         ),
-        in_specs=[any_space] * 2 + [vmem] * 6,
+        in_specs=[vmem, any_space] + [vmem] * 6,
         out_specs=[any_space] * 9 + [vmem] * 6,
         scratch_shapes=[
             pltpu.VMEM((shards,) + rows.shape, BF),
+            pltpu.VMEM(mats.shape[1:], F32),
+            pltpu.VMEM(mats.shape, BF),
             pltpu.VMEM((layers + 1, seq, width), F32),
         ]
         + [pltpu.VMEM(array.shape, array.dtype) for array in saved[1:]]
@@ -747,8 +796,9 @@
     vector_start,
     stats,
     out,
+    clipped,
+    totals,
     row_out,
-    totals,
     blocks_v,
     core_in,
     x_in,
@@ -1194,6 +1244,7 @@
         loss_sum,
         jnp.where(lane == 1, weight_sum, jnp.where(lane == 2, norm, clip)),
     )
+    clipped[...] = (row_out[...].astype(F32) * clip[:1, :1]).T
 
 
 def backward(
@@ -1222,12 +1273,13 @@
         functools.partial(backward_kernel, depth, sides, layers),
         out_shape=(
             jax.ShapeDtypeStruct((layers, count, width), BF),
-            jax.ShapeDtypeStruct((rows, lanes), BF),
+            jax.ShapeDtypeStruct((lanes, rows), F32),
             jax.ShapeDtypeStruct((8, 128), F32),
         ),
         in_specs=[any_space] * (1 + len(saved) + 2) + [vmem] * 8,
         out_specs=[any_space, vmem, vmem],
         scratch_shapes=[
+            room(rows, lanes),
             room(2 * blocks + 2 * SUB, n, width),
             room(IN_FLIGHT, 2, n, width),
             room(blocks, 2, p, width),
@@ -1331,10 +1383,8 @@
     row_id = lax.broadcasted_iota(jnp.int32, (part, count), 0)
     col_id = lax.broadcasted_iota(jnp.int32, (part, count), 1)
 
-    @pl.loop(0, NS_STEPS)
-    def _(turn):
-        now, later = lax.rem(turn, 2), 1 - lax.rem(turn, 2)
-        shift = jnp.where(turn >= NS_STEPS - 2, 1.0, 0.0)
+    def step(turn, shift, use):
+        now = lax.rem(turn, 2)
         linear = coeff_cubic + 2.0 * shift * coeff_quintic
         stay = coeff_linear + shift * (coeff_cubic + shift * coeff_quintic)
         for layer in range(layers):
@@ -1349,28 +1399,34 @@
                 low = low_v[layer, rows, :]
                 poly = linear * low.astype(F32) + coeff_quintic * matmul(low, low_v[layer])
                 value = stay * x_v[layer, rows, :] + matmul(poly.astype(BF), short_v[now, layer])
-                x_v[layer, rows, :] = value
-                short_v[later, layer, rows, :] = value.astype(BF)
+                use(layer, third, rows, value)
+
+    @pl.loop(0, NS_STEPS - 1)
+    def _(turn):
+        def keep(layer, third, rows, value):
+            x_v[layer, rows, :] = value
+            short_v[1 - lax.rem(turn, 2), layer, rows, :] = value.astype(BF)
+
+        step(turn, jnp.where(turn >= NS_STEPS - 2, 1.0, 0.0), keep)
 
     for load in loads[2:]:
         load.wait()
-    for layer in range(layers):
-        for third in range(3):
-            rows = pl.ds(third * part, part)
-            old = mats_v[layer, rows, :]
-            value = old - muon_rate * (
-                hyper * x_v[layer, rows, :] + weight_decay * old
-            )
-            mats_v[layer, rows, :] = value
-            ema_v[layer, rows, :] = ema_decay * ema_v[layer, rows, :] + (1.0 - ema_decay) * value
-            zero_v[layer, rows, :] = mix_share * value + (1.0 - mix_share) * zero_v[layer, rows, :]
-            for turn, (source, target) in enumerate(
-                ((mats_v, new_mats), (ema_v, new_ema), (zero_v, new_mixed))
-            ):
-                sem = out_sem.at[layers + (layer * 3 + third) * 3 + turn]
-                store = pltpu.make_async_copy(source.at[layer, rows], target.at[layer, rows], sem)
-                store.start()
-                stores.append(store)
+
+    def update(layer, third, rows, orth):
+        old = mats_v[layer, rows, :]
+        value = old - muon_rate * (hyper * orth + weight_decay * old)
+        mats_v[layer, rows, :] = value
+        ema_v[layer, rows, :] = ema_decay * ema_v[layer, rows, :] + (1.0 - ema_decay) * value
+        zero_v[layer, rows, :] = mix_share * value + (1.0 - mix_share) * zero_v[layer, rows, :]
+        for turn, (source, target) in enumerate(
+            ((mats_v, new_mats), (ema_v, new_ema), (zero_v, new_mixed))
+        ):
+            sem = out_sem.at[layers + (layer * 3 + third) * 3 + turn]
+            store = pltpu.make_async_copy(source.at[layer, rows], target.at[layer, rows], sem)
+            store.start()
+            stores.append(store)
+
+    step(NS_STEPS - 1, 1.0, update)
     for store in stores:
         store.wait()
 
@@ -1700,19 +1756,18 @@
     lanes = -(-rows // 128) * 128
     valid_mask = pad_mask.astype(F32)
     sent_rows = jnp.pad(row_params.T.astype(BF), ((0, 0), (0, lanes - rows)))
-    classes = jnp.pad(class_emb, ((0, -class_emb.shape[0] % 128), (0, 0)))
     weights, *saved, embedded, vectors, pooled_row, z_rows, feature_rows, start, stats = forward(
         depth,
         sent_rows,
-        layer_mats.astype(BF),
+        layer_mats,
         patches[0],
         valid_mask,
         valid_mask.T,
-        classes,
+        class_emb,
         labels[:, None],
         loss_weights.astype(F32)[:, None],
     )
-    mat_total, row_total, totals = backward(
+    mat_total, clipped, totals = backward(
         depth,
         lax.axis_size("ns"),
         weights,
@@ -1726,13 +1781,12 @@
         start,
         stats,
     )
-    loss_sum, weight_sum, grad_norm, clip = (totals[0, turn] for turn in range(4))
+    loss_sum, weight_sum, grad_norm = (totals[0, turn] for turn in range(3))
     momentum, new_mats, ema_mats, mixed_mats = finish(
         totals, mat_total, layer_momentum, layer_mats, layer_zero, layer_ema
     )
-    clipped = clip * row_total.astype(F32)[:, :rows].T
     return (loss_sum, weight_sum, grad_norm, new_mats, momentum, ema_mats, mixed_mats) + row_updates(
-        clipped, layers, row_params, row_zero, row_ema, row_first, row_second
+        clipped[:rows], layers, row_params, row_zero, row_ema, row_first, row_second
     )
 
 

time: 404 us -> 400 us (0.990)
  local copies, waits for them, and re-layouts: 5.92 us -> 16.2 us
  Pallas kernels: 380 us -> 370 us
    unnamed x12 -> x20, local copies, waits for them, and re-layouts: 0.04 us -> 12.1 us
    pallas_call x1, Pallas kernels: 156 us -> 148 us  [forward(): pl.pallas_call(functools.partial(forward_kernel, depth, halves), out_shap...]
where the time goes in v6:
time: 400 us; the launch traced here: 395 us
  Pallas kernels  370 us (92%)
  local copies, waits for them, and re-layouts  16.2 us (4%)
  other arithmetic  7.21 us (2%)
    pallas_call x1, Pallas kernels, backward(): pl.pallas_call(functools.partial(backward_kernel, depth, sides, layers),...  188 us
    pallas_call x1, Pallas kernels, forward(): pl.pallas_call(functools.partial(forward_kernel, depth, halves), out_shap...  148 us
    pallas_call x1, Pallas kernels, finish(): pl.pallas_call(functools.partial(finish_kernel, 0.2 * math.sqrt(width)),...  33.7 us
    unnamed x20, local copies, waits for them, and re-layouts  12.1 us

profile of v6, /device:TPU:0, one launch (start us, length us, event | category | flops | bytes accessed | tf_op | source)
XLA Modules:
  0.0 395.4 jit_solution(831757006230100677)
XLA Ops:
  0.6 1.2 convert_bitcast_fusion.1
  1.9 0.8 copy.52.keep_column
  2.7 1.0 convert_bitcast_fusion
  3.7 0.7 pad.4.rows
  5.7 148.1 %gather_and_forward.1 = (bf16[2,9216,768]{2,1,0:T(8,128)(2,1)}, f32[2,256,768]{2,1,0:T(8,128)}, bf16[2,256,768]{2,1,0:T(8,128)(2,1)}, bf16[2,256,2304]{2,1,0:T(8...) custom-call(bf16[48,1664]{1,0:T(8,128)(2,1)} %pad.4.rows, ...), custom_call_target="tpu_custom_call" | custom-call | tf_op jit(solution)/shard_map/gather_and_forward/pallas_call | solution.py:612
  153.8 187.9 %backward_and_sum.1 = (bf16[2,576,768]{2,1,0:T(8,128)(2,1)}, f32[1664,48]{1,0:T(8,128)}, f32[8,128]{1,0:T(8,128)}) custom-call(bf16[2,9216,768]{2,1,0:T(8,128)(2,1)} %get-tuple-element.35.weights, f32[2,256,768]{2,1,0:T(8,128)} %get-tuple-element.36.resid, bf16[2,256,768]{2,1,0:T(8,128)(2,1)} %get-tuple-element.37.normed, ...), custom_call_target="tpu_custom_call" | custom-call | tf_op jit(solution)/shard_map/backward_and_sum/pallas_call | solution.py:1272
  341.6 0.0 copy-start.1
  341.7 0.0 copy-start.2
  341.7 0.0 copy-start
  341.7 33.7 %orthogonalize.1 = (f32[2,576,768]{2,1,0:T(8,128)}, f32[2,576,768]{2,1,0:T(8,128)}, f32[2,576,768]{2,1,0:T(8,128)}, f32[2,576,768]{2,1,0:T(8,128)}) custom-call(f32[8,128]{1,0:T(8,128)} %get-tuple-element.50.totals, bf16[2,576,768]{2,1,0:T(8,128)(2,1)} %get-tuple-element.51.grad, f32[2,576,768]{2,1,0:T(8,128)} %momentum.1, f32[2,576,768]{2,1,0:T(8,128)} %mats.3, ...), custom_call_target="tpu_custom_call" | custom-call | tf_op jit(solution)/shard_map/orthogonalize/pallas_call | solution.py:1439
  375.4 0.0 copy-start.3
  375.4 0.0 copy-done.1
  375.4 1.2 copy.54
  376.6 0.0 copy-done.2
  376.6 1.2 copy.56
  377.8 0.0 copy-done
  377.8 1.2 copy.58
  379.0 0.0 copy-done.3
  379.0 1.2 copy.61
  380.1 0.0 copy-start.4
  380.1 2.8 add_multiply_fusion
  383.0 0.0 copy-done.4
  383.0 1.2 copy.59
  384.1 2.2 multiply_add_fusion
  386.3 2.1 copy.65
  388.4 1.0 copy.62
  389.4 1.0 copy.63
  390.4 1.0 copy.64
  391.4 1.0 copy.66
  392.5 0.7 slice.23
  393.2 0.6 slice.25
  393.7 1.4 fusion.2
  (1 shorter events, 0.0 us)
Async XLA Ops:
  341.6 33.8 %copy-start.1 = (f32[1564,48]{0,1:T(8,128)S(1)}, f32[1564,48]{0,1:T(8,128)}, u32[]{:S(2)}) copy-start(f32[1564,48]{0,1:T(8,128)} %param.26) | copy-start | bytes 900868
  341.7 34.9 %copy-start.2 = (f32[1564,48]{0,1:T(8,128)S(1)}, f32[1564,48]{0,1:T(8,128)}, u32[]{:S(2)}) copy-start(f32[1564,48]{0,1:T(8,128)} %param.27) | copy-start | bytes 900868
  341.7 36.1 %copy-start = (f32[1564,48]{0,1:T(8,128)S(1)}, f32[1564,48]{0,1:T(8,128)}, u32[]{:S(2)}) copy-start(f32[1564,48]{0,1:T(8,128)} %param.23) | copy-start | bytes 900868
  375.4 3.6 copy-start.3
  380.1 2.8 copy-start.4

commit v7 on v6

--- a/solution.py
+++ b/solution.py
@@ -1244,7 +1244,7 @@
         loss_sum,
         jnp.where(lane == 1, weight_sum, jnp.where(lane == 2, norm, clip)),
     )
-    clipped[...] = (row_out[...].astype(F32) * clip[:1, :1]).T
+    clipped[...] = row_out[...].astype(F32) * clip[:1, :1]
 
 
 def backward(
@@ -1273,7 +1273,7 @@
         functools.partial(backward_kernel, depth, sides, layers),
         out_shape=(
             jax.ShapeDtypeStruct((layers, count, width), BF),
-            jax.ShapeDtypeStruct((lanes, rows), F32),
+            jax.ShapeDtypeStruct((rows, lanes), F32),
             jax.ShapeDtypeStruct((8, 128), F32),
         ),
         in_specs=[any_space] * (1 + len(saved) + 2) + [vmem] * 8,
@@ -1329,14 +1329,40 @@
     )(weights, *saved, embedded, patches, vectors, keep, keep_column, *head, start, stats)
 
 
+def adam(clipped, row_params, row_zero, row_ema, row_first, row_second):
+    new_first = first_decay * row_first + (1.0 - first_decay) * clipped
+    new_second = second_decay * row_second + (1.0 - second_decay) * clipped * clipped
+    step_size = (
+        new_first
+        / (1.0 - first_decay**STEPS_DONE)
+        / (jnp.sqrt(new_second / (1.0 - second_decay**STEPS_DONE)) + adam_floor)
+    )
+    new_rows = row_params - adam_rate * (step_size + weight_decay * row_params)
+    ema_rows = ema_decay * row_ema + (1.0 - ema_decay) * new_rows
+    mixed_rows = mix_share * new_rows + (1.0 - mix_share) * row_zero
+    return (new_rows, new_first, new_second, ema_rows, mixed_rows)
+
+
 def finish_kernel(
     hyper,
     totals,
+    clipped,
+    row_params,
+    row_zero,
+    row_ema,
+    row_first,
+    row_second,
     grad,
     momentum,
     mats,
     zero,
     ema,
+    new_rows,
+    new_first,
+    new_second,
+    ema_rows,
+    mixed_rows,
+    bias_grad,
     new_momentum,
     new_mats,
     new_ema,
@@ -1358,6 +1384,19 @@
     loads = [pltpu.make_async_copy(a, b, in_sem.at[i]) for i, (a, b) in enumerate(pairs)]
     for load in loads:
         load.start()
+    rows = row_params.shape[1]
+    row_grad = clipped[:, pl.ds(0, rows)]
+    news = adam(row_grad, *(ref[...] for ref in (row_params, row_zero, row_ema, row_first, row_second)))
+    for target, value in zip((new_rows, new_first, new_second, ema_rows, mixed_rows), news):
+        target[...] = value
+    lane = lax.broadcasted_iota(jnp.int32, clipped.shape, 1)
+    spot = lax.broadcasted_iota(jnp.int32, bias_grad.shape, 1)
+    bias = jnp.zeros(bias_grad.shape, F32)
+    for layer in range(layers):
+        index = PIX + EMB + SEQ + 4 + 12 * layer + 7
+        column = jnp.sum(jnp.where(lane == index, clipped[...], 0.0), -1, keepdims=True)
+        bias = jnp.where(spot == layer, column, bias)
+    bias_grad[...] = bias
     part = count // 3
     factor = totals[pl.ds(0, 1), pl.ds(3, 1)]
     loads[0].wait()
@@ -1431,16 +1470,18 @@
         store.wait()
 
 
-def finish(totals, grad, momentum, mats, zero, ema):
+def finish(totals, clipped, tables, grad, momentum, mats, zero, ema):
     layers, count, width = grad.shape
     full = jax.ShapeDtypeStruct(mats.shape, F32)
+    table = jax.ShapeDtypeStruct(tables[0].shape, F32)
     any_space = pl.BlockSpec(memory_space=pl.ANY)
     vmem = pl.BlockSpec(memory_space=pltpu.VMEM)
     return pl.pallas_call(
         functools.partial(finish_kernel, 0.2 * math.sqrt(width)),
-        out_shape=(full, full, full, full),
-        in_specs=[vmem] + [any_space] * 5,
-        out_specs=[any_space] * 4,
+        out_shape=(table,) * 5
+        + (jax.ShapeDtypeStruct((clipped.shape[0], 128), F32), full, full, full, full),
+        in_specs=[vmem] * (2 + len(tables)) + [any_space] * 5,
+        out_specs=[vmem] * 6 + [any_space] * 4,
         scratch_shapes=[
             pltpu.VMEM(grad.shape, BF),
             pltpu.VMEM(mats.shape, F32),
@@ -1455,7 +1496,7 @@
         ],
         name="orthogonalize",
         compiler_params=pltpu.CompilerParams(vmem_limit_bytes=56 * 1024 * 1024),
-    )(totals, grad, momentum, mats, zero, ema)
+    )(totals, clipped, *tables, grad, momentum, mats, zero, ema)
 
 
 def gather_layer(shard):
@@ -1587,20 +1628,10 @@
     return blocks
 
 
-def row_updates(clipped, layers, row_params, row_zero, row_ema, row_first, row_second):
+def row_updates(clipped, layers, *tables):
     front = PIX + EMB + SEQ + 4
-    new_first = first_decay * row_first + (1.0 - first_decay) * clipped
-    new_second = second_decay * row_second + (1.0 - second_decay) * clipped * clipped
-    down_bias_grad = clipped[front:].reshape(layers, 12, row_params.shape[1])[:, 7]
-    step_size = (
-        new_first
-        / (1.0 - first_decay**STEPS_DONE)
-        / (jnp.sqrt(new_second / (1.0 - second_decay**STEPS_DONE)) + adam_floor)
-    )
-    new_rows = row_params - adam_rate * (step_size + weight_decay * row_params)
-    ema_rows = ema_decay * row_ema + (1.0 - ema_decay) * new_rows
-    mixed_rows = mix_share * new_rows + (1.0 - mix_share) * row_zero
-    return (new_rows, new_first, new_second, ema_rows, mixed_rows, down_bias_grad)
+    down_bias_grad = clipped[front:].reshape(layers, 12, clipped.shape[1])[:, 7]
+    return adam(clipped, *tables) + (down_bias_grad,)
 
 
 def plain_body(
@@ -1782,12 +1813,12 @@
         stats,
     )
     loss_sum, weight_sum, grad_norm = (totals[0, turn] for turn in range(3))
-    momentum, new_mats, ema_mats, mixed_mats = finish(
-        totals, mat_total, layer_momentum, layer_mats, layer_zero, layer_ema
-    )
-    return (loss_sum, weight_sum, grad_norm, new_mats, momentum, ema_mats, mixed_mats) + row_updates(
-        clipped[:rows], layers, row_params, row_zero, row_ema, row_first, row_second
-    )
+    tables = [table.T for table in (row_params, row_zero, row_ema, row_first, row_second)]
+    *news, bias, momentum, new_mats, ema_mats, mixed_mats = finish(
+        totals, clipped, tables, mat_total, layer_momentum, layer_mats, layer_zero, layer_ema
+    )
+    news = [table.T for table in news] + [bias[:, :layers].T]
+    return (loss_sum, weight_sum, grad_norm, new_mats, momentum, ema_mats, mixed_mats, *news)
 
 
 def body(*args):

time: 400 us -> 384 us (0.960)
  local copies, waits for them, and re-layouts: 16.2 us -> 4.23 us
  other arithmetic: 7.21 us -> 2.23 us
    unnamed x20 -> x1, local copies, waits for them, and re-layouts: 12.1 us -> 0.64 us
    add x2 -> x0, other arithmetic: 4.98 us -> none  [the longest x1 2.82 us: row_updates(): mixed_rows = mix_share * new_rows + (1.0 - mix_share) * row_zero]
where the time goes in v7:
time: 384 us; the launch traced here: 379 us
  Pallas kernels  371 us (97%)
  local copies, waits for them, and re-layouts  4.23 us (1%)
    pallas_call x1, Pallas kernels, backward(): pl.pallas_call(functools.partial(backward_kernel, depth, sides, layers),...  187 us
    pallas_call x1, Pallas kernels, forward(): pl.pallas_call(functools.partial(forward_kernel, depth, halves), out_shap...  148 us
    pallas_call x1, Pallas kernels, finish(): pl.pallas_call(functools.partial(finish_kernel, 0.2 * math.sqrt(width)),...  35.5 us

profile of v7, /device:TPU:0, one launch (start us, length us, event | category | flops | bytes accessed | tf_op | source)
XLA Modules:
  0.0 379.2 jit_solution(15834213043050241695)
XLA Ops:
  1.9 1.2 convert_bitcast_fusion
  3.2 0.8 copy.28.keep_column
  4.0 1.0 bitcast_convert_fusion
  5.0 0.7 pad.4.rows
  5.7 148.0 %gather_and_forward.1 = (bf16[2,9216,768]{2,1,0:T(8,128)(2,1)}, f32[2,256,768]{2,1,0:T(8,128)}, bf16[2,256,768]{2,1,0:T(8,128)(2,1)}, bf16[2,256,2304]{2,1,0:T(8...) custom-call(bf16[48,1664]{1,0:T(8,128)(2,1)} %pad.4.rows, ...), custom_call_target="tpu_custom_call" | custom-call | tf_op jit(solution)/shard_map/gather_and_forward/pallas_call | solution.py:612
  153.7 186.9 %backward_and_sum.1 = (bf16[2,576,768]{2,1,0:T(8,128)(2,1)}, f32[48,1664]{1,0:T(8,128)}, f32[8,128]{1,0:T(8,128)}) custom-call(bf16[2,9216,768]{2,1,0:T(8,128)(2,1)} %get-tuple-element.41.weights, f32[2,256,768]{2,1,0:T(8,128)} %get-tuple-element.42.resid, bf16[2,256,768]{2,1,0:T(8,128)(2,1)} %get-tuple-element.43.normed, ...), custom_call_target="tpu_custom_call" | custom-call | tf_op jit(solution)/shard_map/backward_and_sum/pallas_call | solution.py:1272
  340.6 1.4 fusion
  342.0 35.5 %orthogonalize.1 = (f32[48,1564]{1,0:T(8,128)}, f32[48,1564]{1,0:T(8,128)}, f32[48,1564]{1,0:T(8,128)}, f32[48,1564]{1,0:T(8,128)}, f32[48,1564]{1,0:T(8,128)}, ...) custom-call(f32[8,128]{1,0:T(8,128)} %get-tuple-element.56.totals, ...), custom_call_target="tpu_custom_call" | custom-call | tf_op jit(solution)/shard_map/orthogonalize/pallas_call | solution.py:1479
  377.6 0.7 slice_bitcast_fusion
  378.3 0.6 copy.30

commit v8 on v7

--- a/solution.py
+++ b/solution.py
@@ -297,8 +297,7 @@
     rows,
     mats,
     patches,
-    keep,
-    keep_column,
+    mask,
     classes,
     label,
     weight,
@@ -317,6 +316,8 @@
     feature_rows,
     vector_start,
     stats,
+    row_own,
+    tail_v,
     rows_v,
     mats_v,
     own_v,
@@ -340,8 +341,14 @@
     links = Links(depth, send_sem, recv_sem)
     layers, count, width = mats.shape
     size = count // halves
-    rows_v[pl.ds(links.me, 1)] = rows[...][None]
-    items = [gather_item(links, rows, lambda shard: rows_v.at[shard], rows.shape[0])]
+    whole = rows.shape[1] // 128 * 128
+    tail_v[...] = jnp.zeros_like(tail_v)
+    tail_v[:, pl.ds(0, rows.shape[1] - whole)] = rows[:, pl.ds(whole, rows.shape[1] - whole)]
+    row_own[:, pl.ds(0, whole)] = rows[:, pl.ds(0, whole)].astype(BF)
+    row_own[:, pl.ds(whole, 128)] = tail_v[...].astype(BF)
+    rows_v[pl.ds(links.me, 1)] = row_own[...][None]
+    items = [gather_item(links, row_own, lambda shard: rows_v.at[shard], rows.shape[0])]
+    keep = mask[...].astype(F32)
     own, loads = [], []
     for layer in range(layers):
         loads.append(pltpu.make_async_copy(mats.at[layer], mats_v, local_sem.at[0]))
@@ -422,7 +429,7 @@
         for head in range(2):
             here = half_lane if head == 0 else jnp.logical_not(half_lane)
             query_h = jnp.where(here, query, jnp.zeros_like(query))
-            scores = jnp.where(keep[...] > 0, matmul_nt(query_h, key) * scale, -1000000000.0)
+            scores = jnp.where(keep > 0, matmul_nt(query_h, key) * scale, -1000000000.0)
             top = jnp.max(scores, -1, keepdims=True)
             expo = jnp.exp(scores - top)
             total = jnp.sum(expo, -1, keepdims=True)
@@ -488,8 +495,9 @@
         class_v[...] = (value * length).astype(BF)
 
     def head():
-        number = jnp.sum(keep[...], -1, keepdims=True)
-        pooled = jnp.sum(resid_v[layers] * keep_column[...], 0, keepdims=True) / number
+        number = jnp.sum(keep, -1, keepdims=True)
+        keep_column = jnp.broadcast_to(keep, (8, seq)).T[:, :1]
+        pooled = jnp.sum(resid_v[layers] * keep_column, 0, keepdims=True) / number
         center = pooled - jnp.mean(pooled, -1, keepdims=True)
         spread = lax.rsqrt(jnp.mean(center * center, -1, keepdims=True) + norm_epsilon)
         normal = center * spread
@@ -588,8 +596,9 @@
         yield 1
 
 
-def forward(depth, rows, mats, patches, keep, keep_column, classes, label, weight):
+def forward(depth, rows, mats, patches, mask, classes, label, weight):
     layers, count, width = mats.shape
+    lanes = (rows.shape[1] // 128 + 1) * 128
     shards = PLANE * depth
     halves = 2
     seq = patches.shape[0]
@@ -622,10 +631,12 @@
             shape(128, width),
             shape(8, 128),
         ),
-        in_specs=[vmem, any_space] + [vmem] * 6,
+        in_specs=[vmem, any_space] + [vmem] * 5,
         out_specs=[any_space] * 9 + [vmem] * 6,
         scratch_shapes=[
-            pltpu.VMEM((shards,) + rows.shape, BF),
+            pltpu.VMEM((rows.shape[0], lanes), BF),
+            pltpu.VMEM((rows.shape[0], 128), F32),
+            pltpu.VMEM((shards, rows.shape[0], lanes), BF),
             pltpu.VMEM(mats.shape[1:], F32),
             pltpu.VMEM(mats.shape, BF),
             pltpu.VMEM((layers + 1, seq, width), F32),
@@ -646,7 +657,7 @@
         compiler_params=pltpu.CompilerParams(
             collective_id=1, has_side_effects=True, vmem_limit_bytes=56 * 1024 * 1024
         ),
-    )(rows, mats, patches, keep, keep_column, classes, label, weight)
+    )(rows, mats, patches, mask, classes, label, weight)
 
 
 def accumulate(target, start, source, begin, count, step):
@@ -788,8 +799,7 @@
     embedded,
     patches,
     vectors,
-    keep,
-    keep_column,
+    mask,
     pooled_row,
     z_rows,
     feature_rows,
@@ -911,7 +921,9 @@
     )
     note[...] = stats[...]
     vector_v[...] = vector_start[...]
-    up_v[...] = keep_column[...] * pooled_row[pl.ds(0, 1), :]
+    keep = mask[...].astype(F32)
+    keep_column = jnp.broadcast_to(keep, (8, keep.shape[1])).T[:, :1]
+    up_v[...] = keep_column * pooled_row[pl.ds(0, 1), :]
     lane = lax.broadcasted_iota(jnp.int32, (8, 128), 1)
     first = lax.broadcasted_iota(jnp.int32, (8, 128), 0) == 0
 
@@ -920,7 +932,7 @@
         note[...] += jnp.where(first & (lane == 0), jnp.sum(value * value), 0.0)
 
     groups, closers = [], []
-    starts = {}
+    starts, members = {}, {}
 
     def add_group(dest, send_out, take_in, sizes, bufs, emit, used=None):
         def load_block(i, side, mine, target, slot):
@@ -931,45 +943,59 @@
 
         groups.append(scatter_group(links, dest, load_block, sizes, bufs, emit, used))
 
+    total_blocks = layers * per_layer
     for order, layer in enumerate(reversed(range(layers))):
         for turn, dest in enumerate(reversed(range(depth))):
-            ring = own
             for part in range(SUB):
-                number, spot = len(groups), layer * SUB + part
+                number, spot = (order * depth + turn) * SUB + part, layer * SUB + part
                 starts[(layer, dest, part)] = number
-                slot = number % IN_FLIGHT
-
-                def send_out(i, side, mine, target, sem_slot, ring=ring, part=part):
-                    source = blocks_v.at[ring + 2 * part + side]
-                    links.send(sem_slot, source, target, links.c_peer)
-
-                def write(source, layer=layer, part=part, spot=spot):
-                    target = out.at[layer, pl.ds(part * n, n)]
-                    return pltpu.make_async_copy(source, target, local_sem.at[spot])
-
-                def emit(result, write=write):
-                    add_squares(result[...])
-                    write(result).start()
-
-                closers.append((dest, write, blocks_v.at[2 * number]))
-
-                def used(number=number):
-                    if number < layers * per_layer - IN_FLIGHT:
-                        pl.semaphore_signal(
-                            free_sem, inc=1, device_id=links.c_peer, device_id_type=MESH
-                        )
-
-                add_group(
-                    dest,
-                    send_out,
-                    lambda i, side, mine: None,
-                    (n, p, n - 2 * p, n // 4),
-                    [blocks_v.at[pl.ds(2 * number, 2)], core_in.at[slot]]
-                    + [ref.at[number] for ref in (x_in, y_in, z_in)]
-                    + [z_last.at[spot], final.at[spot]],
-                    emit,
-                    used,
-                )
+                pieces = 2 if number >= total_blocks - SUB else 1
+                size = n // pieces
+                edge = (size // 4 + 15) // 16 * 16
+                middle = size - edge
+                members[number] = []
+                for half in range(pieces):
+                    members[number].append(len(groups))
+                    inside = pl.ds(half * size, size)
+                    window = pl.ds(half * middle, middle)
+
+                    def send_out(i, side, mine, target, slot, part=part, inside=inside):
+                        source = blocks_v.at[own + 2 * part + side, inside]
+                        links.send(slot, source, target, links.c_peer)
+
+                    def write(source, layer=layer, at=part * n + half * size, size=size, sem=spot + half * (layers * SUB + 2 * depth)):
+                        target = out.at[layer, pl.ds(at, size)]
+                        return pltpu.make_async_copy(source, target, local_sem.at[sem])
+
+                    def emit(result, write=write):
+                        add_squares(result[...])
+                        write(result).start()
+
+                    closers.append((dest, write, blocks_v.at[2 * number, inside]))
+
+                    def used(number=number):
+                        if number < total_blocks - IN_FLIGHT:
+                            pl.semaphore_signal(
+                                free_sem, inc=1, device_id=links.c_peer, device_id_type=MESH
+                            )
+
+                    add_group(
+                        dest,
+                        send_out,
+                        lambda i, side, mine: None,
+                        (size, edge, size - 2 * edge, 48 if pieces == 1 else 32),
+                        [
+                            blocks_v.at[pl.ds(2 * number, 2), inside],
+                            core_in.at[number % IN_FLIGHT, :, inside],
+                            x_in.at[number if half == 0 else total_blocks + part, :, pl.ds(0, edge)],
+                            y_in.at[number, window],
+                            z_in.at[number, window],
+                            z_last.at[spot, window],
+                            final.at[spot, window],
+                        ],
+                        emit,
+                        used,
+                    )
     first_row_group = len(groups)
     rows = row_out.shape[0]
     for dest in reversed(range(depth)):
@@ -998,22 +1024,24 @@
             row_emit,
         )
 
-    begun = []
-
     def release(layer, dest):
+        begun = 0
         for part in range(SUB):
             number = starts[(layer, dest, part)]
             if number >= IN_FLIGHT:
                 pl.semaphore_wait(free_sem, 1)
-            groups[number].begin()
-            begun.append(number)
+            for index in members[number]:
+                groups[index].begin()
+                begun += 1
+        return begun
 
     def recycle(layer, dest):
         for part in range(SUB):
             number = starts[(layer, dest, part)]
             if number >= SUB:
-                for slot in groups[number - SUB].core_slot:
-                    links.finish(slot)
+                for index in members[number - SUB]:
+                    for slot in groups[index].core_slot:
+                        links.finish(slot)
 
     last_turn = [0]
 
@@ -1062,7 +1090,7 @@
             total = jnp.sum(
                 jnp.where(column == 2 * pair + head, totals_now, 0.0), -1, keepdims=True
             )
-            scores = jnp.where(keep[...] > 0, matmul_nt(query_h, key) * scale, -1000000000.0)
+            scores = jnp.where(keep > 0, matmul_nt(query_h, key) * scale, -1000000000.0)
             probs = jnp.exp(scores - total)
             prob_grad = matmul_nt(grad_h, value)
             value_grad += matmul_tn(probs.astype(BF), grad_h)
@@ -1113,15 +1141,15 @@
             else:
                 grad_pieces(layer, 2, hidden_v, 0, 2, short_v, 4)
             if part == 1:
-                release(layer, 3)
-                yield 3
+                begun = release(layer, 3)
+                yield begun
             else:
                 yield None
         grad_pieces(layer, 2, pre_v, 2 * width, 2, two_v, 0)
         yield None
         grad_pieces(layer, 2, pre_v, 3 * width, 2, two_v, 2)
-        release(layer, 2)
-        yield 2
+        begun = release(layer, 2)
+        yield begun
         load(layer, 1).wait()
         inner, gain, shift = norm_back(mixed_v[...], vector(5), total_v[...])
         put(5, gain)
@@ -1139,13 +1167,13 @@
         grad_pieces(layer, 1, pre_v, 0, 2, two_v, 2)
         yield None
         grad_pieces(layer, 1, pre_v, width, 2, two_v, 4)
-        release(layer, 1)
+        begun = release(layer, 1)
         if layer > 0:
             for which in range(3):
                 load(layer - 1, which).start()
         else:
             embed_load.start()
-        yield 1
+        yield begun
         load(layer, 5).wait()
         load(layer, 6).wait()
         for third in range(3):
@@ -1163,8 +1191,8 @@
             grad_pieces(layer, 0, pre_v, third * width, 2, normed_v, 2 * third)
             if third < 2:
                 yield None
-        release(layer, 0)
-        yield 0
+        begun = release(layer, 0)
+        yield begun
         load(layer, 3).wait()
         back = matmul(pre_v[:, pl.ds(0, width)], chunk(chunk0 + 9))
         back += matmul(pre_v[:, pl.ds(width, width)], chunk(chunk0 + 10))
@@ -1185,7 +1213,7 @@
     for order, layer in enumerate(reversed(range(layers))):
         for ready in layer_steps(order, layer):
             if ready is not None:
-                pending += SUB
+                pending += ready
             if pending > 0:
                 advance()
                 pending -= 1
@@ -1248,7 +1276,7 @@
 
 
 def backward(
-    depth, sides, weights, saved, embedded, patches, vectors, keep, keep_column, head, start, stats
+    depth, sides, weights, saved, embedded, patches, vectors, mask, head, start, stats
 ):
     layers, rows_all, width = weights.shape
     seq, pixels = patches.shape
@@ -1268,7 +1296,7 @@
 
     any_space = pl.BlockSpec(memory_space=pl.ANY)
     vmem = pl.BlockSpec(memory_space=pltpu.VMEM)
-    slots = (blocks + depth) * 9
+    slots = (blocks + SUB + depth) * 9
     return pl.pallas_call(
         functools.partial(backward_kernel, depth, sides, layers),
         out_shape=(
@@ -1276,13 +1304,13 @@
             jax.ShapeDtypeStruct((rows, lanes), F32),
             jax.ShapeDtypeStruct((8, 128), F32),
         ),
-        in_specs=[any_space] * (1 + len(saved) + 2) + [vmem] * 8,
+        in_specs=[any_space] * (1 + len(saved) + 2) + [vmem] * 7,
         out_specs=[any_space, vmem, vmem],
         scratch_shapes=[
             room(rows, lanes),
             room(2 * blocks + 2 * SUB, n, width),
             room(IN_FLIGHT, 2, n, width),
-            room(blocks, 2, p, width),
+            room(blocks + SUB, 2, p, width),
             room(blocks, m, width),
             room(blocks, m, width),
             room(layers * SUB, m, width),
@@ -1315,7 +1343,7 @@
             room(everyone, 8, 128, dtype=F32),
             pltpu.SemaphoreType.DMA((slots,)),
             pltpu.SemaphoreType.DMA((slots,)),
-            pltpu.SemaphoreType.DMA((layers * SUB + 2 * depth,)),
+            pltpu.SemaphoreType.DMA((2 * layers * SUB + 2 * depth,)),
             pltpu.SemaphoreType.DMA((4,)),
             pltpu.SemaphoreType.DMA((9,)),
             pltpu.SemaphoreType.DMA((everyone,)),
@@ -1326,7 +1354,7 @@
         compiler_params=pltpu.CompilerParams(
             collective_id=2, has_side_effects=True, vmem_limit_bytes=VMEM_LIMIT
         ),
-    )(weights, *saved, embedded, patches, vectors, keep, keep_column, *head, start, stats)
+    )(weights, *saved, embedded, patches, vectors, mask, *head, start, stats)
 
 
 def adam(clipped, row_params, row_zero, row_ema, row_first, row_second):
@@ -1783,17 +1811,12 @@
     layers, columns, width = layer_mats.shape
     shards = lax.axis_size("fsdp")
     depth = shards // PLANE
-    rows, share = row_params.shape
-    lanes = -(-rows // 128) * 128
-    valid_mask = pad_mask.astype(F32)
-    sent_rows = jnp.pad(row_params.T.astype(BF), ((0, 0), (0, lanes - rows)))
     weights, *saved, embedded, vectors, pooled_row, z_rows, feature_rows, start, stats = forward(
         depth,
-        sent_rows,
+        row_params.T,
         layer_mats,
         patches[0],
-        valid_mask,
-        valid_mask.T,
+        pad_mask,
         class_emb,
         labels[:, None],
         loss_weights.astype(F32)[:, None],
@@ -1806,8 +1829,7 @@
         embedded,
         patches[0],
         vectors,
-        valid_mask,
-        valid_mask.T,
+        pad_mask,
         (pooled_row, z_rows, feature_rows),
         start,
         stats,

time: 384 us -> 376 us (0.979)
  Pallas kernels: 371 us -> 367 us
    pallas_call x1, Pallas kernels: 187 us -> 183 us  [backward(): pl.pallas_call(functools.partial(backward_kernel, depth, sides, layers),...]
where the time goes in v8:
time: 376 us; the launch traced here: 372 us
  Pallas kernels  367 us (98%)
    pallas_call x1, Pallas kernels, backward(): pl.pallas_call(functools.partial(backward_kernel, depth, sides, layers),...  183 us
    pallas_call x1, Pallas kernels, forward(): pl.pallas_call(functools.partial(forward_kernel, depth, halves), out_shap...  148 us
    pallas_call x1, Pallas kernels, finish(): pl.pallas_call(functools.partial(finish_kernel, 0.2 * math.sqrt(width)),...  35.5 us

profile of v8, /device:TPU:0, one launch (start us, length us, event | category | flops | bytes accessed | tf_op | source)
XLA Modules:
  0.0 371.6 jit_solution(5395951219215758289)
XLA Ops:
  1.9 148.1 %gather_and_forward.1 = (bf16[2,9216,768]{2,1,0:T(8,128)(2,1)}, f32[2,256,768]{2,1,0:T(8,128)}, bf16[2,256,768]{2,1,0:T(8,128)(2,1)}, bf16[2,256,2304]{2,1,0:T(8...) custom-call(f32[48,1564]{1,0:T(8,128)} %bitcast.21, ...), custom_call_target="tpu_custom_call" | custom-call | tf_op jit(solution)/shard_map/gather_and_forward/pallas_call | solution.py:621
  150.0 183.0 %backward_and_sum.1 = (bf16[2,576,768]{2,1,0:T(8,128)(2,1)}, f32[48,1664]{1,0:T(8,128)}, f32[8,128]{1,0:T(8,128)}) custom-call(bf16[2,9216,768]{2,1,0:T(8,128)(2,1)} %get-tuple-element.41.weights, f32[2,256,768]{2,1,0:T(8,128)} %get-tuple-element.42.resid, bf16[2,256,768]{2,1,0:T(8,128)(2,1)} %get-tuple-element.43.normed, ...), custom_call_target="tpu_custom_call" | custom-call | tf_op jit(solution)/shard_map/backward_and_sum/pallas_call | solution.py:1300
  333.0 1.4 fusion
  334.4 35.5 %orthogonalize.1 = (f32[48,1564]{1,0:T(8,128)}, f32[48,1564]{1,0:T(8,128)}, f32[48,1564]{1,0:T(8,128)}, f32[48,1564]{1,0:T(8,128)}, f32[48,1564]{1,0:T(8,128)}, ...) custom-call(f32[8,128]{1,0:T(8,128)} %get-tuple-element.56.totals, ...), custom_call_target="tpu_custom_call" | custom-call | tf_op jit(solution)/shard_map/orthogonalize/pallas_call | solution.py:1507
  369.9 0.7 slice_bitcast_fusion
  370.7 0.6 copy.27

commit v9 on v8

--- a/solution.py
+++ b/solution.py
@@ -1425,14 +1425,14 @@
         column = jnp.sum(jnp.where(lane == index, clipped[...], 0.0), -1, keepdims=True)
         bias = jnp.where(spot == layer, column, bias)
     bias_grad[...] = bias
-    part = count // 3
+    part = count // 2
     factor = totals[pl.ds(0, 1), pl.ds(3, 1)]
     loads[0].wait()
     loads[1].wait()
     stores = []
     for layer in range(layers):
         total = jnp.zeros((1, 1), F32)
-        for third in range(3):
+        for third in range(2):
             rows = pl.ds(third * part, part)
             value = momentum_decay * m_v[layer, rows, :] + factor * grad_v[layer, rows, :].astype(F32)
             m_v[layer, rows, :] = value
@@ -1441,7 +1441,7 @@
         store.start()
         stores.append(store)
         inverse = 1.0 / (jnp.sqrt(total) + 1e-07)
-        for third in range(3):
+        for third in range(2):
             rows = pl.ds(third * part, part)
             value = m_v[layer, rows, :] * inverse
             x_v[layer, rows, :] = value
@@ -1455,13 +1455,13 @@
         linear = coeff_cubic + 2.0 * shift * coeff_quintic
         stay = coeff_linear + shift * (coeff_cubic + shift * coeff_quintic)
         for layer in range(layers):
-            for third in range(3):
+            for third in range(2):
                 rows = pl.ds(third * part, part)
                 gram = matmul_nt(short_v[now, layer, rows, :], short_v[now, layer])
                 gram -= jnp.where(row_id + third * part == col_id, shift, 0.0)
                 low_v[layer, rows, :] = gram.astype(BF)
         for layer in range(layers):
-            for third in range(3):
+            for third in range(2):
                 rows = pl.ds(third * part, part)
                 low = low_v[layer, rows, :]
                 poly = linear * low.astype(F32) + coeff_quintic * matmul(low, low_v[layer])

time: 376 us -> 373 us (level)
  Pallas kernels: 367 us -> 363 us
where the time goes in v9:
time: 373 us; the launch traced here: 368 us
  Pallas kernels  363 us (97%)
    pallas_call x1, Pallas kernels, backward(): pl.pallas_call(functools.partial(backward_kernel, depth, sides, layers),...  183 us
    pallas_call x1, Pallas kernels, forward(): pl.pallas_call(functools.partial(forward_kernel, depth, halves), out_shap...  148 us
    pallas_call x1, Pallas kernels, finish(): pl.pallas_call(functools.partial(finish_kernel, 0.2 * math.sqrt(width)),...  32.4 us

profile of v9, /device:TPU:0, one launch (start us, length us, event | category | flops | bytes accessed | tf_op | source)
XLA Modules:
  0.0 368.5 jit_solution(16010378939809793443)
XLA Ops:
  1.9 148.1 %gather_and_forward.1 = (bf16[2,9216,768]{2,1,0:T(8,128)(2,1)}, f32[2,256,768]{2,1,0:T(8,128)}, bf16[2,256,768]{2,1,0:T(8,128)(2,1)}, bf16[2,256,2304]{2,1,0:T(8...) custom-call(f32[48,1564]{1,0:T(8,128)} %bitcast.21, ...), custom_call_target="tpu_custom_call" | custom-call | tf_op jit(solution)/shard_map/gather_and_forward/pallas_call | solution.py:621
  150.0 183.0 %backward_and_sum.1 = (bf16[2,576,768]{2,1,0:T(8,128)(2,1)}, f32[48,1664]{1,0:T(8,128)}, f32[8,128]{1,0:T(8,128)}) custom-call(bf16[2,9216,768]{2,1,0:T(8,128)(2,1)} %get-tuple-element.41.weights, f32[2,256,768]{2,1,0:T(8,128)} %get-tuple-element.42.resid, bf16[2,256,768]{2,1,0:T(8,128)(2,1)} %get-tuple-element.43.normed, ...), custom_call_target="tpu_custom_call" | custom-call | tf_op jit(solution)/shard_map/backward_and_sum/pallas_call | solution.py:1300
  333.0 1.4 fusion
  334.4 32.4 %orthogonalize.1 = (f32[48,1564]{1,0:T(8,128)}, f32[48,1564]{1,0:T(8,128)}, f32[48,1564]{1,0:T(8,128)}, f32[48,1564]{1,0:T(8,128)}, f32[48,1564]{1,0:T(8,128)}, ...) custom-call(f32[8,128]{1,0:T(8,128)} %get-tuple-element.56.totals, ...), custom_call_target="tpu_custom_call" | custom-call | tf_op jit(solution)/shard_map/orthogonalize/pallas_call | solution.py:1507
  366.8 0.7 slice_bitcast_fusion
  367.6 0.6 copy.27
